TPU v7x, 32 devices: a whole 2x2x4 slice. The times are simulated.
32 devices in a mesh: delay: 2 (over y), row: 4 (over x, core), col: 4 (over z).
Axes of the slice: x: 2, y: 2, z: 4, core: 2. Of those that a mesh axis runs over, the one named last changes fastest.
Arguments:
- excitation: bfloat16 [2, 3072, 128], P(None, 'row'), may hold values from -6 to 6
- delay_ops: bfloat16 [2, 3072, 3072], P('delay', 'row', 'col'), may hold values from -0.078125 to 0.078125
- inverse_op: bfloat16 [3072, 3072], P('col', 'row'), may hold values from -0.109375 to 0.109375
- history: bfloat16 [2, 3072, 128], P('delay', 'col'), may hold values from -6 to 6
Outputs:
- currents: bfloat16 [2, 3072, 128], P(None, 'col')
- final_history: bfloat16 [2, 3072, 128], P('delay', 'col')
All inputs are finite; a program needn't handle non-finite values.
Results may differ from a plain program's by a relative error of at most 0.008.
Values may be sent and summed in bfloat16 or wider, within the bound.
No kernel may reach another device: no remote copies, remote signals or barrier semaphores. Data moves between devices by JAX's collectives and lax.ppermute only.
A program may use at most 64 MiB of HBM per device.

v0:
```python
import jax
import jax.numpy as jnp
from jax import lax
from jax.sharding import PartitionSpec as P

STEPS = 2


def from_behind(block, axis, distance):
    devices = range(lax.axis_size(axis))
    route = [(i - distance, i) for i in devices if i - distance in devices]
    return lax.ppermute(block, axis, route)


def spread(block, axis, source):
    block = jnp.where(lax.axis_index(axis) == source, block, jnp.zeros_like(block))
    return lax.psum(block, axis)


def on_device(excitation, delay_ops, inverse_op, history):
    operator = delay_ops[0]
    stored = history[0]
    position = lax.axis_index("delay")
    produced = []
    terms = [jnp.dot(operator, stored, preferred_element_type=jnp.float32)]
    step = 1
    earlier = from_behind(stored, "delay", step)
    terms.append(jnp.dot(operator, earlier, preferred_element_type=jnp.float32))
    leftover = from_behind(stored, "delay", STEPS)
    older_total = lax.psum(jnp.stack(terms), ("delay", "col"))
    lag = 0
    shortest = [spread(operator, "delay", lag)]
    for step in range(STEPS):
        retarded = older_total[step]
        if step > 0:
            lag = 0
            recent = jnp.dot(
                shortest[lag], produced[step - 1 - lag], preferred_element_type=jnp.float32
            )
            retarded = retarded + lax.psum(recent.astype(jnp.bfloat16), "col").astype(jnp.float32)
        rhs = (excitation[step].astype(jnp.float32) - retarded).astype(jnp.bfloat16)
        mine = lax.psum_scatter(
            jnp.dot(inverse_op, rhs, preferred_element_type=jnp.float32),
            "row",
            scatter_dimension=0,
            tiled=True,
        ).astype(jnp.bfloat16)
        produced.append(lax.all_gather(mine, "row", axis=0, tiled=True))
    stacked = jnp.stack(produced)
    picked_index = jnp.clip(STEPS - 1 - position, 0, STEPS - 1)
    picked = lax.dynamic_index_in_dim(stacked, picked_index, 0, keepdims=False)
    hist = jnp.where(position < STEPS, picked, leftover)
    return (stacked, hist[None])


def solution(mesh):
    in_specs = (
        P(None, "row", None),
        P("delay", "row", "col"),
        P("col", "row"),
        P("delay", "col", None),
    )
    out_specs = (P(None, "col", None), P("delay", "col", None))
    return jax.shard_map(
        on_device, mesh=mesh, in_specs=in_specs, out_specs=out_specs, check_vma=False
    )
```

profile of v0, /device:TPU:0, one launch (start us, length us, event | category | flops | bytes accessed | tf_op | source)
XLA Modules:
  0.0 218.8 jit_solution(3749420114005794724)
XLA Ops:
  8.0 0.0 copy-start
  8.0 0.0 copy-start.1
  8.0 0.0 all-reduce.4.cloned.1.call-start
  8.1 5.0 %collective-permute-start = (bf16[768,128]{1,0:T(8,128)(2,1)}, bf16[768,128]{1,0:T(8,128)(2,1)S(1)}, u32[]{:S(2)}, u32[]{:S(2)}) collective-permute-start(bf16[768,128]{1,0:T(8,128)(2,1)} %bitcast.56), channel_id=1, source_target_pairs={{0,16},{1,17},{2,18},{3,19},{4,20},{5,21},{6,22},{7,23},{8,24},{9,... | collective-permute-start | bytes 589832 | tf_op jit(solution)/shard_map/ppermute | solution.py:12
  13.1 1.7 convolution_bitcast_fusion.3
  14.8 2.7 %collective-permute-done = bf16[768,128]{1,0:T(8,128)(2,1)S(1)} collective-permute-done((bf16[768,128]{1,0:T(8,128)(2,1)}, bf16[768,128]{1,0:T(8,128)(2,1)S(1)}, u32[]{:S(2)}, u32[]{:S(2)}) %collective-permute-start) | collective-permute-done | bytes 196640 | tf_op jit(solution)/shard_map/ppermute | solution.py:12
  17.5 0.0 copy-done.1
  17.5 0.5 convolution_bitcast_fusion.2
  18.0 0.0 copy-start.3
  18.0 0.9 pad_maximum_fusion
  19.0 0.0 all-reduce.4.cloned.1.call-update
  19.0 0.0 reduce-scatter.7.cloned.1.call-start
  19.0 76.9 %all-reduce.4.cloned.1.call-done = f32[2,768,128]{2,1,0:T(8,128)} async-done(((f32[2,768,128]{2,1,0:T(8,128)}), f32[2,768,128]{2,1,0:T(8,128)}) %all-reduce.4.cloned.1.call-update) | async-done | bytes 786448 | tf_op jit(solution)/shard_map/psum | solution.py:30
  96.0 0.0 copy-done
  96.0 0.0 copy-done.3
  96.0 1.5 convolution_bitcast_fusion.1
  97.5 0.9 copy.13
  98.4 0.0 reduce-scatter.7.cloned.1.call-update
  98.5 0.0 all-reduce.6.cloned.1.call-start
  98.5 1.1 bitcast_select_fusion
  99.6 0.0 all-reduce.6.cloned.1.call-update
  99.7 0.0 copy-start.2
  99.7 0.0 all-reduce.8.cloned.1.call-start
  99.7 19.5 %reduce-scatter.7.cloned.1.call-done = f32[192,128]{1,0:T(8,128)} async-done(((f32[768,128]{1,0:T(8,128)}), f32[192,128]{1,0:T(8,128)}) %reduce-scatter.7.cloned.1.call-update) | async-done | bytes 98320 | tf_op jit(solution)/shard_map/reduce_scatter | solution.py:42
  119.2 0.9 convert_element_type.34
  120.1 5.6 %all_gather.6 = bf16[768,128]{1,0:T(8,128)(2,1)S(1)} all-gather(bf16[192,128]{1,0:T(8,128)(2,1)S(1)} %convert_element_type.34), channel_id=1, replica_groups=mesh['delay'=2,'row'=4,'col'=4] {'row'}, dimensions={0}, use_global_device_ids=true | all-gather | bytes 245760 | tf_op jit(solution)/shard_map/all_gather | solution.py:48
  125.7 17.5 %all-reduce.6.cloned.1.call-done = bf16[768,768]{1,0:T(8,128)(2,1)} async-done(((bf16[768,768]{1,0:T(8,128)(2,1)}), bf16[768,768]{1,0:T(8,128)(2,1)}) %all-reduce.6.cloned.1.call-update) | async-done | bytes 1179664 | tf_op jit(solution)/shard_map/psum | solution.py:17
  143.2 2.4 %convolution_convert_fusion = bf16[768,128]{1,0:T(8,128)(2,1)} fusion(bf16[768,768]{1,0:T(8,128)(2,1)} %all-reduce.6.cloned.1.call-done, bf16[768,128]{1,0:T(8,128)(2,1)S(1)} %all_gather.6), kind=kOutput, calls=%fused_computation.7 | convolution fusion | flops 151093248 | bytes 1572864 | tf_op jit(solution)/shard_map/dot_general | solution.py:37
  145.6 0.0 all-reduce.8.cloned.1.call-update
  145.6 0.0 reduce-scatter.9.cloned.1.call-start
  145.7 35.1 %all-reduce.8.cloned.1.call-done = bf16[768,128]{1,0:T(8,128)(2,1)} async-done(((bf16[768,128]{1,0:T(8,128)(2,1)}), bf16[768,128]{1,0:T(8,128)(2,1)}) %all-reduce.8.cloned.1.call-update) | async-done | bytes 196624 | tf_op jit(solution)/shard_map/psum | solution.py:40
  180.7 0.0 copy-done.2
  180.7 1.4 convolution_bitcast_fusion
  182.2 0.0 copy-start.4
  182.2 0.9 copy.15
  183.1 0.0 reduce-scatter.9.cloned.1.call-update
  183.1 0.0 copy-done.4
  183.2 0.7 collective-permute-start.1
  183.8 19.8 %reduce-scatter.9.cloned.1.call-done = f32[192,128]{1,0:T(8,128)} async-done(((f32[768,128]{1,0:T(8,128)}), f32[192,128]{1,0:T(8,128)}) %reduce-scatter.9.cloned.1.call-update) | async-done | bytes 98320 | tf_op jit(solution)/shard_map/reduce_scatter | solution.py:42
  203.7 0.9 convert_element_type.40
  204.6 5.6 %all_gather.7 = bf16[768,128]{1,0:T(8,128)(2,1)S(1)} all-gather(bf16[192,128]{1,0:T(8,128)(2,1)S(1)} %convert_element_type.40), channel_id=1, replica_groups=mesh['delay'=2,'row'=4,'col'=4] {'row'}, dimensions={0}, use_global_device_ids=true | all-gather | bytes 245760 | tf_op jit(solution)/shard_map/all_gather | solution.py:48
  210.2 0.8 pad_maximum_fusion.1
  210.9 0.0 collective-permute-done.1
  210.9 0.8 fusion.12
Async XLA Ops:
  8.0 88.0 %copy-start = (bf16[768,768]{1,0:T(8,128)(2,1)S(1)}, bf16[768,768]{1,0:T(8,128)(2,1)}, u32[]{:S(2)}) copy-start(bf16[768,768]{1,0:T(8,128)(2,1)} %param.6) | copy-start | bytes 3538948
  8.0 9.5 %copy-start.1 = (bf16[1,768,768]{2,1,0:T(8,128)(2,1)S(1)}, bf16[1,768,768]{2,1,0:T(8,128)(2,1)}, u32[]{:S(2)}) copy-start(bf16[1,768,768]{2,1,0:T(8,128)(2,1)} %param.5) | copy-start | bytes 3538948
  8.0 87.9 %all-reduce.4.cloned.1.call-start = ((), (), s32[]{:S(2)}) async-start(), calls=%async_computation.2 | async-start | bytes 1572864 | tf_op jit(solution)/shard_map/psum | solution.py:30
  8.1 9.5 %collective-permute-start = (bf16[768,128]{1,0:T(8,128)(2,1)}, bf16[768,128]{1,0:T(8,128)(2,1)S(1)}, u32[]{:S(2)}, u32[]{:S(2)}) collective-permute-start(bf16[768,128]{1,0:T(8,128)(2,1)} %bitcast.56), channel_id=1, source_target_pairs={{0,16},{1,17},{2,18},{3,19},{4,20},{5,21},{6,22},{7,23},{8,24},{9,... | collective-permute-start | bytes 589832 | tf_op jit(solution)/shard_map/ppermute | solution.py:12
  18.0 78.0 %copy-start.3 = (bf16[2,768,128]{2,1,0:T(8,128)(2,1)S(1)}, bf16[2,768,128]{2,1,0:T(8,128)(2,1)}, u32[]{:S(2)}) copy-start(bf16[2,768,128]{2,1,0:T(8,128)(2,1)} %param.4) | copy-start | bytes 1179652
  19.0 100.2 %reduce-scatter.7.cloned.1.call-start = ((), (), s32[]{:S(2)}) async-start(), calls=%async_computation.5 | async-start | bytes 491520 | tf_op jit(solution)/shard_map/reduce_scatter | solution.py:42
  98.5 44.7 %all-reduce.6.cloned.1.call-start = ((), (), s32[]{:S(2)}) async-start(), calls=%async_computation.3 | async-start | bytes 2359296 | tf_op jit(solution)/shard_map/psum | solution.py:17
  99.7 81.1 %copy-start.2 = (f32[2,768,128]{2,1,0:T(8,128)S(1)}, f32[2,768,128]{2,1,0:T(8,128)}, u32[]{:S(2)}) copy-start(f32[2,768,128]{2,1,0:T(8,128)} %all-reduce.4.cloned.1.call-done) | copy-start | bytes 2359300
  99.7 81.1 %all-reduce.8.cloned.1.call-start = ((), (), s32[]{:S(2)}) async-start(), calls=%async_computation.4 | async-start | bytes 393216 | tf_op jit(solution)/shard_map/psum | solution.py:40
  145.6 58.0 %reduce-scatter.9.cloned.1.call-start = ((), (), s32[]{:S(2)}) async-start(), calls=%async_computation.6 | async-start | bytes 491520 | tf_op jit(solution)/shard_map/reduce_scatter | solution.py:42
  182.2 1.0 copy-start.4
  183.2 27.8 %collective-permute-start.1 = (bf16[768,128]{1,0:T(8,128)(2,1)S(1)}, bf16[768,128]{1,0:T(8,128)(2,1)S(1)}, u32[]{:S(2)}, u32[]{:S(2)}) collective-permute-start(bf16[768,128]{1,0:T(8,128)(2,1)S(1)} %bitcast.57), channel_id=1, source_target_pairs={} | collective-permute-start | bytes 589832 | tf_op jit(solution)/shard_map/ppermute | solution.py:12
Sparse Core Ops, SparseCore 0:
  19.1 76.8 all-reduce.3
  99.2 19.9 reduce-scatter.6
  183.3 20.3 reduce-scatter.8
Sparse Core Ops, SparseCore 1:
  101.3 41.8 all-reduce.5
  145.9 34.7 all-reduce.7
where the time goes:
time: 219 us
  waiting for transfers between devices  172 us (79%)
  between operations  15.3 us (7%)
  blocking collectives  11.2 us (5%)
  matrix products  7.63 us (3%)
  starting transfers between devices  5.89 us (3%)
  other arithmetic  5.38 us (2%)
    psum x1, waiting for transfers between devices, on_device(): older_total = lax.psum(jnp.stack(terms), ('delay', 'col'))  76.9 us
    reduce_scatter x2, waiting for transfers between devices, on_device(): lax.psum_scatter(jnp.dot(inverse_op, rhs, preferred_element_type=jnp.floa...  39.3 us
    psum x1, waiting for transfers between devices, on_device(): lax.psum(recent.astype(jnp.bfloat16), 'col').astype(jnp.float32)  35.1 us
    psum x1, waiting for transfers between devices, spread(): return lax.psum(block, axis)  17.5 us
    all_gather x2, blocking collectives, on_device(): produced.append(lax.all_gather(mine, 'row', axis=0, tiled=True))  11.2 us
    ppermute x2, starting transfers between devices, from_behind(): return lax.ppermute(block, axis, route)  5.68 us
  transfers between devices with their start and end apart: 7, of which 6 were waited for; matrix products, arithmetic and copies ran while one was open for 2% of the time, Pallas kernels for 0%

commit v1 on v0

v1 whole, which is shorter than its diff:
```python
import jax
import jax.numpy as jnp
from jax import lax
from jax.sharding import PartitionSpec as P

F32 = jnp.float32
BF16 = jnp.bfloat16


def routes(axis):
    n = lax.axis_size(axis)
    if n & (n - 1) == 0:
        return [[(i, i ^ k) for i in range(n)] for k in range(1, n)]
    return [[(i, (i + k) % n) for i in range(n)] for k in range(1, n)]


def tree_sum(blocks):
    while len(blocks) > 1:
        pairs = [a + b for a, b in zip(blocks[::2], blocks[1::2])]
        blocks = pairs + ([blocks[-1]] if len(blocks) % 2 else [])
    return blocks[0]


def exchange_sum(block, axis):
    block = lax.optimization_barrier(block)
    blocks = [block] + [lax.ppermute(block, axis, route) for route in routes(axis)]
    return tree_sum([b.astype(F32) for b in blocks])


def piece(block, index, rows):
    return lax.dynamic_slice_in_dim(block, index * rows, rows, 0)


def scatter_sum(block, axis):
    n = lax.axis_size(axis)
    rows = block.shape[0] // n
    me = lax.axis_index(axis)
    parts = [piece(block, me, rows)]
    for route in routes(axis):
        target = jnp.array([t for _, t in route])[me]
        parts.append(lax.ppermute(piece(block, target, rows), axis, route))
    return tree_sum([p.astype(F32) for p in parts])


def gather(block, axis):
    n = lax.axis_size(axis)
    rows = block.shape[0]
    me = lax.axis_index(axis)
    whole = jnp.zeros((n * rows,) + block.shape[1:], block.dtype)
    whole = lax.dynamic_update_slice_in_dim(whole, block, me * rows, 0)
    for route in routes(axis):
        source = jnp.array([s for s, _ in sorted(route, key=lambda pair: pair[1])])[me]
        whole = lax.dynamic_update_slice_in_dim(whole, lax.ppermute(block, axis, route), source * rows, 0)
    return whole


def from_behind(block, axis, distance):
    n = lax.axis_size(axis)
    route = [(i - distance, i) for i in range(n) if i >= distance]
    return lax.ppermute(block, axis, route) if route else jnp.zeros_like(block)


def spread(block, axis, source):
    me = lax.axis_index(axis)
    out = block
    for target in range(lax.axis_size(axis)):
        if target != source:
            out = jnp.where(me == target, lax.ppermute(block, axis, [(source, target)]), out)
    return out


def times_transposed(a, b):
    return lax.dot_general(a, b, (((1,), (1,)), ((), ())), preferred_element_type=F32)


def on_device(excitation, delay_ops, inverse_op, history):
    steps, _, exc = excitation.shape
    operator, stored = delay_ops[0], history[0]
    nd = lax.axis_size("delay")
    me = lax.axis_index("delay")
    share = exc // nd
    stored_t = stored.T
    older = [scatter_sum(times_transposed(stored_t, operator).astype(BF16), "delay")]
    for step in range(1, steps):
        earlier = from_behind(stored_t, "delay", step)
        older.append(scatter_sum(times_transposed(earlier, operator).astype(BF16), "delay"))
    shortest = [spread(operator, "delay", lag) for lag in range(min(steps - 1, nd))]
    incident = [piece(excitation[step].T, me, share).astype(F32) for step in range(steps)]
    produced = []
    for step in range(steps):
        total = older[step]
        for lag in range(min(step, nd)):
            total = total + times_transposed(produced[step - 1 - lag], shortest[lag])
        retarded = exchange_sum(total.astype(BF16), "col")
        rhs = (incident[step] - retarded).astype(BF16)
        current = exchange_sum(times_transposed(rhs, inverse_op).astype(BF16), "row").astype(BF16)
        produced.append(current)
    whole = [gather(current, "delay").T for current in produced]
    currents = jnp.stack(whole)
    newest_first = jnp.stack(whole[::-1])
    picked = lax.dynamic_index_in_dim(newest_first, jnp.clip(me, 0, steps - 1), 0, keepdims=False)
    if nd > steps:
        picked = jnp.where(me < steps, picked, from_behind(stored, "delay", steps))
    return currents, picked[None]


def solution(mesh):
    in_specs = (
        P(None, "row", None),
        P("delay", "row", "col"),
        P("col", "row"),
        P("delay", "col", None),
    )
    out_specs = (P(None, "col", None), P("delay", "col", None))
    return jax.shard_map(
        on_device, mesh=mesh, in_specs=in_specs, out_specs=out_specs, check_vma=False
    )
```

time: 219 us -> 76.2 us (0.35)
  waiting for transfers between devices: 172 us -> 23.4 us
  starting transfers between devices: 5.89 us -> 24.9 us
  between operations: 15.3 us -> 1.53 us
  local copies, waits for them, and re-layouts: 1.86 us -> 15.2 us
  blocking collectives: 11.2 us -> 0 us
    psum x3 -> x0, waiting for transfers between devices: 129 us -> none  [the longest x1 76.9 us: on_device(): older_total = lax.psum(jnp.stack(terms), ('delay', 'col'))]
    reduce_scatter x2 -> x0, waiting for transfers between devices: 39.3 us -> none  [on_device(): lax.psum_scatter(jnp.dot(inverse_op, rhs, preferred_element_type=jnp.floa...]
    ppermute x2 -> x18, waiting for transfers between devices: 2.69 us -> 23.4 us  [the longest x12 16.6 us: exchange_sum(): lax.ppermute(block, axis, route)]
    ppermute x2 -> x18, starting transfers between devices: 5.68 us -> 24.9 us  [the longest x12 12.9 us: exchange_sum(): lax.ppermute(block, axis, route)]
    all_gather x2 -> x0, blocking collectives: 11.2 us -> none  [on_device(): produced.append(lax.all_gather(mine, 'row', axis=0, tiled=True))]
    dynamic_update_slice x0 -> x4, local copies, waits for them, and re-layouts: none -> 7.95 us  [the longest x2 4.8 us: gather(): lax.dynamic_update_slice_in_dim(whole, lax.ppermute(block, axis, route),...]
  transfers between devices with their start and end apart: 7 -> 18, of which waited for: 6 -> 8; matrix products, arithmetic and copies ran while one was open for 2% -> 20% of each run, Pallas kernels for 0% -> 0%
where the time goes in v1:
time: 76.2 us; the launch traced here: 75.8 us
  starting transfers between devices  24.9 us (33%)
  waiting for transfers between devices  23.4 us (31%)
  local copies, waits for them, and re-layouts  15.2 us (20%)
  matrix products  7.51 us (10%)
  other arithmetic  3.24 us (4%)
  between operations  1.53 us (2%)
    ppermute x12, waiting for transfers between devices, exchange_sum(): lax.ppermute(block, axis, route)  16.6 us
    ppermute x12, starting transfers between devices, exchange_sum(): lax.ppermute(block, axis, route)  12.9 us
    dot_general x5, matrix products, times_transposed(): lax.dot_general(a, b, (((1,), (1,)), ((), ())), preferred_element_type=F32)  7.51 us
    ppermute x2, waiting for transfers between devices, scatter_sum(): parts.append(lax.ppermute(piece(block, target, rows), axis, route))  6.76 us
    ppermute x2, starting transfers between devices, gather(): lax.ppermute(block, axis, route)  5.02 us
    dynamic_update_slice x2, local copies, waits for them, and re-layouts, gather(): lax.dynamic_update_slice_in_dim(whole, lax.ppermute(block, axis, route),...  4.8 us
    dynamic_update_slice x2, local copies, waits for them, and re-layouts, gather(): whole = lax.dynamic_update_slice_in_dim(whole, block, me * rows, 0)  3.15 us
    ppermute x2, starting transfers between devices, scatter_sum(): parts.append(lax.ppermute(piece(block, target, rows), axis, route))  3.04 us
  transfers between devices with their start and end apart: 18, of which 8 were waited for; matrix products, arithmetic and copies ran while one was open for 20% of the time, Pallas kernels for 0%

profile of v1, /device:TPU:0, one launch (start us, length us, event | category | flops | bytes accessed | tf_op | source)
XLA Modules:
  0.0 75.8 jit_solution(16061470125455975474)
XLA Ops:
  0.7 1.4 %dynamic_slice.31 = s32[1]{0:T(128)} dynamic-slice(s32[2]{0:T(128)} %constant.32.clone, s32[]{:T(128)S(6)} %select_n.37), dynamic_slice_sizes={1} | dynamic-slice | bytes 12 | tf_op jit(solution)/shard_map/dynamic_slice | solution.py:40
  2.7 2.0 %convolution_convert_fusion.1 = bf16[128,768]{1,0:T(8,128)(2,1)S(1)} fusion(bf16[1,768,128]{2,1,0:T(8,128)(2,1)} %param.11, bf16[1,768,768]{2,1,0:T(8,128)(2,1)} %param.9), kind=kOutput, calls=%fused_computation.4 | convolution fusion | flops 151093248 | bytes 1572864 | tf_op jit(solution)/shard_map/dot_general | solution.py:73
  4.7 0.7 constant_dynamic-slice_fusion.2
  5.4 3.0 %collective-permute-start = (bf16[64,768]{1,0:T(8,128)(2,1)}, bf16[64,768]{1,0:T(8,128)(2,1)}, u32[]{:S(2)}, u32[]{:S(2)}) collective-permute-start(bf16[64,768]{1,0:T(8,128)(2,1)} %constant_dynamic-slice_fusion.2), channel_id=1, source_target_pairs={{0,16},{16,0},{1,17},{17,1},{2,18},{18,2},{3,19},{19,3},{4,20},{20... | collective-permute-start | bytes 294920 | tf_op jit(solution)/shard_map/ppermute | solution.py:41
  8.4 2.6 %collective-permute-start.8 = (bf16[128,768]{0,1:T(8,128)(2,1)}, bf16[128,768]{0,1:T(8,128)(2,1)}, u32[]{:S(2)}, u32[]{:S(2)}) collective-permute-start(bf16[128,768]{0,1:T(8,128)(2,1)} %bitcast.9), channel_id=1, source_target_pairs={{0,16},{1,17},{2,18},{3,19},{4,20},{5,21},{6,22},{7,23},{8,24},{9,... | collective-permute-start | bytes 589832 | tf_op jit(solution)/shard_map/ppermute | solution.py:60
  11.0 1.4 %collective-permute-start.10 = (bf16[768,768]{1,0:T(8,128)(2,1)S(1)}, bf16[768,768]{1,0:T(8,128)(2,1)S(1)}, u32[]{:S(2)}, u32[]{:S(2)}) collective-permute-start(bf16[768,768]{1,0:T(8,128)(2,1)S(1)} %bitcast.53), channel_id=1, source_target_pairs={{0,16},{1,17},{2,18},{3,19},{4,20},{5,21},{6,22},{7,23},{8,24},{9,... | collective-permute-start | bytes 3538952 | tf_op jit(solution)/shard_map/ppermute | solution.py:68
  12.3 0.8 fusion.18
  13.1 1.6 %add_convert_fusion.3 = bf16[64,768]{1,0:T(8,128)(2,1)} fusion(bf16[64,768]{1,0:T(8,128)(2,1)} %collective-permute-done, bf16[128,768]{1,0:T(8,128)(2,1)} %copy-done.4, s32[]{:T(128)S(6)} %select_n.36), kind=kLoop, calls=%fused_computation.21 | loop fusion | flops 196608 | bytes 294916 | tf_op jit(solution)/shard_map/convert_element_type | solution.py:94
  14.7 2.1 %collective-permute-start.1 = (bf16[64,768]{1,0:T(8,128)(2,1)}, bf16[64,768]{1,0:T(8,128)(2,1)}, u32[]{:S(2)}, u32[]{:S(2)}) collective-permute-start(bf16[64,768]{1,0:T(8,128)(2,1)} %add_convert_fusion.3), channel_id=1, source_target_pairs={{0,1},{1,0},{2,3},{3,2},{4,5},{5,4},{6,7},{7,6},{8,9},{9,8},{10,11... | collective-permute-start | bytes 294920 | tf_op jit(solution)/shard_map/ppermute | solution.py:26
  16.7 2.6 %collective-permute-start.2 = (bf16[64,768]{1,0:T(8,128)(2,1)}, bf16[64,768]{1,0:T(8,128)(2,1)}, u32[]{:S(2)}, u32[]{:S(2)}) collective-permute-start(bf16[64,768]{1,0:T(8,128)(2,1)} %add_convert_fusion.3), channel_id=1, source_target_pairs={{0,2},{1,3},{2,0},{3,1},{4,6},{5,7},{6,4},{7,5},{8,10},{9,11},{10,... | collective-permute-start | bytes 294920 | tf_op jit(solution)/shard_map/ppermute | solution.py:26
  19.3 1.7 %constant_dynamic-slice_fusion.3 = bf16[1,768,64]{2,1,0:T(8,128)(2,1)} fusion(bf16[1,768,128]{2,1,0:T(8,128)(2,1)} %get-tuple-element.3, s32[]{:T(128)S(6)} %select_n.36), kind=kLoop, calls=%fused_computation.27 | loop fusion | bytes 196612 | tf_op jit(solution)/shard_map/dynamic-slice.2
  21.1 1.7 %copy.17 = bf16[1,768,64]{1,2,0:T(8,128)(2,1)} copy(bf16[1,768,64]{2,1,0:T(8,128)(2,1)} %constant_dynamic-slice_fusion.3) | data formatting | bytes 196608
  22.8 4.2 %collective-permute-done.2 = bf16[64,768]{1,0:T(8,128)(2,1)} collective-permute-done((bf16[64,768]{1,0:T(8,128)(2,1)}, bf16[64,768]{1,0:T(8,128)(2,1)}, u32[]{:S(2)}, u32[]{:S(2)}) %collective-permute-start.2) | collective-permute-done | bytes 98336 | tf_op jit(solution)/shard_map/ppermute | solution.py:26
  27.0 1.6 %convolution_convert_fusion.3 = bf16[64,768]{1,0:T(8,128)(2,1)S(1)} fusion(bf16[768,768]{1,0:T(8,128)(2,1)S(1)} %copy-done, bf16[64,768]{1,0:T(8,128)(2,1)} %collective-permute-done.3, bf16[64,768]{1,0:T(8,128)(2,1)} %collective-permute-done.2, bf16[64,768]{1,0:T(8,128)(2,1)} %collective-permute-done.1, bf16[64,768]{1,0:T(8,128)(2,1)} %add_convert_fusion.3, ...), kind=kOutput, calls=%fused_computation.6 | convolution fusion | flops 76038144 | bytes 1769472 | tf_op jit(solution)/shard_map/dot_general | solution.py:73
  28.5 0.1 collective-permute-start.4
  28.6 1.5 %collective-permute-start.5 = (bf16[64,768]{1,0:T(8,128)(2,1)S(1)}, bf16[64,768]{1,0:T(8,128)(2,1)S(1)}, u32[]{:S(2)}, u32[]{:S(2)}) collective-permute-start(bf16[64,768]{1,0:T(8,128)(2,1)S(1)} %convolution_convert_fusion.3), channel_id=1, source_target_pairs={{0,8},{4,12},{8,0},{12,4},{1,9},{5,13},{9,1},{13,5},{2,10},{6,14},... | collective-permute-start | bytes 294920 | tf_op jit(solution)/shard_map/ppermute | solution.py:26
  30.2 0.3 collective-permute-start.6
  30.5 1.5 %convolution_convert_fusion = bf16[128,768]{1,0:T(8,128)(2,1)S(1)} fusion(bf16[128,768]{0,1:T(8,128)(2,1)} %collective-permute-done.8, bf16[1,768,768]{2,1,0:T(8,128)(2,1)S(1)} %copy-done.1), kind=kOutput, calls=%fused_computation.3 | convolution fusion | flops 151093248 | bytes 1572864 | tf_op jit(solution)/shard_map/dot_general | solution.py:73
  32.0 0.1 collective-permute-start.9
  32.1 2.2 %collective-permute-done.5 = bf16[64,768]{1,0:T(8,128)(2,1)S(1)} collective-permute-done((bf16[64,768]{1,0:T(8,128)(2,1)S(1)}, bf16[64,768]{1,0:T(8,128)(2,1)S(1)}, u32[]{:S(2)}, u32[]{:S(2)}) %collective-permute-start.5) | collective-permute-done | bytes 98336 | tf_op jit(solution)/shard_map/ppermute | solution.py:26
  34.3 1.2 %collective-permute-done.6 = bf16[64,768]{1,0:T(8,128)(2,1)S(1)} collective-permute-done((bf16[64,768]{1,0:T(8,128)(2,1)S(1)}, bf16[64,768]{1,0:T(8,128)(2,1)S(1)}, u32[]{:S(2)}, u32[]{:S(2)}) %collective-permute-start.6) | collective-permute-done | bytes 98336 | tf_op jit(solution)/shard_map/ppermute | solution.py:26
  35.6 6.8 %collective-permute-done.9 = bf16[64,768]{1,0:T(8,128)(2,1)S(1)} collective-permute-done((bf16[64,768]{1,0:T(8,128)(2,1)S(1)}, bf16[64,768]{1,0:T(8,128)(2,1)S(1)}, u32[]{:S(2)}, u32[]{:S(2)}) %collective-permute-start.9) | collective-permute-done | bytes 98336 | tf_op jit(solution)/shard_map/ppermute | solution.py:41
  42.3 1.1 %add_convert_fusion.1 = bf16[64,768]{1,0:T(8,128)(2,1)} fusion(bf16[64,768]{1,0:T(8,128)(2,1)S(1)} %collective-permute-done.9, bf16[128,768]{1,0:T(8,128)(2,1)S(1)} %convolution_convert_fusion, s32[]{:T(128)S(6)} %select_n.36, bf16[64,768]{1,0:T(8,128)(2,1)S(1)} %add_convert_fusion.2, bf16[768,768]{1,0:T(8,128)(2,1)S(1)} %collective-permute-done.10, ...), kind=kOutput, calls=%fused_computation.19 | convolution fusion | flops 76333056 | bytes 2752517 | tf_op jit(solution)/shard_map/dot_general | solution.py:73
  43.5 1.6 %collective-permute-start.11 = (bf16[64,768]{1,0:T(8,128)(2,1)}, bf16[64,768]{1,0:T(8,128)(2,1)S(1)}, u32[]{:S(2)}, u32[]{:S(2)}) collective-permute-start(bf16[64,768]{1,0:T(8,128)(2,1)} %add_convert_fusion.1), channel_id=1, source_target_pairs={{0,1},{1,0},{2,3},{3,2},{4,5},{5,4},{6,7},{7,6},{8,9},{9,8},{10,11... | collective-permute-start | bytes 294920 | tf_op jit(solution)/shard_map/ppermute | solution.py:26
  45.0 2.6 %collective-permute-start.12 = (bf16[64,768]{1,0:T(8,128)(2,1)}, bf16[64,768]{1,0:T(8,128)(2,1)S(1)}, u32[]{:S(2)}, u32[]{:S(2)}) collective-permute-start(bf16[64,768]{1,0:T(8,128)(2,1)} %add_convert_fusion.1), channel_id=1, source_target_pairs={{0,2},{1,3},{2,0},{3,1},{4,6},{5,7},{6,4},{7,5},{8,10},{9,11},{10,... | collective-permute-start | bytes 294920 | tf_op jit(solution)/shard_map/ppermute | solution.py:26
  47.6 0.2 collective-permute-start.13
  47.9 0.1 constant_dynamic-slice_fusion.1
  48.0 0.1 copy.19
  48.1 1.1 %collective-permute-done.11 = bf16[64,768]{1,0:T(8,128)(2,1)S(1)} collective-permute-done((bf16[64,768]{1,0:T(8,128)(2,1)}, bf16[64,768]{1,0:T(8,128)(2,1)S(1)}, u32[]{:S(2)}, u32[]{:S(2)}) %collective-permute-start.11) | collective-permute-done | bytes 98336 | tf_op jit(solution)/shard_map/ppermute | solution.py:26
  49.2 5.4 %collective-permute-done.12 = bf16[64,768]{1,0:T(8,128)(2,1)S(1)} collective-permute-done((bf16[64,768]{1,0:T(8,128)(2,1)}, bf16[64,768]{1,0:T(8,128)(2,1)S(1)}, u32[]{:S(2)}, u32[]{:S(2)}) %collective-permute-start.12) | collective-permute-done | bytes 98336 | tf_op jit(solution)/shard_map/ppermute | solution.py:26
  54.6 1.4 %convolution_convert_fusion.2 = bf16[64,768]{1,0:T(8,128)(2,1)S(1)} fusion(bf16[768,768]{1,0:T(8,128)(2,1)S(1)} %copy-done, bf16[64,768]{1,0:T(8,128)(2,1)S(1)} %collective-permute-done.13, bf16[64,768]{1,0:T(8,128)(2,1)S(1)} %collective-permute-done.12, bf16[64,768]{1,0:T(8,128)(2,1)S(1)} %collective-permute-done.11, ...), kind=kOutput, calls=%fused_computation.5 | convolution fusion | flops 76038144 | bytes 1769472 | tf_op jit(solution)/shard_map/dot_general | solution.py:73
  56.0 0.1 collective-permute-start.14
  56.0 1.5 %collective-permute-start.15 = (bf16[64,768]{1,0:T(8,128)(2,1)S(1)}, bf16[64,768]{1,0:T(8,128)(2,1)S(1)}, u32[]{:S(2)}, u32[]{:S(2)}) collective-permute-start(bf16[64,768]{1,0:T(8,128)(2,1)S(1)} %convolution_convert_fusion.2), channel_id=1, source_target_pairs={{0,8},{4,12},{8,0},{12,4},{1,9},{5,13},{9,1},{13,5},{2,10},{6,14},... | collective-permute-start | bytes 294920 | tf_op jit(solution)/shard_map/ppermute | solution.py:26
  57.6 0.3 collective-permute-start.16
  57.9 2.5 %collective-permute-start.7 = (bf16[64,768]{1,0:T(8,128)(2,1)S(1)}, bf16[64,768]{1,0:T(8,128)(2,1)S(1)}, u32[]{:S(2)}, u32[]{:S(2)}) collective-permute-start(bf16[64,768]{1,0:T(8,128)(2,1)S(1)} %copy-done.3), channel_id=1, source_target_pairs={{0,16},{16,0},{1,17},{17,1},{2,18},{18,2},{3,19},{19,3},{4,20},{20... | collective-permute-start | bytes 294920 | tf_op jit(solution)/shard_map/ppermute | solution.py:53
  60.4 1.3 %collective-permute-done.15 = bf16[64,768]{1,0:T(8,128)(2,1)S(1)} collective-permute-done((bf16[64,768]{1,0:T(8,128)(2,1)S(1)}, bf16[64,768]{1,0:T(8,128)(2,1)S(1)}, u32[]{:S(2)}, u32[]{:S(2)}) %collective-permute-start.15) | collective-permute-done | bytes 98336 | tf_op jit(solution)/shard_map/ppermute | solution.py:26
  61.7 1.2 %collective-permute-done.16 = bf16[64,768]{1,0:T(8,128)(2,1)S(1)} collective-permute-done((bf16[64,768]{1,0:T(8,128)(2,1)S(1)}, bf16[64,768]{1,0:T(8,128)(2,1)S(1)}, u32[]{:S(2)}, u32[]{:S(2)}) %collective-permute-start.16) | collective-permute-done | bytes 98336 | tf_op jit(solution)/shard_map/ppermute | solution.py:26
  62.9 2.5 %collective-permute-start.17 = (bf16[64,768]{1,0:T(8,128)(2,1)S(1)}, bf16[64,768]{1,0:T(8,128)(2,1)S(1)}, u32[]{:S(2)}, u32[]{:S(2)}) collective-permute-start(bf16[64,768]{1,0:T(8,128)(2,1)S(1)} %add_convert_fusion), channel_id=1, source_target_pairs={{0,16},{16,0},{1,17},{17,1},{2,18},{18,2},{3,19},{19,3},{4,20},{20... | collective-permute-start | bytes 294920 | tf_op jit(solution)/shard_map/ppermute | solution.py:53
  65.5 0.2 copy.11
  65.7 1.6 %dynamic_update_slice.12 = bf16[128,768]{0,1:T(8,128)(2,1)S(1)} dynamic-update-slice(bf16[128,768]{0,1:T(8,128)(2,1)S(1)} %broadcast.3.clone.1, bf16[64,768]{0,1:T(8,128)(2,1)S(1)} %copy.11, s32[]{:T(128)S(6)} %select_n.36, s32[]{:T(128)} %constant.24.clone.1) | dynamic-update-slice | bytes 196612 | tf_op jit(solution)/shard_map/dynamic_update_slice | solution.py:50
  67.3 0.2 copy.12
  67.5 2.4 %dynamic_update_slice.13 = bf16[128,768]{0,1:T(8,128)(2,1)S(1)} dynamic-update-slice(bf16[128,768]{0,1:T(8,128)(2,1)S(1)} %dynamic_update_slice.12, bf16[64,768]{0,1:T(8,128)(2,1)S(1)} %copy.12, s32[]{:T(128)S(6)} %select_n.38, s32[]{:T(128)} %constant.24.clone.1) | dynamic-update-slice | bytes 196612 | tf_op jit(solution)/shard_map/dynamic_update_slice | solution.py:53
  69.9 0.2 copy.14
  70.1 1.6 %dynamic_update_slice.14 = bf16[128,768]{0,1:T(8,128)(2,1)S(1)} dynamic-update-slice(bf16[128,768]{0,1:T(8,128)(2,1)S(1)} %broadcast.3.clone, bf16[64,768]{0,1:T(8,128)(2,1)S(1)} %copy.14, s32[]{:T(128)S(6)} %select_n.36, s32[]{:T(128)} %constant.24.clone.1) | dynamic-update-slice | bytes 196612 | tf_op jit(solution)/shard_map/dynamic_update_slice | solution.py:50
  71.7 0.2 copy.15
  71.8 2.4 %dynamic_update_slice.15 = bf16[128,768]{0,1:T(8,128)(2,1)S(1)} dynamic-update-slice(bf16[128,768]{0,1:T(8,128)(2,1)S(1)} %dynamic_update_slice.14, bf16[64,768]{0,1:T(8,128)(2,1)S(1)} %copy.15, s32[]{:T(128)S(6)} %select_n.38, s32[]{:T(128)} %constant.24.clone.1) | dynamic-update-slice | bytes 196612 | tf_op jit(solution)/shard_map/dynamic_update_slice | solution.py:53
  74.2 0.8 %pad_maximum_fusion = bf16[2,768,128]{2,1,0:T(8,128)(2,1)} fusion(bf16[1,768,128]{2,1,0:T(8,128)(2,1)S(1)} %bitcast.54, bf16[1,768,128]{2,1,0:T(8,128)(2,1)S(1)} %bitcast.56), kind=kLoop, calls=%fused_computation.7 | loop fusion | flops 196608 | bytes 786432 | tf_op jit(solution)/shard_map/stack | solution.py:99
  75.0 0.8 fusion.3
  (30 shorter events, 0.3 us)
Async XLA Ops:
  0.6 26.3 %copy-start = (bf16[768,768]{1,0:T(8,128)(2,1)S(1)}, bf16[768,768]{1,0:T(8,128)(2,1)}, u32[]{:S(2)}) copy-start(bf16[768,768]{1,0:T(8,128)(2,1)} %param.10) | copy-start | bytes 3538948
  0.6 10.3 %copy-start.1 = (bf16[1,768,768]{2,1,0:T(8,128)(2,1)S(1)}, bf16[1,768,768]{2,1,0:T(8,128)(2,1)}, u32[]{:S(2)}) copy-start(bf16[1,768,768]{2,1,0:T(8,128)(2,1)} %param.9) | copy-start | bytes 3538948
  2.7 9.6 %copy-start.6 = (bf16[2,768,128]{2,1,0:T(8,128)(2,1)S(1)}, bf16[2,768,128]{2,1,0:T(8,128)(2,1)}, u32[]{:S(2)}) copy-start(bf16[2,768,128]{2,1,0:T(8,128)(2,1)} %param.8) | copy-start | bytes 1179652
  4.7 6.3 %copy-start.4 = (bf16[128,768]{1,0:T(8,128)(2,1)}, bf16[128,768]{1,0:T(8,128)(2,1)S(1)}, u32[]{:S(2)}) copy-start(bf16[128,768]{1,0:T(8,128)(2,1)S(1)} %convolution_convert_fusion.1) | copy-start | bytes 589828
  5.4 7.7 %collective-permute-start = (bf16[64,768]{1,0:T(8,128)(2,1)}, bf16[64,768]{1,0:T(8,128)(2,1)}, u32[]{:S(2)}, u32[]{:S(2)}) collective-permute-start(bf16[64,768]{1,0:T(8,128)(2,1)} %constant_dynamic-slice_fusion.2), channel_id=1, source_target_pairs={{0,16},{16,0},{1,17},{17,1},{2,18},{18,2},{3,19},{19,3},{4,20},{20... | collective-permute-start | bytes 294920 | tf_op jit(solution)/shard_map/ppermute | solution.py:41
  8.4 22.1 %collective-permute-start.8 = (bf16[128,768]{0,1:T(8,128)(2,1)}, bf16[128,768]{0,1:T(8,128)(2,1)}, u32[]{:S(2)}, u32[]{:S(2)}) collective-permute-start(bf16[128,768]{0,1:T(8,128)(2,1)} %bitcast.9), channel_id=1, source_target_pairs={{0,16},{1,17},{2,18},{3,19},{4,20},{5,21},{6,22},{7,23},{8,24},{9,... | collective-permute-start | bytes 589832 | tf_op jit(solution)/shard_map/ppermute | solution.py:60
  11.0 31.4 %collective-permute-start.10 = (bf16[768,768]{1,0:T(8,128)(2,1)S(1)}, bf16[768,768]{1,0:T(8,128)(2,1)S(1)}, u32[]{:S(2)}, u32[]{:S(2)}) collective-permute-start(bf16[768,768]{1,0:T(8,128)(2,1)S(1)} %bitcast.53), channel_id=1, source_target_pairs={{0,16},{1,17},{2,18},{3,19},{4,20},{5,21},{6,22},{7,23},{8,24},{9,... | collective-permute-start | bytes 3538952 | tf_op jit(solution)/shard_map/ppermute | solution.py:68
  14.7 8.1 %collective-permute-start.1 = (bf16[64,768]{1,0:T(8,128)(2,1)}, bf16[64,768]{1,0:T(8,128)(2,1)}, u32[]{:S(2)}, u32[]{:S(2)}) collective-permute-start(bf16[64,768]{1,0:T(8,128)(2,1)} %add_convert_fusion.3), channel_id=1, source_target_pairs={{0,1},{1,0},{2,3},{3,2},{4,5},{5,4},{6,7},{7,6},{8,9},{9,8},{10,11... | collective-permute-start | bytes 294920 | tf_op jit(solution)/shard_map/ppermute | solution.py:26
  16.7 10.2 %collective-permute-start.2 = (bf16[64,768]{1,0:T(8,128)(2,1)}, bf16[64,768]{1,0:T(8,128)(2,1)}, u32[]{:S(2)}, u32[]{:S(2)}) collective-permute-start(bf16[64,768]{1,0:T(8,128)(2,1)} %add_convert_fusion.3), channel_id=1, source_target_pairs={{0,2},{1,3},{2,0},{3,1},{4,6},{5,7},{6,4},{7,5},{8,10},{9,11},{10,... | collective-permute-start | bytes 294920 | tf_op jit(solution)/shard_map/ppermute | solution.py:26
  19.3 7.6 %collective-permute-start.3 = (bf16[64,768]{1,0:T(8,128)(2,1)}, bf16[64,768]{1,0:T(8,128)(2,1)}, u32[]{:S(2)}, u32[]{:S(2)}) collective-permute-start(bf16[64,768]{1,0:T(8,128)(2,1)} %add_convert_fusion.3), channel_id=1, source_target_pairs={{0,3},{1,2},{2,1},{3,0},{4,7},{5,6},{6,5},{7,4},{8,11},{9,10},{10,... | collective-permute-start | bytes 294920 | tf_op jit(solution)/shard_map/ppermute | solution.py:26
  28.5 3.5 %collective-permute-start.4 = (bf16[64,768]{1,0:T(8,128)(2,1)S(1)}, bf16[64,768]{1,0:T(8,128)(2,1)S(1)}, u32[]{:S(2)}, u32[]{:S(2)}) collective-permute-start(bf16[64,768]{1,0:T(8,128)(2,1)S(1)} %convolution_convert_fusion.3), channel_id=1, source_target_pairs={{0,4},{4,0},{8,12},{12,8},{1,5},{5,1},{9,13},{13,9},{2,6},{6,2},{1... | collective-permute-start | bytes 294920 | tf_op jit(solution)/shard_map/ppermute | solution.py:26
  28.6 5.7 %collective-permute-start.5 = (bf16[64,768]{1,0:T(8,128)(2,1)S(1)}, bf16[64,768]{1,0:T(8,128)(2,1)S(1)}, u32[]{:S(2)}, u32[]{:S(2)}) collective-permute-start(bf16[64,768]{1,0:T(8,128)(2,1)S(1)} %convolution_convert_fusion.3), channel_id=1, source_target_pairs={{0,8},{4,12},{8,0},{12,4},{1,9},{5,13},{9,1},{13,5},{2,10},{6,14},... | collective-permute-start | bytes 294920 | tf_op jit(solution)/shard_map/ppermute | solution.py:26
  30.2 5.3 %collective-permute-start.6 = (bf16[64,768]{1,0:T(8,128)(2,1)S(1)}, bf16[64,768]{1,0:T(8,128)(2,1)S(1)}, u32[]{:S(2)}, u32[]{:S(2)}) collective-permute-start(bf16[64,768]{1,0:T(8,128)(2,1)S(1)} %convolution_convert_fusion.3), channel_id=1, source_target_pairs={{0,12},{4,8},{8,4},{12,0},{1,13},{5,9},{9,5},{13,1},{2,14},{6,10},... | collective-permute-start | bytes 294920 | tf_op jit(solution)/shard_map/ppermute | solution.py:26
  32.0 10.3 %collective-permute-start.9 = (bf16[64,768]{1,0:T(8,128)(2,1)S(1)}, bf16[64,768]{1,0:T(8,128)(2,1)S(1)}, u32[]{:S(2)}, u32[]{:S(2)}) collective-permute-start(bf16[64,768]{1,0:T(8,128)(2,1)S(1)} %constant_dynamic-slice_fusion), channel_id=1, source_target_pairs={{0,16},{16,0},{1,17},{17,1},{2,18},{18,2},{3,19},{19,3},{4,20},{20... | collective-permute-start | bytes 294920 | tf_op jit(solution)/shard_map/ppermute | solution.py:41
  35.5 7.9 %copy-start.2 = (bf16[64,768]{1,0:T(8,128)(2,1)}, bf16[64,768]{1,0:T(8,128)(2,1)S(1)}, u32[]{:S(2)}) copy-start(bf16[64,768]{1,0:T(8,128)(2,1)S(1)} %add_convert_fusion.2) | copy-start | bytes 294916
  35.5 12.3 %copy-start.5 = (bf16[1,768,128]{2,1,0:T(8,128)(2,1)S(1)}, bf16[1,768,128]{2,1,0:T(8,128)(2,1)}, u32[]{:S(2)}) copy-start(bf16[1,768,128]{2,1,0:T(8,128)(2,1)} %get-tuple-element.2) | copy-start | bytes 589828
  43.5 5.7 %collective-permute-start.11 = (bf16[64,768]{1,0:T(8,128)(2,1)}, bf16[64,768]{1,0:T(8,128)(2,1)S(1)}, u32[]{:S(2)}, u32[]{:S(2)}) collective-permute-start(bf16[64,768]{1,0:T(8,128)(2,1)} %add_convert_fusion.1), channel_id=1, source_target_pairs={{0,1},{1,0},{2,3},{3,2},{4,5},{5,4},{6,7},{7,6},{8,9},{9,8},{10,11... | collective-permute-start | bytes 294920 | tf_op jit(solution)/shard_map/ppermute | solution.py:26
  45.0 9.5 %collective-permute-start.12 = (bf16[64,768]{1,0:T(8,128)(2,1)}, bf16[64,768]{1,0:T(8,128)(2,1)S(1)}, u32[]{:S(2)}, u32[]{:S(2)}) collective-permute-start(bf16[64,768]{1,0:T(8,128)(2,1)} %add_convert_fusion.1), channel_id=1, source_target_pairs={{0,2},{1,3},{2,0},{3,1},{4,6},{5,7},{6,4},{7,5},{8,10},{9,11},{10,... | collective-permute-start | bytes 294920 | tf_op jit(solution)/shard_map/ppermute | solution.py:26
  47.6 6.9 %collective-permute-start.13 = (bf16[64,768]{1,0:T(8,128)(2,1)}, bf16[64,768]{1,0:T(8,128)(2,1)S(1)}, u32[]{:S(2)}, u32[]{:S(2)}) collective-permute-start(bf16[64,768]{1,0:T(8,128)(2,1)} %add_convert_fusion.1), channel_id=1, source_target_pairs={{0,3},{1,2},{2,1},{3,0},{4,7},{5,6},{6,5},{7,4},{8,11},{9,10},{10,... | collective-permute-start | bytes 294920 | tf_op jit(solution)/shard_map/ppermute | solution.py:26
  47.9 10.0 %copy-start.3 = (bf16[64,768]{1,0:T(8,128)(2,1)S(1)}, bf16[64,768]{1,0:T(8,128)(2,1)}, u32[]{:S(2)}) copy-start(bf16[64,768]{1,0:T(8,128)(2,1)} %copy-done.2) | copy-start | bytes 294916
  56.0 4.4 %collective-permute-start.14 = (bf16[64,768]{1,0:T(8,128)(2,1)S(1)}, bf16[64,768]{1,0:T(8,128)(2,1)S(1)}, u32[]{:S(2)}, u32[]{:S(2)}) collective-permute-start(bf16[64,768]{1,0:T(8,128)(2,1)S(1)} %convolution_convert_fusion.2), channel_id=1, source_target_pairs={{0,4},{4,0},{8,12},{12,8},{1,5},{5,1},{9,13},{13,9},{2,6},{6,2},{1... | collective-permute-start | bytes 294920 | tf_op jit(solution)/shard_map/ppermute | solution.py:26
  56.0 5.7 %collective-permute-start.15 = (bf16[64,768]{1,0:T(8,128)(2,1)S(1)}, bf16[64,768]{1,0:T(8,128)(2,1)S(1)}, u32[]{:S(2)}, u32[]{:S(2)}) collective-permute-start(bf16[64,768]{1,0:T(8,128)(2,1)S(1)} %convolution_convert_fusion.2), channel_id=1, source_target_pairs={{0,8},{4,12},{8,0},{12,4},{1,9},{5,13},{9,1},{13,5},{2,10},{6,14},... | collective-permute-start | bytes 294920 | tf_op jit(solution)/shard_map/ppermute | solution.py:26
  57.6 5.3 %collective-permute-start.16 = (bf16[64,768]{1,0:T(8,128)(2,1)S(1)}, bf16[64,768]{1,0:T(8,128)(2,1)S(1)}, u32[]{:S(2)}, u32[]{:S(2)}) collective-permute-start(bf16[64,768]{1,0:T(8,128)(2,1)S(1)} %convolution_convert_fusion.2), channel_id=1, source_target_pairs={{0,12},{4,8},{8,4},{12,0},{1,13},{5,9},{9,5},{13,1},{2,14},{6,10},... | collective-permute-start | bytes 294920 | tf_op jit(solution)/shard_map/ppermute | solution.py:26
  57.9 9.4 %collective-permute-start.7 = (bf16[64,768]{1,0:T(8,128)(2,1)S(1)}, bf16[64,768]{1,0:T(8,128)(2,1)S(1)}, u32[]{:S(2)}, u32[]{:S(2)}) collective-permute-start(bf16[64,768]{1,0:T(8,128)(2,1)S(1)} %copy-done.3), channel_id=1, source_target_pairs={{0,16},{16,0},{1,17},{17,1},{2,18},{18,2},{3,19},{19,3},{4,20},{20... | collective-permute-start | bytes 294920 | tf_op jit(solution)/shard_map/ppermute | solution.py:53
  62.9 8.7 %collective-permute-start.17 = (bf16[64,768]{1,0:T(8,128)(2,1)S(1)}, bf16[64,768]{1,0:T(8,128)(2,1)S(1)}, u32[]{:S(2)}, u32[]{:S(2)}) collective-permute-start(bf16[64,768]{1,0:T(8,128)(2,1)S(1)} %add_convert_fusion), channel_id=1, source_target_pairs={{0,16},{16,0},{1,17},{17,1},{2,18},{18,2},{3,19},{19,3},{4,20},{20... | collective-permute-start | bytes 294920 | tf_op jit(solution)/shard_map/ppermute | solution.py:53

commit v2 on v1

--- a/solution.py
+++ b/solution.py
@@ -1,10 +1,15 @@
+import functools
+
 import jax
 import jax.numpy as jnp
 from jax import lax
+from jax.experimental import pallas as pl
+from jax.experimental.pallas import tpu as pltpu
 from jax.sharding import PartitionSpec as P
 
 F32 = jnp.float32
 BF16 = jnp.bfloat16
+TILE_ROWS = 16
 
 
 def routes(axis):
@@ -73,7 +78,7 @@
     return lax.dot_general(a, b, (((1,), (1,)), ((), ())), preferred_element_type=F32)
 
 
-def on_device(excitation, delay_ops, inverse_op, history):
+def general(excitation, delay_ops, inverse_op, history):
     steps, _, exc = excitation.shape
     operator, stored = delay_ops[0], history[0]
     nd = lax.axis_size("delay")
@@ -104,6 +109,226 @@
     return currents, picked[None]
 
 
+class Layout:
+    def __init__(self):
+        self.nd = lax.axis_size("delay")
+        self.nr = lax.axis_size("row")
+        self.nc = lax.axis_size("col")
+        self.near = 2 if self.nr % 2 == 0 else 1
+        self.far = self.nr // self.near
+        self.d = lax.axis_index("delay")
+        self.n = lax.axis_index("row") % self.near
+        self.z = lax.axis_index("col")
+
+    def move(self, block, kd=0, kf=0, kn=0, kz=0, only=None):
+        pairs = []
+        for d in range(self.nd) if only is None else only:
+            for r in range(self.nr):
+                for z in range(self.nc):
+                    to = ((d ^ kd) * self.nr + (r ^ (kf * self.near + kn))) * self.nc + (z ^ kz)
+                    pairs.append(((d * self.nr + r) * self.nc + z, to))
+        return lax.ppermute(block, ("delay", "row", "col"), pairs)
+
+    def owners(self):
+        return [(self.n ^ kn) * self.nd + (self.d ^ kd) for kn in range(self.near) for kd in range(self.nd)]
+
+
+def kernel_call(body, out_shape, info, inputs, loose=(), scratch=()):
+    vmem = pl.BlockSpec(memory_space=pltpu.VMEM)
+    return pl.pallas_call(
+        functools.partial(body, len(loose)),
+        out_shape=out_shape,
+        in_specs=[pl.BlockSpec(memory_space=pltpu.SMEM)] + [pl.BlockSpec(memory_space=pl.ANY)] * len(loose) + [vmem] * len(inputs),
+        out_specs=jax.tree.map(lambda _: vmem, out_shape),
+        scratch_shapes=list(scratch),
+        compiler_params=pltpu.CompilerParams(vmem_limit_bytes=24 << 20),
+    )(jnp.stack(info), *loose, *inputs)
+
+
+def total_of(refs):
+    return tree_sum([ref[...].astype(F32) for ref in refs])
+
+
+def part_of(ref, index, rows):
+    return ref[pl.ds(pl.multiple_of(index * rows, rows), rows), :]
+
+
+def begin_body(near, nd, loose, info, *refs):
+    past_ref, operator_ref, incident_ref = refs[:3]
+    count = near * nd
+    pieces, (part_ref, *waves), (total, turned, first, later) = refs[3 : 3 + count], refs[3 + count : -4], refs[-4:]
+    turned[...] = past_ref[...].astype(F32).T
+    total[...] = times_transposed(turned[...].astype(BF16), operator_ref[...])
+    first[...] = incident_ref[0].astype(F32).T * info[0].astype(F32)
+    rows = pieces[0].shape[0]
+    for kn in range(near):
+        for kd in range(nd):
+            k = kn * nd + kd
+            value = part_of(total, info[2 + k], rows)
+            if kd == 0:
+                value = value - part_of(first, info[2 + k], rows)
+            pieces[k][...] = value.astype(BF16)
+    later[...] = incident_ref[1].astype(F32).T
+    for kn in range(near):
+        waves[kn][...] = part_of(later, info[2 + kn * nd], rows).astype(BF16)
+    part_ref[...] = part_of(turned, info[1], part_ref.shape[0]).astype(BF16)
+
+
+def begin(lay, past, operator, incident):
+    columns, exc = past.shape
+    rows = operator.shape[0]
+    owners = lay.owners()
+    share = exc // len(owners)
+    info = [(lay.z == 0).astype(jnp.int32), lay.n, *owners]
+    out = [jax.ShapeDtypeStruct((share, rows), BF16)] * len(owners)
+    out += [jax.ShapeDtypeStruct((share * lay.nd, columns), BF16)]
+    out += [jax.ShapeDtypeStruct((share, rows), BF16)] * lay.near
+    scratch = [pltpu.VMEM((exc, rows), F32), pltpu.VMEM((exc, columns), F32)] + [pltpu.VMEM((exc, rows), F32)] * 2
+    got = kernel_call(functools.partial(begin_body, lay.near, lay.nd), out, info, (past, operator, incident), (), scratch)
+    return got[: len(owners)], got[len(owners)], got[len(owners) + 1 :]
+
+
+def join_body(near, waves, loose, info, *refs):
+    ins, taken, out = refs[loose : len(refs) - 1 - waves], refs[len(refs) - 1 - waves : -1], refs[-1]
+    per, rows = len(ins) // near, ins[0].shape[0]
+    for kn in range(near):
+        value = total_of(ins[kn * per : (kn + 1) * per])
+        if waves:
+            value = value - info[0].astype(F32) * jnp.concatenate([wave[...].astype(F32) for wave in taken], 0)
+        out[pl.ds(kn * rows, rows), :] = value.astype(BF16)
+
+
+def join(lay, groups, loose=(), waves=()):
+    rows, columns = groups[0][0].shape
+    out = jax.ShapeDtypeStruct((rows * len(groups), columns), BF16)
+    body = functools.partial(join_body, len(groups), len(waves))
+    info = [(lay.z == 0).astype(jnp.int32)]
+    return kernel_call(body, out, info, [b for g in groups for b in g] + list(waves), loose)
+
+
+def invert_body(near, loose, info, *refs):
+    parts, operators, out = refs[loose : -1 - near], refs[-1 - near : -1], refs[-1]
+    rhs = (-total_of(parts)).astype(BF16)
+    rows = rhs.shape[0] // near
+    out[...] = tree_sum(
+        [times_transposed(rhs[k * rows : (k + 1) * rows], op[...]) for k, op in enumerate(operators)]
+    ).astype(BF16)
+
+
+def invert(lay, parts, operators, loose=()):
+    out = jax.ShapeDtypeStruct((parts[0].shape[0] // lay.near, operators[0].shape[0]), BF16)
+    return kernel_call(functools.partial(invert_body, lay.near), out, [lay.d], (*parts, *operators), loose)
+
+
+def apply_body(near, nd, loose, info, *refs):
+    refs, (operand, value) = refs[loose:-2], refs[-2:]
+    refs, outs = refs[: -1 - nd], refs[-1 - nd :]
+    parts, past_ref, operators = refs[: -1 - near], refs[-1 - near], refs[-near:]
+    current_ref, totals = outs[0], outs[1:]
+    far = len(parts) // nd
+    rows = parts[0].shape[0]
+    for kd in range(nd):
+        current_ref[pl.ds(kd * rows, rows), :] = total_of(parts[kd * far : (kd + 1) * far]).astype(BF16)
+
+    @pl.when(info[0] == 0)
+    def _():
+        operand[...] = current_ref[...]
+
+    @pl.when(info[0] != 0)
+    def _():
+        operand[...] = past_ref[...]
+
+    for kn in range(near):
+        value[...] = times_transposed(operand[...], operators[kn][...])
+        for kd in range(nd):
+            totals[kd][pl.ds(kn * rows, rows), :] = part_of(value, info[0] ^ kd, rows).astype(BF16)
+
+
+def apply(lay, parts, past, operators):
+    rows, columns = parts[0].shape
+    out = [jax.ShapeDtypeStruct((rows * lay.nd, columns), BF16)]
+    out += [jax.ShapeDtypeStruct((rows * lay.near, operators[0].shape[0]), BF16)] * lay.nd
+    body = functools.partial(apply_body, lay.near, lay.nd)
+    scratch = [pltpu.VMEM(past.shape, BF16), pltpu.VMEM((rows * lay.nd, operators[0].shape[0]), F32)]
+    current, *totals = kernel_call(body, out, [lay.d], (*parts, past, *operators), (), scratch)
+    return current, totals
+
+
+def finish_body(steps, loose, info, *refs):
+    ins, (out, hist, total) = refs[loose:-3], refs[-3:]
+    per = len(ins) // steps
+    pieces = info.shape[0] - 1
+    rows = total.shape[0] // pieces
+    each = ins[0].shape[0] // rows
+    for step in range(steps):
+        for k in range(pieces):
+            start = pl.multiple_of(info[1 + k] * rows, rows)
+            block = ins[step * per + k // each][pl.ds((k % each) * rows, rows), :]
+            total[pl.ds(start, rows), :] = block.astype(F32)
+        turned = total[...].T.astype(BF16)
+        out[step] = turned
+
+        @pl.when(info[0] == steps - 1 - step)
+        def _():
+            hist[0] = turned
+
+
+def finish(lay, blocks):
+    steps = len(blocks)
+    columns, exc = blocks[0][0].shape[1], blocks[0][0].shape[0] * lay.near
+    shapes = [jax.ShapeDtypeStruct((k, columns, exc), BF16) for k in (steps, 1)]
+    flat = [b for g in blocks for b in g]
+    info = [lay.d, *lay.owners()]
+    return kernel_call(functools.partial(finish_body, steps), shapes, info, flat, (), [pltpu.VMEM((exc, columns), F32)])
+
+
+def over_rows(lay, partial):
+    return [
+        lay.move(partial, kd=kd, kf=kf) if kd or kf else partial for kd in range(lay.nd) for kf in range(lay.far)
+    ]
+
+
+def over_near(lay, block):
+    return [block] + [lay.move(block, kn=kn) for kn in range(1, lay.near)]
+
+
+def along_col(lay, total):
+    got = {kz: lay.move(total, kz=kz) for kz in reversed(range(1, lay.nc))}
+    return [total] + [got[kz] for kz in range(1, lay.nc)]
+
+
+def two_steps(excitation, delay_ops, inverse_op, history):
+    lay = Layout()
+    operator, stored = delay_ops[0], history[0]
+    pieces, part, waves = begin(lay, stored, operator, excitation)
+    got = [
+        [lay.move(pieces[kn * lay.nd + kd], kd=kd, kn=kn) if kd or kn else pieces[0] for kd in range(lay.nd)]
+        for kn in range(lay.near)
+    ]
+    inverse = over_near(lay, inverse_op)
+    total = join(lay, got)
+    past = from_behind(part, "delay", 1)
+    waves = [lay.move(wave, kn=kn) if kn else wave for kn, wave in enumerate(waves)]
+    direct = over_near(lay, operator)
+    partial = invert(lay, along_col(lay, total), inverse, ())
+    current, totals = apply(lay, over_rows(lay, partial), past, direct)
+    total = join(lay, [[lay.move(block, kd=kd) if kd else block for kd, block in enumerate(totals)]], (), waves)
+    partial = invert(lay, along_col(lay, total), inverse)
+    across = over_rows(lay, partial)
+    last = join(lay, [across[kd * lay.far : (kd + 1) * lay.far] for kd in range(lay.nd)])
+    return tuple(finish(lay, [over_near(lay, current), over_near(lay, last)]))
+
+
+def on_device(excitation, delay_ops, inverse_op, history):
+    sizes = [lax.axis_size(axis) for axis in ("delay", "row", "col")]
+    steps, _, exc = excitation.shape
+    follows = range(1, steps)
+    share = exc // (sizes[0] * 2)
+    if all(n & (n - 1) == 0 and n > 1 for n in sizes) and len(follows) == 1 and share and share % TILE_ROWS == 0:
+        return two_steps(excitation, delay_ops, inverse_op, history)
+    return general(excitation, delay_ops, inverse_op, history)
+
+
 def solution(mesh):
     in_specs = (
         P(None, "row", None),

time: 76.2 us -> 58.2 us (0.76)
  local copies, waits for them, and re-layouts: 15.2 us -> 3.37 us
  matrix products: 7.51 us -> 0 us
  Pallas kernels: 0 us -> 5.36 us
  other arithmetic: 3.24 us -> 0 us
  waiting for transfers between devices: 23.4 us -> 24.9 us
  starting transfers between devices: 24.9 us -> 23.6 us
  between operations: 1.53 us -> 0.71 us
    dynamic_update_slice x4 -> x0, local copies, waits for them, and re-layouts: 7.95 us -> none  [the longest x2 4.8 us: gather(): lax.dynamic_update_slice_in_dim(whole, lax.ppermute(block, axis, route),...]
    dot_general x5 -> x0, matrix products: 7.51 us -> none  [times_transposed(): lax.dot_general(a, b, (((1,), (1,)), ((), ())), preferred_element_type=F32)]
    pallas_call x0 -> x8, Pallas kernels: none -> 5.36 us  [kernel_call(): pl.pallas_call(functools.partial(body, len(loose)), out_shape=out_shape,...]
    dynamic_slice x3 -> x0, local copies, waits for them, and re-layouts: 2.12 us -> none  [the longest x1 1.39 us: scatter_sum(): target = jnp.array([t for _, t in route])[me]]
    another operation x4 -> x2, local copies, waits for them, and re-layouts: 1.9 us -> 0.17 us  [kernel_call(): jnp.stack(info)]
    convert_element_type x3 -> x0, other arithmetic: 1.7 us -> none  [the longest x1 1.6 us: on_device(): retarded = exchange_sum(total.astype(BF16), 'col')]
    ppermute x17 -> x21, waiting for transfers between devices: 23.4 us -> 24.9 us  [move(): return lax.ppermute(block, ('delay', 'row', 'col'), pairs)]
    another operation x2 -> x0, other arithmetic: 1.53 us -> none  [the longest x1 0.78 us: on_device(): currents = jnp.stack(whole)]
  transfers between devices with their start and end apart: 18 -> 22, of which waited for: 8 -> 15; matrix products, arithmetic and copies ran while one was open for 20% -> 0% of each run, Pallas kernels for 0% -> 3%
where the time goes in v2:
time: 58.2 us; the launch traced here: 58 us
  waiting for transfers between devices  24.9 us (43%)
  starting transfers between devices  23.6 us (41%)
  Pallas kernels  5.36 us (9%)
  local copies, waits for them, and re-layouts  3.37 us (6%)
  between operations  0.71 us (1%)
    ppermute x21, waiting for transfers between devices, move(): return lax.ppermute(block, ('delay', 'row', 'col'), pairs)  24.9 us
    ppermute x21, starting transfers between devices, move(): return lax.ppermute(block, ('delay', 'row', 'col'), pairs)  20.8 us
    pallas_call x8, Pallas kernels, kernel_call(): pl.pallas_call(functools.partial(body, len(loose)), out_shape=out_shape,...  5.36 us
    unnamed x10, local copies, waits for them, and re-layouts  3.2 us
    ppermute x1, starting transfers between devices, from_behind(): return lax.ppermute(block, axis, route) if route else jnp.zeros_like(block)  2.84 us
  transfers between devices with their start and end apart: 22, of which 15 were waited for; matrix products, arithmetic and copies ran while one was open for 0% of the time, Pallas kernels for 3%

profile of v2, /device:TPU:0, one launch (start us, length us, event | category | flops | bytes accessed | tf_op | source)
XLA Modules:
  0.0 58.0 jit_solution(11722495666583814061)
XLA Ops:
  0.6 0.5 collective-permute-start.6
  1.1 0.1 collective-permute-start.11
  1.2 0.1 stack.48.info
  1.3 1.3 %copy-done = bf16[1,768,768]{2,1,0:T(8,128)(2,1)S(1)} copy-done((bf16[1,768,768]{2,1,0:T(8,128)(2,1)S(1)}, bf16[1,768,768]{2,1,0:T(8,128)(2,1)}, u32[]{:S(2)}) %copy-start) | copy-done | bytes 1179672
  2.6 1.0 %copy-done.3 = bf16[2,768,128]{2,1,0:T(8,128)(2,1)S(1)} copy-done((bf16[2,768,128]{2,1,0:T(8,128)(2,1)S(1)}, bf16[2,768,128]{2,1,0:T(8,128)(2,1)}, u32[]{:S(2)}) %copy-start.3) | copy-done | bytes 393240
  3.6 0.9 %copy-done.4 = bf16[1,768,128]{2,1,0:T(8,128)(2,1)S(1)} copy-done((bf16[1,768,128]{2,1,0:T(8,128)(2,1)S(1)}, bf16[1,768,128]{2,1,0:T(8,128)(2,1)}, u32[]{:S(2)}) %copy-start.4) | copy-done | bytes 196632
  4.5 1.1 %shard_map.59 = (bf16[32,768]{1,0:T(8,128)(2,1)S(1)}, bf16[32,768]{1,0:T(8,128)(2,1)S(1)}, bf16[32,768]{1,0:T(8,128)(2,1)S(1)}, bf16[32,768]{1,0:T(8,128)(2,1)S(...) custom-call(s32[6]{0:T(128)S(1)} %stack.48.info, ...), custom_call_target="tpu_custom_call" | custom-call | tf_op jit(solution)/shard_map/pallas_call | solution.py:138
  5.6 3.0 %collective-permute-start = (bf16[32,768]{1,0:T(8,128)(2,1)S(1)}, bf16[32,768]{1,0:T(8,128)(2,1)S(1)}, u32[]{:S(2)}, u32[]{:S(2)}) collective-permute-start(bf16[32,768]{1,0:T(8,128)(2,1)S(1)} %get-tuple-element.13), channel_id=1, source_target_pairs={{0,16},{1,17},{2,18},{3,19},{4,20},{5,21},{6,22},{7,23},{8,24},{9,... | collective-permute-start | bytes 147464 | tf_op jit(solution)/shard_map/ppermute | solution.py:130
  8.7 0.2 collective-permute-start.2
  8.9 1.9 %collective-permute-done.refs_1_ = bf16[32,768]{1,0:T(8,128)(2,1)S(1)} collective-permute-done((bf16[32,768]{1,0:T(8,128)(2,1)S(1)}, bf16[32,768]{1,0:T(8,128)(2,1)S(1)}, u32[]{:S(2)}, u32[]{:S(2)}) %collective-permute-start) | collective-permute-done | bytes 49184 | tf_op jit(solution)/shard_map/ppermute | solution.py:130
  10.7 1.4 %collective-permute-done.2.refs_3_ = bf16[32,768]{1,0:T(8,128)(2,1)S(1)} collective-permute-done((bf16[32,768]{1,0:T(8,128)(2,1)S(1)}, bf16[32,768]{1,0:T(8,128)(2,1)S(1)}, u32[]{:S(2)}, u32[]{:S(2)}) %collective-permute-start.2) | collective-permute-done | bytes 49184 | tf_op jit(solution)/shard_map/ppermute | solution.py:130
  12.2 3.7 %collective-permute-start.5 = (bf16[64,768]{1,0:T(8,128)(2,1)S(1)}, bf16[64,768]{1,0:T(8,128)(2,1)S(1)}, u32[]{:S(2)}, u32[]{:S(2)}) collective-permute-start(bf16[64,768]{1,0:T(8,128)(2,1)S(1)} %shard_map.60.refs_0_), channel_id=1, source_target_pairs={{0,3},{1,2},{2,1},{3,0},{4,7},{5,6},{6,5},{7,4},{8,11},{9,10},{10,... | collective-permute-start | bytes 294920 | tf_op jit(solution)/shard_map/ppermute | solution.py:130
  15.9 0.0 collective-permute-start.4
  15.9 0.8 %collective-permute-start.3 = (bf16[64,768]{1,0:T(8,128)(2,1)S(1)}, bf16[64,768]{1,0:T(8,128)(2,1)S(1)}, u32[]{:S(2)}, u32[]{:S(2)}) collective-permute-start(bf16[64,768]{1,0:T(8,128)(2,1)S(1)} %shard_map.60.refs_0_), channel_id=1, source_target_pairs={{0,1},{1,0},{2,3},{3,2},{4,5},{5,4},{6,7},{7,6},{8,9},{9,8},{10,11... | collective-permute-start | bytes 294920 | tf_op jit(solution)/shard_map/ppermute | solution.py:130
  16.7 3.1 %collective-permute-done.5.refs_3_ = bf16[64,768]{1,0:T(8,128)(2,1)S(1)} collective-permute-done((bf16[64,768]{1,0:T(8,128)(2,1)S(1)}, bf16[64,768]{1,0:T(8,128)(2,1)S(1)}, u32[]{:S(2)}, u32[]{:S(2)}) %collective-permute-start.5) | collective-permute-done | bytes 98336 | tf_op jit(solution)/shard_map/ppermute | solution.py:130
  19.8 2.8 %collective-permute-start.10 = (bf16[64,768]{1,0:T(8,128)(2,1)S(1)}, bf16[64,768]{1,0:T(8,128)(2,1)S(1)}, u32[]{:S(2)}, u32[]{:S(2)}) collective-permute-start(bf16[64,768]{1,0:T(8,128)(2,1)S(1)} %get-tuple-element.16), channel_id=1, source_target_pairs={{0,16},{1,17},{2,18},{3,19},{4,20},{5,21},{6,22},{7,23},{8,24},{9,... | collective-permute-start | bytes 294920 | tf_op jit(solution)/shard_map/ppermute | solution.py:65
  22.6 2.2 %collective-permute-done.4.refs_2_ = bf16[64,768]{1,0:T(8,128)(2,1)S(1)} collective-permute-done((bf16[64,768]{1,0:T(8,128)(2,1)S(1)}, bf16[64,768]{1,0:T(8,128)(2,1)S(1)}, u32[]{:S(2)}, u32[]{:S(2)}) %collective-permute-start.4) | collective-permute-done | bytes 98336 | tf_op jit(solution)/shard_map/ppermute | solution.py:130
  24.8 0.0 collective-permute-done.3.refs_1_
  24.8 0.0 collective-permute-done.6.refs_5_
  24.8 0.0 copy-start.1
  24.8 0.8 %shard_map.61.refs_0_ = bf16[32,768]{1,0:T(8,128)(2,1)S(1)} custom-call(s32[1]{0:T(128)} %bitcast.info, bf16[64,768]{1,0:T(8,128)(2,1)S(1)} %shard_map.60.refs_0_, bf16[64,768]{1,0:T(8,128)(2,1)S(1)} %collective-permute-done.3.refs_1_, bf16[64,768]{1,0:T(8,128)(2,1)S(1)} %collective-permute-done.4.refs_2_, ...), custom_call_target="tpu_custom_call" | custom-call | tf_op jit(solution)/shard_map/pallas_call | solution.py:138
  25.6 1.8 %collective-permute-start.9 = (bf16[32,768]{1,0:T(8,128)(2,1)S(1)}, bf16[32,768]{1,0:T(8,128)(2,1)S(1)}, u32[]{:S(2)}, u32[]{:S(2)}) collective-permute-start(bf16[32,768]{1,0:T(8,128)(2,1)S(1)} %shard_map.61.refs_0_), channel_id=1, source_target_pairs={{0,24},{1,25},{2,26},{3,27},{4,28},{5,29},{6,30},{7,31},{8,16},{9,... | collective-permute-start | bytes 147464 | tf_op jit(solution)/shard_map/ppermute | solution.py:130
  27.5 1.2 %collective-permute-start.8 = (bf16[32,768]{1,0:T(8,128)(2,1)S(1)}, bf16[32,768]{1,0:T(8,128)(2,1)S(1)}, u32[]{:S(2)}, u32[]{:S(2)}) collective-permute-start(bf16[32,768]{1,0:T(8,128)(2,1)S(1)} %shard_map.61.refs_0_), channel_id=1, source_target_pairs={{0,16},{1,17},{2,18},{3,19},{4,20},{5,21},{6,22},{7,23},{8,24},{9,... | collective-permute-start | bytes 147464 | tf_op jit(solution)/shard_map/ppermute | solution.py:130
  28.6 0.5 collective-permute-start.7
  29.2 1.7 %collective-permute-done.9.refs_3_ = bf16[32,768]{1,0:T(8,128)(2,1)S(1)} collective-permute-done((bf16[32,768]{1,0:T(8,128)(2,1)S(1)}, bf16[32,768]{1,0:T(8,128)(2,1)S(1)}, u32[]{:S(2)}, u32[]{:S(2)}) %collective-permute-start.9) | collective-permute-done | bytes 49184 | tf_op jit(solution)/shard_map/ppermute | solution.py:130
  30.9 0.7 %collective-permute-done.8.refs_2_ = bf16[32,768]{1,0:T(8,128)(2,1)S(1)} collective-permute-done((bf16[32,768]{1,0:T(8,128)(2,1)S(1)}, bf16[32,768]{1,0:T(8,128)(2,1)S(1)}, u32[]{:S(2)}, u32[]{:S(2)}) %collective-permute-start.8) | collective-permute-done | bytes 49184 | tf_op jit(solution)/shard_map/ppermute | solution.py:130
  31.6 1.2 %collective-permute-done.7.refs_1_ = bf16[32,768]{1,0:T(8,128)(2,1)S(1)} collective-permute-done((bf16[32,768]{1,0:T(8,128)(2,1)S(1)}, bf16[32,768]{1,0:T(8,128)(2,1)S(1)}, u32[]{:S(2)}, u32[]{:S(2)}) %collective-permute-start.7) | collective-permute-done | bytes 49184 | tf_op jit(solution)/shard_map/ppermute | solution.py:130
  32.7 0.9 %shard_map.62 = (bf16[64,768]{1,0:T(8,128)(2,1)S(1)}, bf16[64,768]{1,0:T(8,128)(2,1)S(1)}, bf16[64,768]{1,0:T(8,128)(2,1)S(1)}) custom-call(s32[1]{0:T(128)} %bitcast.info, bf16[32,768]{1,0:T(8,128)(2,1)S(1)} %shard_map.61.refs_0_, bf16[32,768]{1,0:T(8,128)(2,1)S(1)} %collective-permute-done.7.refs_1_, bf16[32,768]{1,0:T(8,128)(2,1)S(1)} %collective-permute-done.8.refs_2_, ...), custom_call_target="tpu_custom_call" | custom-call | tf_op jit(solution)/shard_map/pallas_call | solution.py:138
  33.6 0.9 %collective-permute-start.13 = (bf16[64,768]{1,0:T(8,128)(2,1)S(1)}, bf16[64,768]{1,0:T(8,128)(2,1)S(1)}, u32[]{:S(2)}, u32[]{:S(2)}) collective-permute-start(bf16[64,768]{1,0:T(8,128)(2,1)S(1)} %get-tuple-element.19), channel_id=1, source_target_pairs={{0,16},{1,17},{2,18},{3,19},{4,20},{5,21},{6,22},{7,23},{8,24},{9,... | collective-permute-start | bytes 294920 | tf_op jit(solution)/shard_map/ppermute | solution.py:130
  34.5 0.0 collective-permute-start.14
  34.5 1.2 %collective-permute-done.14.refs_3_ = bf16[32,768]{1,0:T(8,128)(2,1)S(1)} collective-permute-done((bf16[32,768]{1,0:T(8,128)(2,1)S(1)}, bf16[32,768]{1,0:T(8,128)(2,1)S(1)}, u32[]{:S(2)}, u32[]{:S(2)}) %collective-permute-start.14) | collective-permute-done | bytes 49184 | tf_op jit(solution)/shard_map/ppermute | solution.py:130
  35.8 2.5 %collective-permute-done.13.refs_1_ = bf16[64,768]{1,0:T(8,128)(2,1)S(1)} collective-permute-done((bf16[64,768]{1,0:T(8,128)(2,1)S(1)}, bf16[64,768]{1,0:T(8,128)(2,1)S(1)}, u32[]{:S(2)}, u32[]{:S(2)}) %collective-permute-start.13) | collective-permute-done | bytes 98336 | tf_op jit(solution)/shard_map/ppermute | solution.py:130
  38.3 2.5 %collective-permute-start.17 = (bf16[64,768]{1,0:T(8,128)(2,1)S(1)}, bf16[64,768]{1,0:T(8,128)(2,1)S(1)}, u32[]{:S(2)}, u32[]{:S(2)}) collective-permute-start(bf16[64,768]{1,0:T(8,128)(2,1)S(1)} %shard_map.63.refs_0_), channel_id=1, source_target_pairs={{0,3},{1,2},{2,1},{3,0},{4,7},{5,6},{6,5},{7,4},{8,11},{9,10},{10,... | collective-permute-start | bytes 294920 | tf_op jit(solution)/shard_map/ppermute | solution.py:130
  40.9 0.8 %collective-permute-start.16 = (bf16[64,768]{1,0:T(8,128)(2,1)S(1)}, bf16[64,768]{1,0:T(8,128)(2,1)S(1)}, u32[]{:S(2)}, u32[]{:S(2)}) collective-permute-start(bf16[64,768]{1,0:T(8,128)(2,1)S(1)} %shard_map.63.refs_0_), channel_id=1, source_target_pairs={{0,2},{1,3},{2,0},{3,1},{4,6},{5,7},{6,4},{7,5},{8,10},{9,11},{10,... | collective-permute-start | bytes 294920 | tf_op jit(solution)/shard_map/ppermute | solution.py:130
  41.7 1.1 %collective-permute-start.15 = (bf16[64,768]{1,0:T(8,128)(2,1)S(1)}, bf16[64,768]{1,0:T(8,128)(2,1)S(1)}, u32[]{:S(2)}, u32[]{:S(2)}) collective-permute-start(bf16[64,768]{1,0:T(8,128)(2,1)S(1)} %shard_map.63.refs_0_), channel_id=1, source_target_pairs={{0,1},{1,0},{2,3},{3,2},{4,5},{5,4},{6,7},{7,6},{8,9},{9,8},{10,11... | collective-permute-start | bytes 294920 | tf_op jit(solution)/shard_map/ppermute | solution.py:130
  42.8 2.2 %collective-permute-done.17.refs_3_ = bf16[64,768]{1,0:T(8,128)(2,1)S(1)} collective-permute-done((bf16[64,768]{1,0:T(8,128)(2,1)S(1)}, bf16[64,768]{1,0:T(8,128)(2,1)S(1)}, u32[]{:S(2)}, u32[]{:S(2)}) %collective-permute-start.17) | collective-permute-done | bytes 98336 | tf_op jit(solution)/shard_map/ppermute | solution.py:130
  45.0 3.0 %collective-permute-done.16.refs_2_ = bf16[64,768]{1,0:T(8,128)(2,1)S(1)} collective-permute-done((bf16[64,768]{1,0:T(8,128)(2,1)S(1)}, bf16[64,768]{1,0:T(8,128)(2,1)S(1)}, u32[]{:S(2)}, u32[]{:S(2)}) %collective-permute-start.16) | collective-permute-done | bytes 98336 | tf_op jit(solution)/shard_map/ppermute | solution.py:130
  48.0 0.8 %shard_map.64.refs_0_ = bf16[32,768]{1,0:T(8,128)(2,1)S(1)} custom-call(s32[1]{0:T(128)} %bitcast.info, bf16[64,768]{1,0:T(8,128)(2,1)S(1)} %shard_map.63.refs_0_, bf16[64,768]{1,0:T(8,128)(2,1)S(1)} %collective-permute-done.15.refs_1_, bf16[64,768]{1,0:T(8,128)(2,1)S(1)} %collective-permute-done.16.refs_2_, ...), custom_call_target="tpu_custom_call" | custom-call | tf_op jit(solution)/shard_map/pallas_call | solution.py:138
  48.8 1.5 %collective-permute-start.20 = (bf16[32,768]{1,0:T(8,128)(2,1)S(1)}, bf16[32,768]{1,0:T(8,128)(2,1)S(1)}, u32[]{:S(2)}, u32[]{:S(2)}) collective-permute-start(bf16[32,768]{1,0:T(8,128)(2,1)S(1)} %shard_map.64.refs_0_), channel_id=1, source_target_pairs={{0,24},{1,25},{2,26},{3,27},{4,28},{5,29},{6,30},{7,31},{8,16},{9,... | collective-permute-start | bytes 147464 | tf_op jit(solution)/shard_map/ppermute | solution.py:130
  50.3 0.6 collective-permute-start.19
  50.8 1.5 %collective-permute-start.18 = (bf16[32,768]{1,0:T(8,128)(2,1)S(1)}, bf16[32,768]{1,0:T(8,128)(2,1)S(1)}, u32[]{:S(2)}, u32[]{:S(2)}) collective-permute-start(bf16[32,768]{1,0:T(8,128)(2,1)S(1)} %shard_map.64.refs_0_), channel_id=1, source_target_pairs={{0,8},{1,9},{2,10},{3,11},{4,12},{5,13},{6,14},{7,15},{8,0},{9,1},... | collective-permute-start | bytes 147464 | tf_op jit(solution)/shard_map/ppermute | solution.py:130
  52.3 1.5 %collective-permute-done.20.refs_3_ = bf16[32,768]{1,0:T(8,128)(2,1)S(1)} collective-permute-done((bf16[32,768]{1,0:T(8,128)(2,1)S(1)}, bf16[32,768]{1,0:T(8,128)(2,1)S(1)}, u32[]{:S(2)}, u32[]{:S(2)}) %collective-permute-start.20) | collective-permute-done | bytes 49184 | tf_op jit(solution)/shard_map/ppermute | solution.py:130
  53.8 0.5 collective-permute-done.19.refs_2_
  54.4 0.6 collective-permute-done.18.refs_1_
  55.0 0.1 collective-permute-start.21
  55.0 0.1 stack.44.info
  55.1 1.2 %collective-permute-done.21.refs_3_ = bf16[64,768]{1,0:T(8,128)(2,1)S(1)} collective-permute-done((bf16[64,768]{1,0:T(8,128)(2,1)S(1)}, bf16[64,768]{1,0:T(8,128)(2,1)S(1)}, u32[]{:S(2)}, u32[]{:S(2)}) %collective-permute-start.21) | collective-permute-done | bytes 98336 | tf_op jit(solution)/shard_map/ppermute | solution.py:130
  56.3 1.7 %shard_map.66 = (bf16[2,768,128]{2,1,0:T(8,128)(2,1)}, bf16[1,768,128]{2,1,0:T(8,128)(2,1)}) custom-call(s32[5]{0:T(128)S(1)} %stack.44.info, bf16[64,768]{1,0:T(8,128)(2,1)S(1)} %get-tuple-element.17.refs_0_, bf16[64,768]{1,0:T(8,128)(2,1)S(1)} %collective-permute-done.12.refs_1_, bf16[64,768]{1,0:T(8,128)(2,1)S(1)} %shard_map.65.refs_2_, ...), custom_call_target="tpu_custom_call" | custom-call | tf_op jit(solution)/shard_map/pallas_call | solution.py:138
  (16 shorter events, 0.1 us)
Async XLA Ops:
  0.6 24.2 %collective-permute-start.6 = (bf16[768,768]{1,0:T(8,128)(2,1)}, bf16[768,768]{1,0:T(8,128)(2,1)S(1)}, u32[]{:S(2)}, u32[]{:S(2)}) collective-permute-start(bf16[768,768]{1,0:T(8,128)(2,1)} %refs_4_.3), channel_id=1, source_target_pairs={{0,4},{1,5},{2,6},{3,7},{4,0},{5,1},{6,2},{7,3},{8,12},{9,13},{10,... | collective-permute-start | bytes 3538952 | tf_op jit(solution)/shard_map/ppermute | solution.py:130
  1.1 28.0 %collective-permute-start.11 = (bf16[768,768]{1,0:T(8,128)(2,1)}, bf16[768,768]{1,0:T(8,128)(2,1)S(1)}, u32[]{:S(2)}, u32[]{:S(2)}) collective-permute-start(bf16[768,768]{1,0:T(8,128)(2,1)} %bitcast.9), channel_id=1, source_target_pairs={{0,4},{1,5},{2,6},{3,7},{4,0},{5,1},{6,2},{7,3},{8,12},{9,13},{10,... | collective-permute-start | bytes 3538952 | tf_op jit(solution)/shard_map/ppermute | solution.py:130
  1.3 1.3 %copy-start = (bf16[1,768,768]{2,1,0:T(8,128)(2,1)S(1)}, bf16[1,768,768]{2,1,0:T(8,128)(2,1)}, u32[]{:S(2)}) copy-start(bf16[1,768,768]{2,1,0:T(8,128)(2,1)} %param.5) | copy-start | bytes 3538948
  2.6 1.0 %copy-start.3 = (bf16[2,768,128]{2,1,0:T(8,128)(2,1)S(1)}, bf16[2,768,128]{2,1,0:T(8,128)(2,1)}, u32[]{:S(2)}) copy-start(bf16[2,768,128]{2,1,0:T(8,128)(2,1)} %refs_2_.1) | copy-start | bytes 1179652
  3.6 0.9 %copy-start.4 = (bf16[1,768,128]{2,1,0:T(8,128)(2,1)S(1)}, bf16[1,768,128]{2,1,0:T(8,128)(2,1)}, u32[]{:S(2)}) copy-start(bf16[1,768,128]{2,1,0:T(8,128)(2,1)} %param.7) | copy-start | bytes 589828
  4.5 20.3 %copy-start.2 = (bf16[768,768]{1,0:T(8,128)(2,1)S(1)}, bf16[768,768]{1,0:T(8,128)(2,1)}, u32[]{:S(2)}) copy-start(bf16[768,768]{1,0:T(8,128)(2,1)} %refs_4_.3) | copy-start | bytes 3538948
  5.6 5.1 %collective-permute-start = (bf16[32,768]{1,0:T(8,128)(2,1)S(1)}, bf16[32,768]{1,0:T(8,128)(2,1)S(1)}, u32[]{:S(2)}, u32[]{:S(2)}) collective-permute-start(bf16[32,768]{1,0:T(8,128)(2,1)S(1)} %get-tuple-element.13), channel_id=1, source_target_pairs={{0,16},{1,17},{2,18},{3,19},{4,20},{5,21},{6,22},{7,23},{8,24},{9,... | collective-permute-start | bytes 147464 | tf_op jit(solution)/shard_map/ppermute | solution.py:130
  8.7 2.1 %collective-permute-start.1 = (bf16[32,768]{1,0:T(8,128)(2,1)S(1)}, bf16[32,768]{1,0:T(8,128)(2,1)S(1)}, u32[]{:S(2)}, u32[]{:S(2)}) collective-permute-start(bf16[32,768]{1,0:T(8,128)(2,1)S(1)} %get-tuple-element.14), channel_id=1, source_target_pairs={{0,4},{1,5},{2,6},{3,7},{4,0},{5,1},{6,2},{7,3},{8,12},{9,13},{10,... | collective-permute-start | bytes 147464 | tf_op jit(solution)/shard_map/ppermute | solution.py:130
  8.7 3.5 %collective-permute-start.2 = (bf16[32,768]{1,0:T(8,128)(2,1)S(1)}, bf16[32,768]{1,0:T(8,128)(2,1)S(1)}, u32[]{:S(2)}, u32[]{:S(2)}) collective-permute-start(bf16[32,768]{1,0:T(8,128)(2,1)S(1)} %get-tuple-element.15), channel_id=1, source_target_pairs={{0,20},{1,21},{2,22},{3,23},{4,16},{5,17},{6,18},{7,19},{8,28},{9,... | collective-permute-start | bytes 147464 | tf_op jit(solution)/shard_map/ppermute | solution.py:130
  12.2 7.5 %collective-permute-start.5 = (bf16[64,768]{1,0:T(8,128)(2,1)S(1)}, bf16[64,768]{1,0:T(8,128)(2,1)S(1)}, u32[]{:S(2)}, u32[]{:S(2)}) collective-permute-start(bf16[64,768]{1,0:T(8,128)(2,1)S(1)} %shard_map.60.refs_0_), channel_id=1, source_target_pairs={{0,3},{1,2},{2,1},{3,0},{4,7},{5,6},{6,5},{7,4},{8,11},{9,10},{10,... | collective-permute-start | bytes 294920 | tf_op jit(solution)/shard_map/ppermute | solution.py:130
  15.9 8.9 %collective-permute-start.4 = (bf16[64,768]{1,0:T(8,128)(2,1)S(1)}, bf16[64,768]{1,0:T(8,128)(2,1)S(1)}, u32[]{:S(2)}, u32[]{:S(2)}) collective-permute-start(bf16[64,768]{1,0:T(8,128)(2,1)S(1)} %shard_map.60.refs_0_), channel_id=1, source_target_pairs={{0,2},{1,3},{2,0},{3,1},{4,6},{5,7},{6,4},{7,5},{8,10},{9,11},{10,... | collective-permute-start | bytes 294920 | tf_op jit(solution)/shard_map/ppermute | solution.py:130
  15.9 8.9 %collective-permute-start.3 = (bf16[64,768]{1,0:T(8,128)(2,1)S(1)}, bf16[64,768]{1,0:T(8,128)(2,1)S(1)}, u32[]{:S(2)}, u32[]{:S(2)}) collective-permute-start(bf16[64,768]{1,0:T(8,128)(2,1)S(1)} %shard_map.60.refs_0_), channel_id=1, source_target_pairs={{0,1},{1,0},{2,3},{3,2},{4,5},{5,4},{6,7},{7,6},{8,9},{9,8},{10,11... | collective-permute-start | bytes 294920 | tf_op jit(solution)/shard_map/ppermute | solution.py:130
  19.8 9.4 %collective-permute-start.10 = (bf16[64,768]{1,0:T(8,128)(2,1)S(1)}, bf16[64,768]{1,0:T(8,128)(2,1)S(1)}, u32[]{:S(2)}, u32[]{:S(2)}) collective-permute-start(bf16[64,768]{1,0:T(8,128)(2,1)S(1)} %get-tuple-element.16), channel_id=1, source_target_pairs={{0,16},{1,17},{2,18},{3,19},{4,20},{5,21},{6,22},{7,23},{8,24},{9,... | collective-permute-start | bytes 294920 | tf_op jit(solution)/shard_map/ppermute | solution.py:65
  24.8 7.9 %copy-start.1 = (bf16[1,768,768]{2,1,0:T(8,128)(2,1)S(1)}, bf16[1,768,768]{2,1,0:T(8,128)(2,1)}, u32[]{:S(2)}) copy-start(bf16[1,768,768]{2,1,0:T(8,128)(2,1)} %param.5) | copy-start | bytes 3538948
  25.6 5.3 %collective-permute-start.9 = (bf16[32,768]{1,0:T(8,128)(2,1)S(1)}, bf16[32,768]{1,0:T(8,128)(2,1)S(1)}, u32[]{:S(2)}, u32[]{:S(2)}) collective-permute-start(bf16[32,768]{1,0:T(8,128)(2,1)S(1)} %shard_map.61.refs_0_), channel_id=1, source_target_pairs={{0,24},{1,25},{2,26},{3,27},{4,28},{5,29},{6,30},{7,31},{8,16},{9,... | collective-permute-start | bytes 147464 | tf_op jit(solution)/shard_map/ppermute | solution.py:130
  27.5 4.1 %collective-permute-start.8 = (bf16[32,768]{1,0:T(8,128)(2,1)S(1)}, bf16[32,768]{1,0:T(8,128)(2,1)S(1)}, u32[]{:S(2)}, u32[]{:S(2)}) collective-permute-start(bf16[32,768]{1,0:T(8,128)(2,1)S(1)} %shard_map.61.refs_0_), channel_id=1, source_target_pairs={{0,16},{1,17},{2,18},{3,19},{4,20},{5,21},{6,22},{7,23},{8,24},{9,... | collective-permute-start | bytes 147464 | tf_op jit(solution)/shard_map/ppermute | solution.py:130
  28.6 4.1 %collective-permute-start.7 = (bf16[32,768]{1,0:T(8,128)(2,1)S(1)}, bf16[32,768]{1,0:T(8,128)(2,1)S(1)}, u32[]{:S(2)}, u32[]{:S(2)}) collective-permute-start(bf16[32,768]{1,0:T(8,128)(2,1)S(1)} %shard_map.61.refs_0_), channel_id=1, source_target_pairs={{0,8},{1,9},{2,10},{3,11},{4,12},{5,13},{6,14},{7,15},{8,0},{9,1},... | collective-permute-start | bytes 147464 | tf_op jit(solution)/shard_map/ppermute | solution.py:130
  33.6 4.7 %collective-permute-start.13 = (bf16[64,768]{1,0:T(8,128)(2,1)S(1)}, bf16[64,768]{1,0:T(8,128)(2,1)S(1)}, u32[]{:S(2)}, u32[]{:S(2)}) collective-permute-start(bf16[64,768]{1,0:T(8,128)(2,1)S(1)} %get-tuple-element.19), channel_id=1, source_target_pairs={{0,16},{1,17},{2,18},{3,19},{4,20},{5,21},{6,22},{7,23},{8,24},{9,... | collective-permute-start | bytes 294920 | tf_op jit(solution)/shard_map/ppermute | solution.py:130
  34.5 1.2 %collective-permute-start.14 = (bf16[32,768]{1,0:T(8,128)(2,1)S(1)}, bf16[32,768]{1,0:T(8,128)(2,1)S(1)}, u32[]{:S(2)}, u32[]{:S(2)}) collective-permute-start(bf16[32,768]{1,0:T(8,128)(2,1)S(1)} %get-tuple-element.21), channel_id=1, source_target_pairs={{0,4},{1,5},{2,6},{3,7},{4,0},{5,1},{6,2},{7,3},{8,12},{9,13},{10,... | collective-permute-start | bytes 147464 | tf_op jit(solution)/shard_map/ppermute | solution.py:130
  38.3 6.7 %collective-permute-start.17 = (bf16[64,768]{1,0:T(8,128)(2,1)S(1)}, bf16[64,768]{1,0:T(8,128)(2,1)S(1)}, u32[]{:S(2)}, u32[]{:S(2)}) collective-permute-start(bf16[64,768]{1,0:T(8,128)(2,1)S(1)} %shard_map.63.refs_0_), channel_id=1, source_target_pairs={{0,3},{1,2},{2,1},{3,0},{4,7},{5,6},{6,5},{7,4},{8,11},{9,10},{10,... | collective-permute-start | bytes 294920 | tf_op jit(solution)/shard_map/ppermute | solution.py:130
  40.9 7.2 %collective-permute-start.16 = (bf16[64,768]{1,0:T(8,128)(2,1)S(1)}, bf16[64,768]{1,0:T(8,128)(2,1)S(1)}, u32[]{:S(2)}, u32[]{:S(2)}) collective-permute-start(bf16[64,768]{1,0:T(8,128)(2,1)S(1)} %shard_map.63.refs_0_), channel_id=1, source_target_pairs={{0,2},{1,3},{2,0},{3,1},{4,6},{5,7},{6,4},{7,5},{8,10},{9,11},{10,... | collective-permute-start | bytes 294920 | tf_op jit(solution)/shard_map/ppermute | solution.py:130
  41.7 6.3 %collective-permute-start.15 = (bf16[64,768]{1,0:T(8,128)(2,1)S(1)}, bf16[64,768]{1,0:T(8,128)(2,1)S(1)}, u32[]{:S(2)}, u32[]{:S(2)}) collective-permute-start(bf16[64,768]{1,0:T(8,128)(2,1)S(1)} %shard_map.63.refs_0_), channel_id=1, source_target_pairs={{0,1},{1,0},{2,3},{3,2},{4,5},{5,4},{6,7},{7,6},{8,9},{9,8},{10,11... | collective-permute-start | bytes 294920 | tf_op jit(solution)/shard_map/ppermute | solution.py:130
  48.8 5.0 %collective-permute-start.20 = (bf16[32,768]{1,0:T(8,128)(2,1)S(1)}, bf16[32,768]{1,0:T(8,128)(2,1)S(1)}, u32[]{:S(2)}, u32[]{:S(2)}) collective-permute-start(bf16[32,768]{1,0:T(8,128)(2,1)S(1)} %shard_map.64.refs_0_), channel_id=1, source_target_pairs={{0,24},{1,25},{2,26},{3,27},{4,28},{5,29},{6,30},{7,31},{8,16},{9,... | collective-permute-start | bytes 147464 | tf_op jit(solution)/shard_map/ppermute | solution.py:130
  50.3 4.1 %collective-permute-start.19 = (bf16[32,768]{1,0:T(8,128)(2,1)S(1)}, bf16[32,768]{1,0:T(8,128)(2,1)S(1)}, u32[]{:S(2)}, u32[]{:S(2)}) collective-permute-start(bf16[32,768]{1,0:T(8,128)(2,1)S(1)} %shard_map.64.refs_0_), channel_id=1, source_target_pairs={{0,16},{1,17},{2,18},{3,19},{4,20},{5,21},{6,22},{7,23},{8,24},{9,... | collective-permute-start | bytes 147464 | tf_op jit(solution)/shard_map/ppermute | solution.py:130
  50.8 4.1 %collective-permute-start.18 = (bf16[32,768]{1,0:T(8,128)(2,1)S(1)}, bf16[32,768]{1,0:T(8,128)(2,1)S(1)}, u32[]{:S(2)}, u32[]{:S(2)}) collective-permute-start(bf16[32,768]{1,0:T(8,128)(2,1)S(1)} %shard_map.64.refs_0_), channel_id=1, source_target_pairs={{0,8},{1,9},{2,10},{3,11},{4,12},{5,13},{6,14},{7,15},{8,0},{9,1},... | collective-permute-start | bytes 147464 | tf_op jit(solution)/shard_map/ppermute | solution.py:130
  52.3 2.8 %collective-permute-start.12 = (bf16[64,768]{1,0:T(8,128)(2,1)S(1)}, bf16[64,768]{1,0:T(8,128)(2,1)S(1)}, u32[]{:S(2)}, u32[]{:S(2)}) collective-permute-start(bf16[64,768]{1,0:T(8,128)(2,1)S(1)} %get-tuple-element.17.refs_0_), channel_id=1, source_target_pairs={{0,4},{1,5},{2,6},{3,7},{4,0},{5,1},{6,2},{7,3},{8,12},{9,13},{10,... | collective-permute-start | bytes 294920 | tf_op jit(solution)/shard_map/ppermute | solution.py:130
  55.0 1.4 %collective-permute-start.21 = (bf16[64,768]{1,0:T(8,128)(2,1)S(1)}, bf16[64,768]{1,0:T(8,128)(2,1)S(1)}, u32[]{:S(2)}, u32[]{:S(2)}) collective-permute-start(bf16[64,768]{1,0:T(8,128)(2,1)S(1)} %shard_map.65.refs_2_), channel_id=1, source_target_pairs={{0,4},{1,5},{2,6},{3,7},{4,0},{5,1},{6,2},{7,3},{8,12},{9,13},{10,... | collective-permute-start | bytes 294920 | tf_op jit(solution)/shard_map/ppermute | solution.py:130

commit v3 on v2

--- a/solution.py
+++ b/solution.py
@@ -133,16 +133,21 @@
         return [(self.n ^ kn) * self.nd + (self.d ^ kd) for kn in range(self.near) for kd in range(self.nd)]
 
 
+def turned_about(body, loose, count, info, *refs):
+    inputs = refs[loose : loose + count][::-1]
+    body(loose, info, *refs[:loose], *inputs, *refs[loose + count :])
+
+
 def kernel_call(body, out_shape, info, inputs, loose=(), scratch=()):
     vmem = pl.BlockSpec(memory_space=pltpu.VMEM)
     return pl.pallas_call(
-        functools.partial(body, len(loose)),
+        functools.partial(turned_about, body, len(loose), len(inputs)),
         out_shape=out_shape,
         in_specs=[pl.BlockSpec(memory_space=pltpu.SMEM)] + [pl.BlockSpec(memory_space=pl.ANY)] * len(loose) + [vmem] * len(inputs),
         out_specs=jax.tree.map(lambda _: vmem, out_shape),
         scratch_shapes=list(scratch),
-        compiler_params=pltpu.CompilerParams(vmem_limit_bytes=24 << 20),
-    )(jnp.stack(info), *loose, *inputs)
+        compiler_params=pltpu.CompilerParams(vmem_limit_bytes=8 << 20),
+    )(jnp.stack(info), *loose, *inputs[::-1])
 
 
 def total_of(refs):
@@ -153,71 +158,74 @@
     return ref[pl.ds(pl.multiple_of(index * rows, rows), rows), :]
 
 
-def begin_body(near, nd, loose, info, *refs):
-    past_ref, operator_ref, incident_ref = refs[:3]
-    count = near * nd
-    pieces, (part_ref, *waves), (total, turned, first, later) = refs[3 : 3 + count], refs[3 + count : -4], refs[-4:]
+def begin_body(loose, info, total_ref, *pieces):
+    for k, piece in enumerate(pieces):
+        piece[...] = part_of(total_ref, info[k], piece.shape[0])
+
+
+def begin(lay, past, operator):
+    total = lax.dot_general(past, operator, (((0,), (1,)), ((), ())), preferred_element_type=F32).astype(BF16)
+    owners = lay.owners()
+    out = [jax.ShapeDtypeStruct((total.shape[0] // len(owners), total.shape[1]), BF16)] * len(owners)
+    return kernel_call(begin_body, out, owners, (total,))
+
+
+def part_body(loose, info, *refs):
+    past_ref, part_ref, turned = refs[loose:]
     turned[...] = past_ref[...].astype(F32).T
-    total[...] = times_transposed(turned[...].astype(BF16), operator_ref[...])
-    first[...] = incident_ref[0].astype(F32).T * info[0].astype(F32)
-    rows = pieces[0].shape[0]
-    for kn in range(near):
-        for kd in range(nd):
-            k = kn * nd + kd
-            value = part_of(total, info[2 + k], rows)
-            if kd == 0:
-                value = value - part_of(first, info[2 + k], rows)
-            pieces[k][...] = value.astype(BF16)
-    later[...] = incident_ref[1].astype(F32).T
-    for kn in range(near):
-        waves[kn][...] = part_of(later, info[2 + kn * nd], rows).astype(BF16)
-    part_ref[...] = part_of(turned, info[1], part_ref.shape[0]).astype(BF16)
-
-
-def begin(lay, past, operator, incident):
+    part_ref[...] = part_of(turned, info[0], part_ref.shape[0]).astype(BF16)
+
+
+def part_cut(lay, past, after):
     columns, exc = past.shape
-    rows = operator.shape[0]
-    owners = lay.owners()
-    share = exc // len(owners)
-    info = [(lay.z == 0).astype(jnp.int32), lay.n, *owners]
-    out = [jax.ShapeDtypeStruct((share, rows), BF16)] * len(owners)
-    out += [jax.ShapeDtypeStruct((share * lay.nd, columns), BF16)]
-    out += [jax.ShapeDtypeStruct((share, rows), BF16)] * lay.near
-    scratch = [pltpu.VMEM((exc, rows), F32), pltpu.VMEM((exc, columns), F32)] + [pltpu.VMEM((exc, rows), F32)] * 2
-    got = kernel_call(functools.partial(begin_body, lay.near, lay.nd), out, info, (past, operator, incident), (), scratch)
-    return got[: len(owners)], got[len(owners)], got[len(owners) + 1 :]
-
-
-def join_body(near, waves, loose, info, *refs):
-    ins, taken, out = refs[loose : len(refs) - 1 - waves], refs[len(refs) - 1 - waves : -1], refs[-1]
+    out = jax.ShapeDtypeStruct((exc // lay.near, columns), BF16)
+    return kernel_call(part_body, out, [lay.n], (past,), after, [pltpu.VMEM((exc, columns), F32)])
+
+
+def wave_body(step, loose, info, *refs):
+    incident_ref, outs, turned = refs[loose], refs[loose + 1 : -1], refs[-1]
+    turned[...] = incident_ref[step].astype(F32).T
+    for kn, out in enumerate(outs):
+        out[...] = part_of(turned, info[kn], out.shape[0]).astype(BF16)
+
+
+def wave_cut(lay, incident, step, after):
+    rows, exc = incident.shape[1:]
+    owners = lay.owners()[:: lay.nd]
+    out = [jax.ShapeDtypeStruct((exc // (lay.near * lay.nd), rows), BF16)] * lay.near
+    body = functools.partial(wave_body, step)
+    return kernel_call(body, out, owners, (incident,), after, [pltpu.VMEM((exc, rows), F32)])
+
+
+def join_body(near, loose, info, *refs):
+    ins, out = refs[loose:-1], refs[-1]
     per, rows = len(ins) // near, ins[0].shape[0]
     for kn in range(near):
-        value = total_of(ins[kn * per : (kn + 1) * per])
-        if waves:
-            value = value - info[0].astype(F32) * jnp.concatenate([wave[...].astype(F32) for wave in taken], 0)
-        out[pl.ds(kn * rows, rows), :] = value.astype(BF16)
-
-
-def join(lay, groups, loose=(), waves=()):
+        out[pl.ds(kn * rows, rows), :] = total_of(ins[kn * per : (kn + 1) * per]).astype(BF16)
+
+
+def join(lay, groups, loose=()):
     rows, columns = groups[0][0].shape
     out = jax.ShapeDtypeStruct((rows * len(groups), columns), BF16)
-    body = functools.partial(join_body, len(groups), len(waves))
-    info = [(lay.z == 0).astype(jnp.int32)]
-    return kernel_call(body, out, info, [b for g in groups for b in g] + list(waves), loose)
+    return kernel_call(functools.partial(join_body, len(groups)), out, [lay.d], [b for g in groups for b in g], loose)
 
 
 def invert_body(near, loose, info, *refs):
-    parts, operators, out = refs[loose : -1 - near], refs[-1 - near : -1], refs[-1]
-    rhs = (-total_of(parts)).astype(BF16)
-    rows = rhs.shape[0] // near
-    out[...] = tree_sum(
-        [times_transposed(rhs[k * rows : (k + 1) * rows], op[...]) for k, op in enumerate(operators)]
-    ).astype(BF16)
-
-
-def invert(lay, parts, operators, loose=()):
+    refs, out = refs[loose:-1], refs[-1]
+    parts, waves, operators = refs[: -2 * near], refs[-2 * near : -near], refs[-near:]
+    retarded = total_of(parts)
+    rows = retarded.shape[0] // near
+    terms = []
+    for kn in range(near):
+        rhs = (waves[kn][...].astype(F32) - retarded[kn * rows : (kn + 1) * rows]).astype(BF16)
+        terms.append(times_transposed(rhs, operators[kn][...]))
+    out[...] = tree_sum(terms).astype(BF16)
+
+
+def invert(lay, parts, waves, operators, loose=()):
     out = jax.ShapeDtypeStruct((parts[0].shape[0] // lay.near, operators[0].shape[0]), BF16)
-    return kernel_call(functools.partial(invert_body, lay.near), out, [lay.d], (*parts, *operators), loose)
+    body = functools.partial(invert_body, lay.near)
+    return kernel_call(body, out, [lay.d], (*parts, *waves, *operators), loose)
 
 
 def apply_body(near, nd, loose, info, *refs):
@@ -254,32 +262,60 @@
     return current, totals
 
 
-def finish_body(steps, loose, info, *refs):
-    ins, (out, hist, total) = refs[loose:-3], refs[-3:]
-    per = len(ins) // steps
+def place(info, blocks, total):
     pieces = info.shape[0] - 1
     rows = total.shape[0] // pieces
-    each = ins[0].shape[0] // rows
-    for step in range(steps):
-        for k in range(pieces):
-            start = pl.multiple_of(info[1 + k] * rows, rows)
-            block = ins[step * per + k // each][pl.ds((k % each) * rows, rows), :]
-            total[pl.ds(start, rows), :] = block.astype(F32)
-        turned = total[...].T.astype(BF16)
-        out[step] = turned
-
-        @pl.when(info[0] == steps - 1 - step)
+    each = blocks[0].shape[0] // rows
+    for k in range(pieces):
+        start = pl.multiple_of(info[1 + k] * rows, rows)
+        total[pl.ds(start, rows), :] = blocks[k // each][pl.ds((k % each) * rows, rows), :].astype(F32)
+    return total[...].T.astype(BF16)
+
+
+def turn_body(loose, info, *refs):
+    refs[-2][...] = place(info, refs[loose:-2], refs[-1])
+
+
+def turn(lay, blocks):
+    columns, exc = blocks[0].shape[1], blocks[0].shape[0] * lay.near
+    out = jax.ShapeDtypeStruct((columns, exc), BF16)
+    return kernel_call(turn_body, out, [lay.d, *lay.owners()], blocks, (), [pltpu.VMEM((exc, columns), F32)])
+
+
+def finish_body(done, info, *refs):
+    earlier, blocks, (out, hist, total, turned, sems) = refs[:done], refs[done:-5], refs[-5:]
+
+    def store(step, source):
+        kept = pltpu.make_async_copy(source, hist.at[0], sems.at[done + 1])
+
+        @pl.when(info[0] == done - step)
         def _():
-            hist[0] = turned
-
-
-def finish(lay, blocks):
-    steps = len(blocks)
-    columns, exc = blocks[0][0].shape[1], blocks[0][0].shape[0] * lay.near
-    shapes = [jax.ShapeDtypeStruct((k, columns, exc), BF16) for k in (steps, 1)]
-    flat = [b for g in blocks for b in g]
-    info = [lay.d, *lay.owners()]
-    return kernel_call(functools.partial(finish_body, steps), shapes, info, flat, (), [pltpu.VMEM((exc, columns), F32)])
+            kept.start()
+
+        copy = pltpu.make_async_copy(source, out.at[step], sems.at[step])
+        copy.start()
+        return copy, kept
+
+    copies = [store(step, source) for step, source in enumerate(earlier)]
+    turned[...] = place(info, blocks, total)
+    copies.append(store(done, turned))
+    for copy, _ in copies:
+        copy.wait()
+    copies[-1][1].wait()
+
+
+def finish(lay, earlier, blocks):
+    done = len(earlier)
+    columns, exc = earlier[0].shape
+    hbm, vmem = pl.BlockSpec(memory_space=pltpu.HBM), pl.BlockSpec(memory_space=pltpu.VMEM)
+    return pl.pallas_call(
+        functools.partial(finish_body, done),
+        out_shape=[jax.ShapeDtypeStruct((k, columns, exc), BF16) for k in (done + 1, 1)],
+        in_specs=[pl.BlockSpec(memory_space=pltpu.SMEM)] + [vmem] * (done + len(blocks)),
+        out_specs=[hbm] * 2,
+        scratch_shapes=[pltpu.VMEM((exc, columns), F32), pltpu.VMEM((columns, exc), BF16), pltpu.SemaphoreType.DMA((done + 2,))],
+        compiler_params=pltpu.CompilerParams(vmem_limit_bytes=8 << 20),
+    )(jnp.stack([lay.d, *lay.owners()]), *earlier, *blocks)
 
 
 def over_rows(lay, partial):
@@ -297,26 +333,33 @@
     return [total] + [got[kz] for kz in range(1, lay.nc)]
 
 
+def from_cores(lay, pieces):
+    return [lay.move(piece, kn=kn) if kn else piece for kn, piece in enumerate(pieces)]
+
+
 def two_steps(excitation, delay_ops, inverse_op, history):
     lay = Layout()
     operator, stored = delay_ops[0], history[0]
-    pieces, part, waves = begin(lay, stored, operator, excitation)
+    pieces = begin(lay, stored, operator)
+    part = part_cut(lay, stored, (pieces[0],))
     got = [
         [lay.move(pieces[kn * lay.nd + kd], kd=kd, kn=kn) if kd or kn else pieces[0] for kd in range(lay.nd)]
         for kn in range(lay.near)
     ]
+    cuts = wave_cut(lay, excitation, 0, (pieces[0],))
     inverse = over_near(lay, inverse_op)
-    total = join(lay, got)
+    total = join(lay, got, (*cuts, part))
     past = from_behind(part, "delay", 1)
-    waves = [lay.move(wave, kn=kn) if kn else wave for kn, wave in enumerate(waves)]
     direct = over_near(lay, operator)
-    partial = invert(lay, along_col(lay, total), inverse, ())
+    partial = invert(lay, along_col(lay, total), from_cores(lay, cuts), inverse)
     current, totals = apply(lay, over_rows(lay, partial), past, direct)
-    total = join(lay, [[lay.move(block, kd=kd) if kd else block for kd, block in enumerate(totals)]], (), waves)
-    partial = invert(lay, along_col(lay, total), inverse)
+    cuts = wave_cut(lay, excitation, 1, (totals[0],))
+    total = join(lay, [[lay.move(block, kd=kd) if kd else block for kd, block in enumerate(totals)]], cuts)
+    turned = turn(lay, over_near(lay, current))
+    partial = invert(lay, along_col(lay, total), from_cores(lay, cuts), inverse, ())
     across = over_rows(lay, partial)
     last = join(lay, [across[kd * lay.far : (kd + 1) * lay.far] for kd in range(lay.nd)])
-    return tuple(finish(lay, [over_near(lay, current), over_near(lay, last)]))
+    return tuple(finish(lay, [turned], over_near(lay, last)))
 
 
 def on_device(excitation, delay_ops, inverse_op, history):
@@ -324,7 +367,7 @@
     steps, _, exc = excitation.shape
     follows = range(1, steps)
     share = exc // (sizes[0] * 2)
-    if all(n & (n - 1) == 0 and n > 1 for n in sizes) and len(follows) == 1 and share and share % TILE_ROWS == 0:
+    if all(n & (n - 1) == 0 and n > 1 for n in sizes) and len(follows) == 1 and sizes[0] <= steps and share and share % TILE_ROWS == 0:
         return two_steps(excitation, delay_ops, inverse_op, history)
     return general(excitation, delay_ops, inverse_op, history)
 

time: 58.2 us -> 55.2 us (0.948)
  waiting for transfers between devices: 24.9 us -> 19.9 us
  local copies, waits for them, and re-layouts: 3.37 us -> 0.11 us
  matrix products: 0 us -> 1.99 us
  starting transfers between devices: 23.6 us -> 25.4 us
  Pallas kernels: 5.36 us -> 6.76 us
    ppermute x21 -> x22, waiting for transfers between devices: 24.9 us -> 19.9 us  [move(): return lax.ppermute(block, ('delay', 'row', 'col'), pairs)]
    unnamed x10 -> x8, local copies, waits for them, and re-layouts: 3.2 us -> 0.02 us
    dot_general x0 -> x1, matrix products: none -> 1.99 us  [begin(): lax.dot_general(past, operator, (((0,), (1,)), ((), ())), preferred_eleme...]
    ppermute x21 -> x22, starting transfers between devices: 20.8 us -> 22.2 us  [move(): return lax.ppermute(block, ('delay', 'row', 'col'), pairs)]
    pallas_call x8 -> x12, Pallas kernels: 5.36 us -> 6.76 us  [the longest x11 5.28 us: kernel_call(): pl.pallas_call(functools.partial(turned_about, body, len(loose), len(inpu...]
  transfers between devices with their start and end apart: 22 -> 23, of which waited for: 15 -> 16; matrix products, arithmetic and copies ran while one was open for 0% -> 4% of each run, Pallas kernels for 3% -> 7%
where the time goes in v3:
time: 55.2 us; the launch traced here: 55 us
  starting transfers between devices  25.4 us (46%)
  waiting for transfers between devices  19.9 us (36%)
  Pallas kernels  6.76 us (12%)
  matrix products  1.99 us (4%)
  between operations  0.76 us (1%)
    ppermute x22, starting transfers between devices, move(): return lax.ppermute(block, ('delay', 'row', 'col'), pairs)  22.2 us
    ppermute x22, waiting for transfers between devices, move(): return lax.ppermute(block, ('delay', 'row', 'col'), pairs)  19.9 us
    pallas_call x11, Pallas kernels, kernel_call(): pl.pallas_call(functools.partial(turned_about, body, len(loose), len(inpu...  5.28 us
    ppermute x1, starting transfers between devices, from_behind(): return lax.ppermute(block, axis, route) if route else jnp.zeros_like(block)  3.18 us
    dot_general x1, matrix products, begin(): lax.dot_general(past, operator, (((0,), (1,)), ((), ())), preferred_eleme...  1.99 us
    pallas_call x1, Pallas kernels, finish(): pl.pallas_call(functools.partial(finish_body, done), out_shape=[jax.Shape...  1.48 us
  transfers between devices with their start and end apart: 23, of which 16 were waited for; matrix products, arithmetic and copies ran while one was open for 4% of the time, Pallas kernels for 7%

profile of v3, /device:TPU:0, one launch (start us, length us, event | category | flops | bytes accessed | tf_op | source)
XLA Modules:
  0.0 55.0 jit_solution(716691926646932881)
XLA Ops:
  0.7 0.5 collective-permute-start.2
  1.2 0.1 collective-permute-start
  1.2 0.1 pad_add_fusion.info
  1.3 2.0 %convolution_convert_fusion.refs_0_ = bf16[128,768]{1,0:T(8,128)(2,1)S(1)} fusion(bf16[1,768,128]{2,1,0:T(8,128)(2,1)} %param.7, bf16[1,768,768]{2,1,0:T(8,128)(2,1)} %param.5), kind=kOutput, calls=%fused_computation | convolution fusion | flops 151093248 | bytes 1572864 | tf_op jit(solution)/shard_map/dot_general | solution.py:167
  3.3 0.6 %shard_map.59 = (bf16[32,768]{1,0:T(8,128)(2,1)S(1)}, bf16[32,768]{1,0:T(8,128)(2,1)S(1)}, bf16[32,768]{1,0:T(8,128)(2,1)S(1)}, bf16[32,768]{1,0:T(8,128)(2,1)S(1)}) custom-call(s32[4]{0:T(128)S(1)} %pad_add_fusion.info, bf16[128,768]{1,0:T(8,128)(2,1)S(1)} %convolution_convert_fusion.refs_0_), custom_call_target="tpu_custom_call" | custom-call | tf_op jit(solution)/shard_map/pallas_call | solution.py:143
  3.9 2.7 %collective-permute-start.4 = (bf16[32,768]{1,0:T(8,128)(2,1)S(1)}, bf16[32,768]{1,0:T(8,128)(2,1)S(1)}, u32[]{:S(2)}, u32[]{:S(2)}) collective-permute-start(bf16[32,768]{1,0:T(8,128)(2,1)S(1)} %get-tuple-element.16), channel_id=1, source_target_pairs={{0,20},{1,21},{2,22},{3,23},{4,16},{5,17},{6,18},{7,19},{8,28},{9,... | collective-permute-start | bytes 147464 | tf_op jit(solution)/shard_map/ppermute | solution.py:130
  6.6 0.4 collective-permute-start.5
  7.1 0.1 pad_add_fusion.1.info
  7.1 0.7 %shard_map.61 = (bf16[32,768]{1,0:T(8,128)(2,1)S(1)}, bf16[32,768]{1,0:T(8,128)(2,1)S(1)}) custom-call(s32[2]{0:T(128)S(1)} %pad_add_fusion.1.info, bf16[32,768]{1,0:T(8,128)(2,1)S(1)} %get-tuple-element.13.refs_0_.refs_6_, bf16[2,768,128]{2,1,0:T(8,128)(2,1)S(1)} %copy-done.2), custom_call_target="tpu_custom_call" | custom-call | tf_op jit(solution)/shard_map/pallas_call | solution.py:143
  7.8 0.1 shard_map.60.refs_2_
  8.0 0.7 %collective-permute-done.4.refs_3_ = bf16[32,768]{1,0:T(8,128)(2,1)S(1)} collective-permute-done((bf16[32,768]{1,0:T(8,128)(2,1)S(1)}, bf16[32,768]{1,0:T(8,128)(2,1)S(1)}, u32[]{:S(2)}, u32[]{:S(2)}) %collective-permute-start.4) | collective-permute-done | bytes 49184 | tf_op jit(solution)/shard_map/ppermute | solution.py:130
  8.7 0.1 collective-permute-start.3
  8.8 2.3 %collective-permute-done.6.refs_5_ = bf16[32,768]{1,0:T(8,128)(2,1)S(1)} collective-permute-done((bf16[32,768]{1,0:T(8,128)(2,1)S(1)}, bf16[32,768]{1,0:T(8,128)(2,1)S(1)}, u32[]{:S(2)}, u32[]{:S(2)}) %collective-permute-start.6) | collective-permute-done | bytes 49184 | tf_op jit(solution)/shard_map/ppermute | solution.py:130
  11.1 3.7 %collective-permute-start.7 = (bf16[64,768]{1,0:T(8,128)(2,1)S(1)}, bf16[64,768]{1,0:T(8,128)(2,1)S(1)}, u32[]{:S(2)}, u32[]{:S(2)}) collective-permute-start(bf16[64,768]{1,0:T(8,128)(2,1)S(1)} %shard_map.62.refs_7_), channel_id=1, source_target_pairs={{0,3},{1,2},{2,1},{3,0},{4,7},{5,6},{6,5},{7,4},{8,11},{9,10},{10,... | collective-permute-start | bytes 294920 | tf_op jit(solution)/shard_map/ppermute | solution.py:130
  14.8 0.8 %collective-permute-start.9 = (bf16[64,768]{1,0:T(8,128)(2,1)S(1)}, bf16[64,768]{1,0:T(8,128)(2,1)S(1)}, u32[]{:S(2)}, u32[]{:S(2)}) collective-permute-start(bf16[64,768]{1,0:T(8,128)(2,1)S(1)} %shard_map.62.refs_7_), channel_id=1, source_target_pairs={{0,1},{1,0},{2,3},{3,2},{4,5},{5,4},{6,7},{7,6},{8,9},{9,8},{10,11... | collective-permute-start | bytes 294920 | tf_op jit(solution)/shard_map/ppermute | solution.py:130
  15.6 2.6 %collective-permute-done.7.refs_4_ = bf16[64,768]{1,0:T(8,128)(2,1)S(1)} collective-permute-done((bf16[64,768]{1,0:T(8,128)(2,1)S(1)}, bf16[64,768]{1,0:T(8,128)(2,1)S(1)}, u32[]{:S(2)}, u32[]{:S(2)}) %collective-permute-start.7) | collective-permute-done | bytes 98336 | tf_op jit(solution)/shard_map/ppermute | solution.py:130
  18.2 3.2 %collective-permute-start.1 = (bf16[64,768]{1,0:T(8,128)(2,1)S(1)}, bf16[64,768]{1,0:T(8,128)(2,1)S(1)}, u32[]{:S(2)}, u32[]{:S(2)}) collective-permute-start(bf16[64,768]{1,0:T(8,128)(2,1)S(1)} %shard_map.60.refs_2_), channel_id=1, source_target_pairs={{0,16},{1,17},{2,18},{3,19},{4,20},{5,21},{6,22},{7,23},{8,24},{9,... | collective-permute-start | bytes 294920 | tf_op jit(solution)/shard_map/ppermute | solution.py:65
  21.3 0.8 %collective-permute-done.8.refs_5_ = bf16[64,768]{1,0:T(8,128)(2,1)S(1)} collective-permute-done((bf16[64,768]{1,0:T(8,128)(2,1)S(1)}, bf16[64,768]{1,0:T(8,128)(2,1)S(1)}, u32[]{:S(2)}, u32[]{:S(2)}) %collective-permute-start.8) | collective-permute-done | bytes 98336 | tf_op jit(solution)/shard_map/ppermute | solution.py:130
  22.2 0.8 %shard_map.63.refs_6_ = bf16[32,768]{1,0:T(8,128)(2,1)S(1)} custom-call(s32[1]{0:T(128)} %bitcast.info, bf16[768,768]{1,0:T(8,128)(2,1)S(1)} %collective-permute-done.2.refs_0_, bf16[768,768]{1,0:T(8,128)(2,1)S(1)} %copy-done.1, bf16[32,768]{1,0:T(8,128)(2,1)S(1)} %collective-permute-done.3.refs_2_, bf16[32,768]{1,0:T(8,128)(2,1)S(1)} %get-tuple-element.15.refs_0_.refs_3_, ...), custom_call_target="tpu_custom_call" | custom-call | tf_op jit(solution)/shard_map/pallas_call | solution.py:143
  23.0 2.8 %collective-permute-start.10 = (bf16[32,768]{1,0:T(8,128)(2,1)S(1)}, bf16[32,768]{1,0:T(8,128)(2,1)S(1)}, u32[]{:S(2)}, u32[]{:S(2)}) collective-permute-start(bf16[32,768]{1,0:T(8,128)(2,1)S(1)} %shard_map.63.refs_6_), channel_id=1, source_target_pairs={{0,24},{1,25},{2,26},{3,27},{4,28},{5,29},{6,30},{7,31},{8,16},{9,... | collective-permute-start | bytes 147464 | tf_op jit(solution)/shard_map/ppermute | solution.py:130
  25.7 0.2 collective-permute-start.11
  26.0 0.5 collective-permute-start.12
  26.5 1.6 %collective-permute-done.10.refs_3_ = bf16[32,768]{1,0:T(8,128)(2,1)S(1)} collective-permute-done((bf16[32,768]{1,0:T(8,128)(2,1)S(1)}, bf16[32,768]{1,0:T(8,128)(2,1)S(1)}, u32[]{:S(2)}, u32[]{:S(2)}) %collective-permute-start.10) | collective-permute-done | bytes 49184 | tf_op jit(solution)/shard_map/ppermute | solution.py:130
  28.1 1.7 %collective-permute-done.11.refs_4_ = bf16[32,768]{1,0:T(8,128)(2,1)S(1)} collective-permute-done((bf16[32,768]{1,0:T(8,128)(2,1)S(1)}, bf16[32,768]{1,0:T(8,128)(2,1)S(1)}, u32[]{:S(2)}, u32[]{:S(2)}) %collective-permute-start.11) | collective-permute-done | bytes 49184 | tf_op jit(solution)/shard_map/ppermute | solution.py:130
  29.8 0.2 collective-permute-done.12.refs_5_
  30.1 0.9 %shard_map.64 = (bf16[64,768]{1,0:T(8,128)(2,1)S(1)}, bf16[64,768]{1,0:T(8,128)(2,1)S(1)}, bf16[64,768]{1,0:T(8,128)(2,1)S(1)}) custom-call(s32[1]{0:T(128)} %bitcast.info, bf16[768,768]{1,0:T(8,128)(2,1)S(1)} %collective-permute-done.refs_0_, bf16[768,768]{1,0:T(8,128)(2,1)S(1)} %bitcast.13, bf16[64,768]{1,0:T(8,128)(2,1)S(1)} %collective-permute-done.1.refs_2_, ...), custom_call_target="tpu_custom_call" | custom-call | tf_op jit(solution)/shard_map/pallas_call | solution.py:143
  30.9 1.9 %collective-permute-start.15 = (bf16[64,768]{1,0:T(8,128)(2,1)S(1)}, bf16[64,768]{1,0:T(8,128)(2,1)S(1)}, u32[]{:S(2)}, u32[]{:S(2)}) collective-permute-start(bf16[64,768]{1,0:T(8,128)(2,1)S(1)} %get-tuple-element.23), channel_id=1, source_target_pairs={{0,16},{1,17},{2,18},{3,19},{4,20},{5,21},{6,22},{7,23},{8,24},{9,... | collective-permute-start | bytes 294920 | tf_op jit(solution)/shard_map/ppermute | solution.py:130
  32.8 0.7 %shard_map.66 = (bf16[32,768]{1,0:T(8,128)(2,1)S(1)}, bf16[32,768]{1,0:T(8,128)(2,1)S(1)}) custom-call(s32[2]{0:T(128)S(1)} %pad_add_fusion.1.info, bf16[64,768]{1,0:T(8,128)(2,1)S(1)} %get-tuple-element.20.refs_0_.refs_3_, bf16[2,768,128]{2,1,0:T(8,128)(2,1)S(1)} %copy-done.2), custom_call_target="tpu_custom_call" | custom-call | tf_op jit(solution)/shard_map/pallas_call | solution.py:143
  33.5 2.1 %collective-permute-done.15.refs_2_ = bf16[64,768]{1,0:T(8,128)(2,1)S(1)} collective-permute-done((bf16[64,768]{1,0:T(8,128)(2,1)S(1)}, bf16[64,768]{1,0:T(8,128)(2,1)S(1)}, u32[]{:S(2)}, u32[]{:S(2)}) %collective-permute-start.15) | collective-permute-done | bytes 98336 | tf_op jit(solution)/shard_map/ppermute | solution.py:130
  35.6 3.0 %collective-permute-start.16 = (bf16[64,768]{1,0:T(8,128)(2,1)S(1)}, bf16[64,768]{1,0:T(8,128)(2,1)S(1)}, u32[]{:S(2)}, u32[]{:S(2)}) collective-permute-start(bf16[64,768]{1,0:T(8,128)(2,1)S(1)} %shard_map.67.refs_7_), channel_id=1, source_target_pairs={{0,3},{1,2},{2,1},{3,0},{4,7},{5,6},{6,5},{7,4},{8,11},{9,10},{10,... | collective-permute-start | bytes 294920 | tf_op jit(solution)/shard_map/ppermute | solution.py:130
  38.7 1.7 %collective-permute-start.17 = (bf16[64,768]{1,0:T(8,128)(2,1)S(1)}, bf16[64,768]{1,0:T(8,128)(2,1)S(1)}, u32[]{:S(2)}, u32[]{:S(2)}) collective-permute-start(bf16[64,768]{1,0:T(8,128)(2,1)S(1)} %shard_map.67.refs_7_), channel_id=1, source_target_pairs={{0,2},{1,3},{2,0},{3,1},{4,6},{5,7},{6,4},{7,5},{8,10},{9,11},{10,... | collective-permute-start | bytes 294920 | tf_op jit(solution)/shard_map/ppermute | solution.py:130
  40.3 0.2 collective-permute-start.18
  40.6 1.2 %collective-permute-done.14.refs_2_ = bf16[32,768]{1,0:T(8,128)(2,1)S(1)} collective-permute-done((bf16[32,768]{1,0:T(8,128)(2,1)S(1)}, bf16[32,768]{1,0:T(8,128)(2,1)S(1)}, u32[]{:S(2)}, u32[]{:S(2)}) %collective-permute-start.14) | collective-permute-done | bytes 49184 | tf_op jit(solution)/shard_map/ppermute | solution.py:130
  41.8 0.3 collective-permute-done.16.refs_4_
  42.1 2.1 %collective-permute-done.17.refs_5_ = bf16[64,768]{1,0:T(8,128)(2,1)S(1)} collective-permute-done((bf16[64,768]{1,0:T(8,128)(2,1)S(1)}, bf16[64,768]{1,0:T(8,128)(2,1)S(1)}, u32[]{:S(2)}, u32[]{:S(2)}) %collective-permute-start.17) | collective-permute-done | bytes 98336 | tf_op jit(solution)/shard_map/ppermute | solution.py:130
  44.3 1.0 %collective-permute-done.18.refs_6_ = bf16[64,768]{1,0:T(8,128)(2,1)S(1)} collective-permute-done((bf16[64,768]{1,0:T(8,128)(2,1)S(1)}, bf16[64,768]{1,0:T(8,128)(2,1)S(1)}, u32[]{:S(2)}, u32[]{:S(2)}) %collective-permute-start.18) | collective-permute-done | bytes 98336 | tf_op jit(solution)/shard_map/ppermute | solution.py:130
  45.3 0.8 %shard_map.68.refs_3_ = bf16[32,768]{1,0:T(8,128)(2,1)S(1)} custom-call(s32[1]{0:T(128)} %bitcast.info, bf16[768,768]{1,0:T(8,128)(2,1)S(1)} %collective-permute-done.2.refs_0_, bf16[768,768]{1,0:T(8,128)(2,1)S(1)} %copy-done.1, bf16[32,768]{1,0:T(8,128)(2,1)S(1)} %collective-permute-done.14.refs_2_, bf16[32,768]{1,0:T(8,128)(2,1)S(1)} %get-tuple-element.22.refs_0_.refs_3_, ...), custom_call_target="tpu_custom_call" | custom-call | tf_op jit(solution)/shard_map/pallas_call | solution.py:143
  46.1 1.3 %collective-permute-start.19 = (bf16[32,768]{1,0:T(8,128)(2,1)S(1)}, bf16[32,768]{1,0:T(8,128)(2,1)S(1)}, u32[]{:S(2)}, u32[]{:S(2)}) collective-permute-start(bf16[32,768]{1,0:T(8,128)(2,1)S(1)} %shard_map.68.refs_3_), channel_id=1, source_target_pairs={{0,24},{1,25},{2,26},{3,27},{4,28},{5,29},{6,30},{7,31},{8,16},{9,... | collective-permute-start | bytes 147464 | tf_op jit(solution)/shard_map/ppermute | solution.py:130
  47.4 0.7 %collective-permute-start.20 = (bf16[32,768]{1,0:T(8,128)(2,1)S(1)}, bf16[32,768]{1,0:T(8,128)(2,1)S(1)}, u32[]{:S(2)}, u32[]{:S(2)}) collective-permute-start(bf16[32,768]{1,0:T(8,128)(2,1)S(1)} %shard_map.68.refs_3_), channel_id=1, source_target_pairs={{0,16},{1,17},{2,18},{3,19},{4,20},{5,21},{6,22},{7,23},{8,24},{9,... | collective-permute-start | bytes 147464 | tf_op jit(solution)/shard_map/ppermute | solution.py:130
  48.1 1.5 %collective-permute-start.21 = (bf16[32,768]{1,0:T(8,128)(2,1)S(1)}, bf16[32,768]{1,0:T(8,128)(2,1)S(1)}, u32[]{:S(2)}, u32[]{:S(2)}) collective-permute-start(bf16[32,768]{1,0:T(8,128)(2,1)S(1)} %shard_map.68.refs_3_), channel_id=1, source_target_pairs={{0,8},{1,9},{2,10},{3,11},{4,12},{5,13},{6,14},{7,15},{8,0},{9,1},... | collective-permute-start | bytes 147464 | tf_op jit(solution)/shard_map/ppermute | solution.py:130
  49.6 1.5 %collective-permute-done.19.refs_0_ = bf16[32,768]{1,0:T(8,128)(2,1)S(1)} collective-permute-done((bf16[32,768]{1,0:T(8,128)(2,1)S(1)}, bf16[32,768]{1,0:T(8,128)(2,1)S(1)}, u32[]{:S(2)}, u32[]{:S(2)}) %collective-permute-start.19) | collective-permute-done | bytes 49184 | tf_op jit(solution)/shard_map/ppermute | solution.py:130
  51.1 0.5 collective-permute-done.20.refs_1_
  51.6 0.6 %collective-permute-done.21.refs_2_ = bf16[32,768]{1,0:T(8,128)(2,1)S(1)} collective-permute-done((bf16[32,768]{1,0:T(8,128)(2,1)S(1)}, bf16[32,768]{1,0:T(8,128)(2,1)S(1)}, u32[]{:S(2)}, u32[]{:S(2)}) %collective-permute-start.21) | collective-permute-done | bytes 49184 | tf_op jit(solution)/shard_map/ppermute | solution.py:130
  52.2 0.1 collective-permute-start.22
  52.3 0.1 stack.23.info
  52.4 0.7 %shard_map.65.refs_0_ = bf16[768,128]{1,0:T(8,128)(2,1)S(1)} custom-call(s32[5]{0:T(128)S(1)} %stack.23.info, bf16[64,768]{1,0:T(8,128)(2,1)S(1)} %collective-permute-done.13.refs_0_, bf16[64,768]{1,0:T(8,128)(2,1)S(1)} %get-tuple-element.19.refs_1_), custom_call_target="tpu_custom_call" | custom-call | tf_op jit(solution)/shard_map/pallas_call | solution.py:143
  53.1 0.5 collective-permute-done.22.refs_2_
  53.6 1.5 %shard_map.70 = (bf16[2,768,128]{2,1,0:T(8,128)(2,1)}, bf16[1,768,128]{2,1,0:T(8,128)(2,1)}) custom-call(s32[5]{0:T(128)S(1)} %stack.23.info, bf16[768,128]{1,0:T(8,128)(2,1)S(1)} %shard_map.65.refs_0_, bf16[64,768]{1,0:T(8,128)(2,1)S(1)} %shard_map.69.refs_1_, bf16[64,768]{1,0:T(8,128)(2,1)S(1)} %collective-permute-done.22.refs_2_), custom_call_target="tpu_custom_call" | custom-call | tf_op jit(solution)/shard_map/pallas_call | solution.py:311
  (22 shorter events, 0.2 us)
Async XLA Ops:
  0.6 7.2 %copy-start.3 = (bf16[1,768,128]{2,1,0:T(8,128)(2,1)S(1)}, bf16[1,768,128]{2,1,0:T(8,128)(2,1)}, u32[]{:S(2)}) copy-start(bf16[1,768,128]{2,1,0:T(8,128)(2,1)} %param.7) | copy-start | bytes 589828
  0.6 6.5 %copy-start.2 = (bf16[2,768,128]{2,1,0:T(8,128)(2,1)S(1)}, bf16[2,768,128]{2,1,0:T(8,128)(2,1)}, u32[]{:S(2)}) copy-start(bf16[2,768,128]{2,1,0:T(8,128)(2,1)} %refs_1_.6) | copy-start | bytes 1179652
  0.7 21.5 %collective-permute-start.2 = (bf16[768,768]{1,0:T(8,128)(2,1)}, bf16[768,768]{1,0:T(8,128)(2,1)S(1)}, u32[]{:S(2)}, u32[]{:S(2)}) collective-permute-start(bf16[768,768]{1,0:T(8,128)(2,1)} %refs_1_.7), channel_id=1, source_target_pairs={{0,4},{1,5},{2,6},{3,7},{4,0},{5,1},{6,2},{7,3},{8,12},{9,13},{10,... | collective-permute-start | bytes 3538952 | tf_op jit(solution)/shard_map/ppermute | solution.py:130
  1.2 25.3 %collective-permute-start = (bf16[768,768]{1,0:T(8,128)(2,1)}, bf16[768,768]{1,0:T(8,128)(2,1)S(1)}, u32[]{:S(2)}, u32[]{:S(2)}) collective-permute-start(bf16[768,768]{1,0:T(8,128)(2,1)} %bitcast.12), channel_id=1, source_target_pairs={{0,4},{1,5},{2,6},{3,7},{4,0},{5,1},{6,2},{7,3},{8,12},{9,13},{10,... | collective-permute-start | bytes 3538952 | tf_op jit(solution)/shard_map/ppermute | solution.py:130
  1.3 20.9 %copy-start.1 = (bf16[768,768]{1,0:T(8,128)(2,1)S(1)}, bf16[768,768]{1,0:T(8,128)(2,1)}, u32[]{:S(2)}) copy-start(bf16[768,768]{1,0:T(8,128)(2,1)} %refs_1_.7) | copy-start | bytes 3538948
  3.9 4.8 %collective-permute-start.4 = (bf16[32,768]{1,0:T(8,128)(2,1)S(1)}, bf16[32,768]{1,0:T(8,128)(2,1)S(1)}, u32[]{:S(2)}, u32[]{:S(2)}) collective-permute-start(bf16[32,768]{1,0:T(8,128)(2,1)S(1)} %get-tuple-element.16), channel_id=1, source_target_pairs={{0,20},{1,21},{2,22},{3,23},{4,16},{5,17},{6,18},{7,19},{8,28},{9,... | collective-permute-start | bytes 147464 | tf_op jit(solution)/shard_map/ppermute | solution.py:130
  6.6 2.2 %collective-permute-start.5 = (bf16[32,768]{1,0:T(8,128)(2,1)S(1)}, bf16[32,768]{1,0:T(8,128)(2,1)S(1)}, u32[]{:S(2)}, u32[]{:S(2)}) collective-permute-start(bf16[32,768]{1,0:T(8,128)(2,1)S(1)} %get-tuple-element.17), channel_id=1, source_target_pairs={{0,4},{1,5},{2,6},{3,7},{4,0},{5,1},{6,2},{7,3},{8,12},{9,13},{10,... | collective-permute-start | bytes 147464 | tf_op jit(solution)/shard_map/ppermute | solution.py:130
  7.0 4.1 %collective-permute-start.6 = (bf16[32,768]{1,0:T(8,128)(2,1)S(1)}, bf16[32,768]{1,0:T(8,128)(2,1)S(1)}, u32[]{:S(2)}, u32[]{:S(2)}) collective-permute-start(bf16[32,768]{1,0:T(8,128)(2,1)S(1)} %get-tuple-element.18), channel_id=1, source_target_pairs={{0,16},{1,17},{2,18},{3,19},{4,20},{5,21},{6,22},{7,23},{8,24},{9,... | collective-permute-start | bytes 147464 | tf_op jit(solution)/shard_map/ppermute | solution.py:130
  8.7 6.1 %collective-permute-start.3 = (bf16[32,768]{1,0:T(8,128)(2,1)S(1)}, bf16[32,768]{1,0:T(8,128)(2,1)S(1)}, u32[]{:S(2)}, u32[]{:S(2)}) collective-permute-start(bf16[32,768]{1,0:T(8,128)(2,1)S(1)} %get-tuple-element.14.refs_1_), channel_id=1, source_target_pairs={{0,4},{1,5},{2,6},{3,7},{4,0},{5,1},{6,2},{7,3},{8,12},{9,13},{10,... | collective-permute-start | bytes 147464 | tf_op jit(solution)/shard_map/ppermute | solution.py:130
  11.1 18.9 %copy-start = (bf16[1,768,768]{2,1,0:T(8,128)(2,1)S(1)}, bf16[1,768,768]{2,1,0:T(8,128)(2,1)}, u32[]{:S(2)}) copy-start(bf16[1,768,768]{2,1,0:T(8,128)(2,1)} %param.5) | copy-start | bytes 3538948
  11.1 7.0 %collective-permute-start.7 = (bf16[64,768]{1,0:T(8,128)(2,1)S(1)}, bf16[64,768]{1,0:T(8,128)(2,1)S(1)}, u32[]{:S(2)}, u32[]{:S(2)}) collective-permute-start(bf16[64,768]{1,0:T(8,128)(2,1)S(1)} %shard_map.62.refs_7_), channel_id=1, source_target_pairs={{0,3},{1,2},{2,1},{3,0},{4,7},{5,6},{6,5},{7,4},{8,11},{9,10},{10,... | collective-permute-start | bytes 294920 | tf_op jit(solution)/shard_map/ppermute | solution.py:130
  14.8 7.4 %collective-permute-start.8 = (bf16[64,768]{1,0:T(8,128)(2,1)S(1)}, bf16[64,768]{1,0:T(8,128)(2,1)S(1)}, u32[]{:S(2)}, u32[]{:S(2)}) collective-permute-start(bf16[64,768]{1,0:T(8,128)(2,1)S(1)} %shard_map.62.refs_7_), channel_id=1, source_target_pairs={{0,2},{1,3},{2,0},{3,1},{4,6},{5,7},{6,4},{7,5},{8,10},{9,11},{10,... | collective-permute-start | bytes 294920 | tf_op jit(solution)/shard_map/ppermute | solution.py:130
  14.8 7.3 %collective-permute-start.9 = (bf16[64,768]{1,0:T(8,128)(2,1)S(1)}, bf16[64,768]{1,0:T(8,128)(2,1)S(1)}, u32[]{:S(2)}, u32[]{:S(2)}) collective-permute-start(bf16[64,768]{1,0:T(8,128)(2,1)S(1)} %shard_map.62.refs_7_), channel_id=1, source_target_pairs={{0,1},{1,0},{2,3},{3,2},{4,5},{5,4},{6,7},{7,6},{8,9},{9,8},{10,11... | collective-permute-start | bytes 294920 | tf_op jit(solution)/shard_map/ppermute | solution.py:130
  18.2 8.3 %collective-permute-start.1 = (bf16[64,768]{1,0:T(8,128)(2,1)S(1)}, bf16[64,768]{1,0:T(8,128)(2,1)S(1)}, u32[]{:S(2)}, u32[]{:S(2)}) collective-permute-start(bf16[64,768]{1,0:T(8,128)(2,1)S(1)} %shard_map.60.refs_2_), channel_id=1, source_target_pairs={{0,16},{1,17},{2,18},{3,19},{4,20},{5,21},{6,22},{7,23},{8,24},{9,... | collective-permute-start | bytes 294920 | tf_op jit(solution)/shard_map/ppermute | solution.py:65
  23.0 5.1 %collective-permute-start.10 = (bf16[32,768]{1,0:T(8,128)(2,1)S(1)}, bf16[32,768]{1,0:T(8,128)(2,1)S(1)}, u32[]{:S(2)}, u32[]{:S(2)}) collective-permute-start(bf16[32,768]{1,0:T(8,128)(2,1)S(1)} %shard_map.63.refs_6_), channel_id=1, source_target_pairs={{0,24},{1,25},{2,26},{3,27},{4,28},{5,29},{6,30},{7,31},{8,16},{9,... | collective-permute-start | bytes 147464 | tf_op jit(solution)/shard_map/ppermute | solution.py:130
  25.7 4.1 %collective-permute-start.11 = (bf16[32,768]{1,0:T(8,128)(2,1)S(1)}, bf16[32,768]{1,0:T(8,128)(2,1)S(1)}, u32[]{:S(2)}, u32[]{:S(2)}) collective-permute-start(bf16[32,768]{1,0:T(8,128)(2,1)S(1)} %shard_map.63.refs_6_), channel_id=1, source_target_pairs={{0,16},{1,17},{2,18},{3,19},{4,20},{5,21},{6,22},{7,23},{8,24},{9,... | collective-permute-start | bytes 147464 | tf_op jit(solution)/shard_map/ppermute | solution.py:130
  26.0 4.1 %collective-permute-start.12 = (bf16[32,768]{1,0:T(8,128)(2,1)S(1)}, bf16[32,768]{1,0:T(8,128)(2,1)S(1)}, u32[]{:S(2)}, u32[]{:S(2)}) collective-permute-start(bf16[32,768]{1,0:T(8,128)(2,1)S(1)} %shard_map.63.refs_6_), channel_id=1, source_target_pairs={{0,8},{1,9},{2,10},{3,11},{4,12},{5,13},{6,14},{7,15},{8,0},{9,1},... | collective-permute-start | bytes 147464 | tf_op jit(solution)/shard_map/ppermute | solution.py:130
  30.9 4.7 %collective-permute-start.15 = (bf16[64,768]{1,0:T(8,128)(2,1)S(1)}, bf16[64,768]{1,0:T(8,128)(2,1)S(1)}, u32[]{:S(2)}, u32[]{:S(2)}) collective-permute-start(bf16[64,768]{1,0:T(8,128)(2,1)S(1)} %get-tuple-element.23), channel_id=1, source_target_pairs={{0,16},{1,17},{2,18},{3,19},{4,20},{5,21},{6,22},{7,23},{8,24},{9,... | collective-permute-start | bytes 294920 | tf_op jit(solution)/shard_map/ppermute | solution.py:130
  35.6 6.5 %collective-permute-start.16 = (bf16[64,768]{1,0:T(8,128)(2,1)S(1)}, bf16[64,768]{1,0:T(8,128)(2,1)S(1)}, u32[]{:S(2)}, u32[]{:S(2)}) collective-permute-start(bf16[64,768]{1,0:T(8,128)(2,1)S(1)} %shard_map.67.refs_7_), channel_id=1, source_target_pairs={{0,3},{1,2},{2,1},{3,0},{4,7},{5,6},{6,5},{7,4},{8,11},{9,10},{10,... | collective-permute-start | bytes 294920 | tf_op jit(solution)/shard_map/ppermute | solution.py:130
  38.7 5.6 %collective-permute-start.17 = (bf16[64,768]{1,0:T(8,128)(2,1)S(1)}, bf16[64,768]{1,0:T(8,128)(2,1)S(1)}, u32[]{:S(2)}, u32[]{:S(2)}) collective-permute-start(bf16[64,768]{1,0:T(8,128)(2,1)S(1)} %shard_map.67.refs_7_), channel_id=1, source_target_pairs={{0,2},{1,3},{2,0},{3,1},{4,6},{5,7},{6,4},{7,5},{8,10},{9,11},{10,... | collective-permute-start | bytes 294920 | tf_op jit(solution)/shard_map/ppermute | solution.py:130
  40.3 5.0 %collective-permute-start.18 = (bf16[64,768]{1,0:T(8,128)(2,1)S(1)}, bf16[64,768]{1,0:T(8,128)(2,1)S(1)}, u32[]{:S(2)}, u32[]{:S(2)}) collective-permute-start(bf16[64,768]{1,0:T(8,128)(2,1)S(1)} %shard_map.67.refs_7_), channel_id=1, source_target_pairs={{0,1},{1,0},{2,3},{3,2},{4,5},{5,4},{6,7},{7,6},{8,9},{9,8},{10,11... | collective-permute-start | bytes 294920 | tf_op jit(solution)/shard_map/ppermute | solution.py:130
  40.6 1.2 %collective-permute-start.14 = (bf16[32,768]{1,0:T(8,128)(2,1)S(1)}, bf16[32,768]{1,0:T(8,128)(2,1)S(1)}, u32[]{:S(2)}, u32[]{:S(2)}) collective-permute-start(bf16[32,768]{1,0:T(8,128)(2,1)S(1)} %get-tuple-element.21.refs_1_), channel_id=1, source_target_pairs={{0,4},{1,5},{2,6},{3,7},{4,0},{5,1},{6,2},{7,3},{8,12},{9,13},{10,... | collective-permute-start | bytes 147464 | tf_op jit(solution)/shard_map/ppermute | solution.py:130
  46.1 5.0 %collective-permute-start.19 = (bf16[32,768]{1,0:T(8,128)(2,1)S(1)}, bf16[32,768]{1,0:T(8,128)(2,1)S(1)}, u32[]{:S(2)}, u32[]{:S(2)}) collective-permute-start(bf16[32,768]{1,0:T(8,128)(2,1)S(1)} %shard_map.68.refs_3_), channel_id=1, source_target_pairs={{0,24},{1,25},{2,26},{3,27},{4,28},{5,29},{6,30},{7,31},{8,16},{9,... | collective-permute-start | bytes 147464 | tf_op jit(solution)/shard_map/ppermute | solution.py:130
  47.4 4.2 %collective-permute-start.20 = (bf16[32,768]{1,0:T(8,128)(2,1)S(1)}, bf16[32,768]{1,0:T(8,128)(2,1)S(1)}, u32[]{:S(2)}, u32[]{:S(2)}) collective-permute-start(bf16[32,768]{1,0:T(8,128)(2,1)S(1)} %shard_map.68.refs_3_), channel_id=1, source_target_pairs={{0,16},{1,17},{2,18},{3,19},{4,20},{5,21},{6,22},{7,23},{8,24},{9,... | collective-permute-start | bytes 147464 | tf_op jit(solution)/shard_map/ppermute | solution.py:130
  48.1 4.1 %collective-permute-start.21 = (bf16[32,768]{1,0:T(8,128)(2,1)S(1)}, bf16[32,768]{1,0:T(8,128)(2,1)S(1)}, u32[]{:S(2)}, u32[]{:S(2)}) collective-permute-start(bf16[32,768]{1,0:T(8,128)(2,1)S(1)} %shard_map.68.refs_3_), channel_id=1, source_target_pairs={{0,8},{1,9},{2,10},{3,11},{4,12},{5,13},{6,14},{7,15},{8,0},{9,1},... | collective-permute-start | bytes 147464 | tf_op jit(solution)/shard_map/ppermute | solution.py:130
  49.6 2.8 %collective-permute-start.13 = (bf16[64,768]{1,0:T(8,128)(2,1)S(1)}, bf16[64,768]{1,0:T(8,128)(2,1)S(1)}, u32[]{:S(2)}, u32[]{:S(2)}) collective-permute-start(bf16[64,768]{1,0:T(8,128)(2,1)S(1)} %get-tuple-element.19.refs_1_), channel_id=1, source_target_pairs={{0,4},{1,5},{2,6},{3,7},{4,0},{5,1},{6,2},{7,3},{8,12},{9,13},{10,... | collective-permute-start | bytes 294920 | tf_op jit(solution)/shard_map/ppermute | solution.py:130
  52.2 1.4 %collective-permute-start.22 = (bf16[64,768]{1,0:T(8,128)(2,1)S(1)}, bf16[64,768]{1,0:T(8,128)(2,1)S(1)}, u32[]{:S(2)}, u32[]{:S(2)}) collective-permute-start(bf16[64,768]{1,0:T(8,128)(2,1)S(1)} %shard_map.69.refs_1_), channel_id=1, source_target_pairs={{0,4},{1,5},{2,6},{3,7},{4,0},{5,1},{6,2},{7,3},{8,12},{9,13},{10,... | collective-permute-start | bytes 294920 | tf_op jit(solution)/shard_map/ppermute | solution.py:130

commit v4 on v3

--- a/solution.py
+++ b/solution.py
@@ -129,25 +129,27 @@
                     pairs.append(((d * self.nr + r) * self.nc + z, to))
         return lax.ppermute(block, ("delay", "row", "col"), pairs)
 
-    def owners(self):
-        return [(self.n ^ kn) * self.nd + (self.d ^ kd) for kn in range(self.near) for kd in range(self.nd)]
-
-
-def turned_about(body, loose, count, info, *refs):
+
+def farthest_first(body, numbers, loose, count, *refs):
+    info, refs = [ref[0] for ref in refs[:numbers]], refs[numbers:]
     inputs = refs[loose : loose + count][::-1]
     body(loose, info, *refs[:loose], *inputs, *refs[loose + count :])
 
 
 def kernel_call(body, out_shape, info, inputs, loose=(), scratch=()):
-    vmem = pl.BlockSpec(memory_space=pltpu.VMEM)
+    vmem, smem = pl.BlockSpec(memory_space=pltpu.VMEM), pl.BlockSpec(memory_space=pltpu.SMEM)
     return pl.pallas_call(
-        functools.partial(turned_about, body, len(loose), len(inputs)),
+        functools.partial(farthest_first, body, len(info), len(loose), len(inputs)),
         out_shape=out_shape,
-        in_specs=[pl.BlockSpec(memory_space=pltpu.SMEM)] + [pl.BlockSpec(memory_space=pl.ANY)] * len(loose) + [vmem] * len(inputs),
+        in_specs=[smem] * len(info) + [pl.BlockSpec(memory_space=pl.ANY)] * len(loose) + [vmem] * len(inputs),
         out_specs=jax.tree.map(lambda _: vmem, out_shape),
         scratch_shapes=list(scratch),
         compiler_params=pltpu.CompilerParams(vmem_limit_bytes=8 << 20),
-    )(jnp.stack(info), *loose, *inputs[::-1])
+    )(*[jnp.reshape(number, (1,)) for number in info], *loose, *inputs[::-1])
+
+
+def owner(info, nd, k):
+    return (info[1] ^ (k // nd)) * nd + (info[0] ^ (k % nd))
 
 
 def total_of(refs):
@@ -158,16 +160,16 @@
     return ref[pl.ds(pl.multiple_of(index * rows, rows), rows), :]
 
 
-def begin_body(loose, info, total_ref, *pieces):
+def begin_body(nd, loose, info, total_ref, *pieces):
     for k, piece in enumerate(pieces):
-        piece[...] = part_of(total_ref, info[k], piece.shape[0])
+        piece[...] = part_of(total_ref, owner(info, nd, k), piece.shape[0])
 
 
 def begin(lay, past, operator):
     total = lax.dot_general(past, operator, (((0,), (1,)), ((), ())), preferred_element_type=F32).astype(BF16)
-    owners = lay.owners()
-    out = [jax.ShapeDtypeStruct((total.shape[0] // len(owners), total.shape[1]), BF16)] * len(owners)
-    return kernel_call(begin_body, out, owners, (total,))
+    count = lay.near * lay.nd
+    out = [jax.ShapeDtypeStruct((total.shape[0] // count, total.shape[1]), BF16)] * count
+    return kernel_call(functools.partial(begin_body, lay.nd), out, [lay.d, lay.n], (total,))
 
 
 def part_body(loose, info, *refs):
@@ -182,32 +184,32 @@
     return kernel_call(part_body, out, [lay.n], (past,), after, [pltpu.VMEM((exc, columns), F32)])
 
 
-def wave_body(step, loose, info, *refs):
+def wave_body(step, nd, loose, info, *refs):
     incident_ref, outs, turned = refs[loose], refs[loose + 1 : -1], refs[-1]
     turned[...] = incident_ref[step].astype(F32).T
     for kn, out in enumerate(outs):
-        out[...] = part_of(turned, info[kn], out.shape[0]).astype(BF16)
+        out[...] = part_of(turned, owner(info, nd, kn * nd), out.shape[0]).astype(BF16)
 
 
 def wave_cut(lay, incident, step, after):
     rows, exc = incident.shape[1:]
-    owners = lay.owners()[:: lay.nd]
     out = [jax.ShapeDtypeStruct((exc // (lay.near * lay.nd), rows), BF16)] * lay.near
-    body = functools.partial(wave_body, step)
-    return kernel_call(body, out, owners, (incident,), after, [pltpu.VMEM((exc, rows), F32)])
-
-
-def join_body(near, loose, info, *refs):
+    body = functools.partial(wave_body, step, lay.nd)
+    return kernel_call(body, out, [lay.d, lay.n], (incident,), after, [pltpu.VMEM((exc, rows), F32)])
+
+
+def join_body(count, loose, info, *refs):
     ins, out = refs[loose:-1], refs[-1]
-    per, rows = len(ins) // near, ins[0].shape[0]
-    for kn in range(near):
-        out[pl.ds(kn * rows, rows), :] = total_of(ins[kn * per : (kn + 1) * per]).astype(BF16)
+    rows = ins[0].shape[0]
+    for k in range(count):
+        out[pl.ds(k * rows, rows), :] = total_of(ins[k::count]).astype(BF16)
 
 
 def join(lay, groups, loose=()):
     rows, columns = groups[0][0].shape
     out = jax.ShapeDtypeStruct((rows * len(groups), columns), BF16)
-    return kernel_call(functools.partial(join_body, len(groups)), out, [lay.d], [b for g in groups for b in g], loose)
+    flat = [block for blocks in zip(*groups) for block in blocks]
+    return kernel_call(functools.partial(join_body, len(groups)), out, [lay.d], flat, loose)
 
 
 def invert_body(near, loose, info, *refs):
@@ -233,10 +235,9 @@
     refs, outs = refs[: -1 - nd], refs[-1 - nd :]
     parts, past_ref, operators = refs[: -1 - near], refs[-1 - near], refs[-near:]
     current_ref, totals = outs[0], outs[1:]
-    far = len(parts) // nd
     rows = parts[0].shape[0]
     for kd in range(nd):
-        current_ref[pl.ds(kd * rows, rows), :] = total_of(parts[kd * far : (kd + 1) * far]).astype(BF16)
+        current_ref[pl.ds(kd * rows, rows), :] = total_of(parts[kd::nd]).astype(BF16)
 
     @pl.when(info[0] == 0)
     def _():
@@ -262,27 +263,27 @@
     return current, totals
 
 
-def place(info, blocks, total):
-    pieces = info.shape[0] - 1
-    rows = total.shape[0] // pieces
-    each = blocks[0].shape[0] // rows
-    for k in range(pieces):
-        start = pl.multiple_of(info[1 + k] * rows, rows)
-        total[pl.ds(start, rows), :] = blocks[k // each][pl.ds((k % each) * rows, rows), :].astype(F32)
+def place(info, nd, blocks, total):
+    rows = blocks[0].shape[0] // nd
+    for k in range(total.shape[0] // rows):
+        start = pl.multiple_of(owner(info, nd, k) * rows, rows)
+        total[pl.ds(start, rows), :] = blocks[k // nd][pl.ds((k % nd) * rows, rows), :].astype(F32)
     return total[...].T.astype(BF16)
 
 
-def turn_body(loose, info, *refs):
-    refs[-2][...] = place(info, refs[loose:-2], refs[-1])
+def turn_body(nd, loose, info, *refs):
+    refs[-2][...] = place(info, nd, refs[loose:-2], refs[-1])
 
 
 def turn(lay, blocks):
     columns, exc = blocks[0].shape[1], blocks[0].shape[0] * lay.near
     out = jax.ShapeDtypeStruct((columns, exc), BF16)
-    return kernel_call(turn_body, out, [lay.d, *lay.owners()], blocks, (), [pltpu.VMEM((exc, columns), F32)])
-
-
-def finish_body(done, info, *refs):
+    scratch = [pltpu.VMEM((exc, columns), F32)]
+    return kernel_call(functools.partial(turn_body, lay.nd), out, [lay.d, lay.n], blocks, (), scratch)
+
+
+def finish_body(done, nd, d_ref, n_ref, *refs):
+    info = [d_ref[0], n_ref[0]]
     earlier, blocks, (out, hist, total, turned, sems) = refs[:done], refs[done:-5], refs[-5:]
 
     def store(step, source):
@@ -297,7 +298,7 @@
         return copy, kept
 
     copies = [store(step, source) for step, source in enumerate(earlier)]
-    turned[...] = place(info, blocks, total)
+    turned[...] = place(info, nd, blocks, total)
     copies.append(store(done, turned))
     for copy, _ in copies:
         copy.wait()
@@ -307,20 +308,21 @@
 def finish(lay, earlier, blocks):
     done = len(earlier)
     columns, exc = earlier[0].shape
-    hbm, vmem = pl.BlockSpec(memory_space=pltpu.HBM), pl.BlockSpec(memory_space=pltpu.VMEM)
+    hbm, vmem, smem = [pl.BlockSpec(memory_space=space) for space in (pltpu.HBM, pltpu.VMEM, pltpu.SMEM)]
+    scratch = [pltpu.VMEM((exc, columns), F32), pltpu.VMEM((columns, exc), BF16), pltpu.SemaphoreType.DMA((done + 2,))]
     return pl.pallas_call(
-        functools.partial(finish_body, done),
+        functools.partial(finish_body, done, lay.nd),
         out_shape=[jax.ShapeDtypeStruct((k, columns, exc), BF16) for k in (done + 1, 1)],
-        in_specs=[pl.BlockSpec(memory_space=pltpu.SMEM)] + [vmem] * (done + len(blocks)),
+        in_specs=[smem] * 2 + [vmem] * (done + len(blocks)),
         out_specs=[hbm] * 2,
-        scratch_shapes=[pltpu.VMEM((exc, columns), F32), pltpu.VMEM((columns, exc), BF16), pltpu.SemaphoreType.DMA((done + 2,))],
+        scratch_shapes=scratch,
         compiler_params=pltpu.CompilerParams(vmem_limit_bytes=8 << 20),
-    )(jnp.stack([lay.d, *lay.owners()]), *earlier, *blocks)
+    )(jnp.reshape(lay.d, (1,)), jnp.reshape(lay.n, (1,)), *earlier, *blocks)
 
 
 def over_rows(lay, partial):
     return [
-        lay.move(partial, kd=kd, kf=kf) if kd or kf else partial for kd in range(lay.nd) for kf in range(lay.far)
+        lay.move(partial, kd=kd, kf=kf) if kd or kf else partial for kf in range(lay.far) for kd in range(lay.nd)
     ]
 
 
@@ -358,7 +360,7 @@
     turned = turn(lay, over_near(lay, current))
     partial = invert(lay, along_col(lay, total), from_cores(lay, cuts), inverse, ())
     across = over_rows(lay, partial)
-    last = join(lay, [across[kd * lay.far : (kd + 1) * lay.far] for kd in range(lay.nd)])
+    last = join(lay, [across[kd :: lay.nd] for kd in range(lay.nd)])
     return tuple(finish(lay, [turned], over_near(lay, last)))
 
 

time: 55.2 us -> 54 us (0.978)
  waiting for transfers between devices: 19.9 us -> 23.8 us
  Pallas kernels: 6.76 us -> 4.07 us
  starting transfers between devices: 25.4 us -> 23.2 us
    ppermute x22, waiting for transfers between devices: 19.9 us -> 23.8 us  [move(): return lax.ppermute(block, ('delay', 'row', 'col'), pairs)]
    pallas_call x12, Pallas kernels: 6.76 us -> 4.07 us  [the longest x11 3.14 us: kernel_call(): pl.pallas_call(functools.partial(farthest_first, body, len(info), len(loo...]
    ppermute x22, starting transfers between devices: 22.2 us -> 20 us  [move(): return lax.ppermute(block, ('delay', 'row', 'col'), pairs)]
  transfers between devices with their start and end apart: 23 -> 23, of which waited for: 16 -> 15; matrix products, arithmetic and copies ran while one was open for 4% -> 4% of each run, Pallas kernels for 7% -> 3%
where the time goes in v4:
time: 54 us; the launch traced here: 53.9 us
  waiting for transfers between devices  23.8 us (44%)
  starting transfers between devices  23.2 us (43%)
  Pallas kernels  4.07 us (8%)
  matrix products  1.98 us (4%)
  between operations  0.77 us (1%)
    ppermute x22, waiting for transfers between devices, move(): return lax.ppermute(block, ('delay', 'row', 'col'), pairs)  23.8 us
    ppermute x22, starting transfers between devices, move(): return lax.ppermute(block, ('delay', 'row', 'col'), pairs)  20 us
    ppermute x1, starting transfers between devices, from_behind(): return lax.ppermute(block, axis, route) if route else jnp.zeros_like(block)  3.21 us
    pallas_call x11, Pallas kernels, kernel_call(): pl.pallas_call(functools.partial(farthest_first, body, len(info), len(loo...  3.14 us
    dot_general x1, matrix products, begin(): lax.dot_general(past, operator, (((0,), (1,)), ((), ())), preferred_eleme...  1.98 us
  transfers between devices with their start and end apart: 23, of which 15 were waited for; matrix products, arithmetic and copies ran while one was open for 4% of the time, Pallas kernels for 3%

profile of v4, /device:TPU:0, one launch (start us, length us, event | category | flops | bytes accessed | tf_op | source)
XLA Modules:
  0.0 53.9 jit_solution(8545564496357789107)
XLA Ops:
  0.6 0.5 collective-permute-start.2
  1.2 0.1 collective-permute-start
  1.2 2.0 %convolution_convert_fusion.refs_2_ = bf16[128,768]{1,0:T(8,128)(2,1)S(1)} fusion(bf16[1,768,128]{2,1,0:T(8,128)(2,1)} %param.7, bf16[1,768,768]{2,1,0:T(8,128)(2,1)} %param.5), kind=kOutput, calls=%fused_computation | convolution fusion | flops 151093248 | bytes 1572864 | tf_op jit(solution)/shard_map/dot_general | solution.py:169
  3.3 2.7 %collective-permute-start.4 = (bf16[32,768]{1,0:T(8,128)(2,1)S(1)}, bf16[32,768]{1,0:T(8,128)(2,1)S(1)}, u32[]{:S(2)}, u32[]{:S(2)}) collective-permute-start(bf16[32,768]{1,0:T(8,128)(2,1)S(1)} %get-tuple-element.16), channel_id=1, source_target_pairs={{0,20},{1,21},{2,22},{3,23},{4,16},{5,17},{6,18},{7,19},{8,28},{9,... | collective-permute-start | bytes 147464 | tf_op jit(solution)/shard_map/ppermute | solution.py:130
  6.0 0.4 collective-permute-start.5
  6.4 0.0 collective-permute-start.6
  6.4 0.1 shard_map.61
  6.6 0.1 shard_map.60.refs_3_
  6.7 1.4 %collective-permute-done.4.refs_4_ = bf16[32,768]{1,0:T(8,128)(2,1)S(1)} collective-permute-done((bf16[32,768]{1,0:T(8,128)(2,1)S(1)}, bf16[32,768]{1,0:T(8,128)(2,1)S(1)}, u32[]{:S(2)}, u32[]{:S(2)}) %collective-permute-start.4) | collective-permute-done | bytes 49184 | tf_op jit(solution)/shard_map/ppermute | solution.py:130
  8.1 0.1 collective-permute-start.3
  8.2 1.9 %collective-permute-done.5.refs_5_ = bf16[32,768]{1,0:T(8,128)(2,1)S(1)} collective-permute-done((bf16[32,768]{1,0:T(8,128)(2,1)S(1)}, bf16[32,768]{1,0:T(8,128)(2,1)S(1)}, u32[]{:S(2)}, u32[]{:S(2)}) %collective-permute-start.5) | collective-permute-done | bytes 49184 | tf_op jit(solution)/shard_map/ppermute | solution.py:130
  10.1 0.0 collective-permute-done.6.refs_6_
  10.1 0.0 copy-start
  10.1 3.7 %collective-permute-start.7 = (bf16[64,768]{1,0:T(8,128)(2,1)S(1)}, bf16[64,768]{1,0:T(8,128)(2,1)S(1)}, u32[]{:S(2)}, u32[]{:S(2)}) collective-permute-start(bf16[64,768]{1,0:T(8,128)(2,1)S(1)} %shard_map.62.refs_8_), channel_id=1, source_target_pairs={{0,3},{1,2},{2,1},{3,0},{4,7},{5,6},{6,5},{7,4},{8,11},{9,10},{10,... | collective-permute-start | bytes 294920 | tf_op jit(solution)/shard_map/ppermute | solution.py:130
  13.8 0.8 %collective-permute-start.9 = (bf16[64,768]{1,0:T(8,128)(2,1)S(1)}, bf16[64,768]{1,0:T(8,128)(2,1)S(1)}, u32[]{:S(2)}, u32[]{:S(2)}) collective-permute-start(bf16[64,768]{1,0:T(8,128)(2,1)S(1)} %shard_map.62.refs_8_), channel_id=1, source_target_pairs={{0,1},{1,0},{2,3},{3,2},{4,5},{5,4},{6,7},{7,6},{8,9},{9,8},{10,11... | collective-permute-start | bytes 294920 | tf_op jit(solution)/shard_map/ppermute | solution.py:130
  14.6 2.9 %collective-permute-done.7.refs_5_ = bf16[64,768]{1,0:T(8,128)(2,1)S(1)} collective-permute-done((bf16[64,768]{1,0:T(8,128)(2,1)S(1)}, bf16[64,768]{1,0:T(8,128)(2,1)S(1)}, u32[]{:S(2)}, u32[]{:S(2)}) %collective-permute-start.7) | collective-permute-done | bytes 98336 | tf_op jit(solution)/shard_map/ppermute | solution.py:130
  17.5 3.2 %collective-permute-start.1 = (bf16[64,768]{1,0:T(8,128)(2,1)S(1)}, bf16[64,768]{1,0:T(8,128)(2,1)S(1)}, u32[]{:S(2)}, u32[]{:S(2)}) collective-permute-start(bf16[64,768]{1,0:T(8,128)(2,1)S(1)} %shard_map.60.refs_3_), channel_id=1, source_target_pairs={{0,16},{1,17},{2,18},{3,19},{4,20},{5,21},{6,22},{7,23},{8,24},{9,... | collective-permute-start | bytes 294920 | tf_op jit(solution)/shard_map/ppermute | solution.py:65
  20.7 0.8 %collective-permute-done.8.refs_6_ = bf16[64,768]{1,0:T(8,128)(2,1)S(1)} collective-permute-done((bf16[64,768]{1,0:T(8,128)(2,1)S(1)}, bf16[64,768]{1,0:T(8,128)(2,1)S(1)}, u32[]{:S(2)}, u32[]{:S(2)}) %collective-permute-start.8) | collective-permute-done | bytes 98336 | tf_op jit(solution)/shard_map/ppermute | solution.py:130
  21.5 0.0 collective-permute-done.9.refs_7_
  21.5 0.0 collective-permute-done.2.refs_1_
  21.5 0.8 %shard_map.63.refs_7_ = bf16[32,768]{1,0:T(8,128)(2,1)S(1)} custom-call(s32[1]{0:T(128)} %bitcast.refs_0_.d_ref, bf16[768,768]{1,0:T(8,128)(2,1)S(1)} %collective-permute-done.2.refs_1_, bf16[768,768]{1,0:T(8,128)(2,1)S(1)} %copy-done.1, bf16[32,768]{1,0:T(8,128)(2,1)S(1)} %collective-permute-done.3.refs_3_, ...), custom_call_target="tpu_custom_call" | custom-call | tf_op jit(solution)/shard_map/pallas_call | solution.py:141
  22.3 2.9 %collective-permute-start.10 = (bf16[32,768]{1,0:T(8,128)(2,1)S(1)}, bf16[32,768]{1,0:T(8,128)(2,1)S(1)}, u32[]{:S(2)}, u32[]{:S(2)}) collective-permute-start(bf16[32,768]{1,0:T(8,128)(2,1)S(1)} %shard_map.63.refs_7_), channel_id=1, source_target_pairs={{0,24},{1,25},{2,26},{3,27},{4,28},{5,29},{6,30},{7,31},{8,16},{9,... | collective-permute-start | bytes 147464 | tf_op jit(solution)/shard_map/ppermute | solution.py:130
  25.1 0.5 collective-permute-start.11
  25.7 0.1 collective-permute-start.12
  25.8 1.5 %collective-permute-done.10.refs_4_ = bf16[32,768]{1,0:T(8,128)(2,1)S(1)} collective-permute-done((bf16[32,768]{1,0:T(8,128)(2,1)S(1)}, bf16[32,768]{1,0:T(8,128)(2,1)S(1)}, u32[]{:S(2)}, u32[]{:S(2)}) %collective-permute-start.10) | collective-permute-done | bytes 49184 | tf_op jit(solution)/shard_map/ppermute | solution.py:130
  27.3 1.9 %collective-permute-done.11.refs_5_ = bf16[32,768]{1,0:T(8,128)(2,1)S(1)} collective-permute-done((bf16[32,768]{1,0:T(8,128)(2,1)S(1)}, bf16[32,768]{1,0:T(8,128)(2,1)S(1)}, u32[]{:S(2)}, u32[]{:S(2)}) %collective-permute-start.11) | collective-permute-done | bytes 49184 | tf_op jit(solution)/shard_map/ppermute | solution.py:130
  29.2 0.5 collective-permute-done.12.refs_6_
  29.8 0.9 %shard_map.64 = (bf16[64,768]{1,0:T(8,128)(2,1)S(1)}, bf16[64,768]{1,0:T(8,128)(2,1)S(1)}, bf16[64,768]{1,0:T(8,128)(2,1)S(1)}) custom-call(s32[1]{0:T(128)} %bitcast.refs_0_.d_ref, bf16[768,768]{1,0:T(8,128)(2,1)S(1)} %collective-permute-done.refs_1_, bf16[768,768]{1,0:T(8,128)(2,1)S(1)} %bitcast.9, bf16[64,768]{1,0:T(8,128)(2,1)S(1)} %collective-permute-done.1.refs_3_, ...), custom_call_target="tpu_custom_call" | custom-call | tf_op jit(solution)/shard_map/pallas_call | solution.py:141
  30.6 0.2 collective-permute-start.15
  30.8 0.1 shard_map.66
  31.0 4.3 %collective-permute-done.15.refs_3_ = bf16[64,768]{1,0:T(8,128)(2,1)S(1)} collective-permute-done((bf16[64,768]{1,0:T(8,128)(2,1)S(1)}, bf16[64,768]{1,0:T(8,128)(2,1)S(1)}, u32[]{:S(2)}, u32[]{:S(2)}) %collective-permute-start.15) | collective-permute-done | bytes 98336 | tf_op jit(solution)/shard_map/ppermute | solution.py:130
  35.4 2.6 %collective-permute-start.16 = (bf16[64,768]{1,0:T(8,128)(2,1)S(1)}, bf16[64,768]{1,0:T(8,128)(2,1)S(1)}, u32[]{:S(2)}, u32[]{:S(2)}) collective-permute-start(bf16[64,768]{1,0:T(8,128)(2,1)S(1)} %shard_map.67.refs_8_), channel_id=1, source_target_pairs={{0,3},{1,2},{2,1},{3,0},{4,7},{5,6},{6,5},{7,4},{8,11},{9,10},{10,... | collective-permute-start | bytes 294920 | tf_op jit(solution)/shard_map/ppermute | solution.py:130
  37.9 0.4 collective-permute-start.17
  38.3 1.5 %collective-permute-start.18 = (bf16[64,768]{1,0:T(8,128)(2,1)S(1)}, bf16[64,768]{1,0:T(8,128)(2,1)S(1)}, u32[]{:S(2)}, u32[]{:S(2)}) collective-permute-start(bf16[64,768]{1,0:T(8,128)(2,1)S(1)} %shard_map.67.refs_8_), channel_id=1, source_target_pairs={{0,1},{1,0},{2,3},{3,2},{4,5},{5,4},{6,7},{7,6},{8,9},{9,8},{10,11... | collective-permute-start | bytes 294920 | tf_op jit(solution)/shard_map/ppermute | solution.py:130
  39.8 1.2 %collective-permute-done.14.refs_3_ = bf16[32,768]{1,0:T(8,128)(2,1)S(1)} collective-permute-done((bf16[32,768]{1,0:T(8,128)(2,1)S(1)}, bf16[32,768]{1,0:T(8,128)(2,1)S(1)}, u32[]{:S(2)}, u32[]{:S(2)}) %collective-permute-start.14) | collective-permute-done | bytes 49184 | tf_op jit(solution)/shard_map/ppermute | solution.py:130
  41.0 0.9 %collective-permute-done.16.refs_5_ = bf16[64,768]{1,0:T(8,128)(2,1)S(1)} collective-permute-done((bf16[64,768]{1,0:T(8,128)(2,1)S(1)}, bf16[64,768]{1,0:T(8,128)(2,1)S(1)}, u32[]{:S(2)}, u32[]{:S(2)}) %collective-permute-start.16) | collective-permute-done | bytes 98336 | tf_op jit(solution)/shard_map/ppermute | solution.py:130
  41.9 2.6 %collective-permute-done.17.refs_6_ = bf16[64,768]{1,0:T(8,128)(2,1)S(1)} collective-permute-done((bf16[64,768]{1,0:T(8,128)(2,1)S(1)}, bf16[64,768]{1,0:T(8,128)(2,1)S(1)}, u32[]{:S(2)}, u32[]{:S(2)}) %collective-permute-start.17) | collective-permute-done | bytes 98336 | tf_op jit(solution)/shard_map/ppermute | solution.py:130
  44.5 0.8 %shard_map.68.refs_4_ = bf16[32,768]{1,0:T(8,128)(2,1)S(1)} custom-call(s32[1]{0:T(128)} %bitcast.refs_0_.d_ref, bf16[768,768]{1,0:T(8,128)(2,1)S(1)} %collective-permute-done.2.refs_1_, bf16[768,768]{1,0:T(8,128)(2,1)S(1)} %copy-done.1, bf16[32,768]{1,0:T(8,128)(2,1)S(1)} %collective-permute-done.14.refs_3_, ...), custom_call_target="tpu_custom_call" | custom-call | tf_op jit(solution)/shard_map/pallas_call | solution.py:141
  45.3 1.6 %collective-permute-start.19 = (bf16[32,768]{1,0:T(8,128)(2,1)S(1)}, bf16[32,768]{1,0:T(8,128)(2,1)S(1)}, u32[]{:S(2)}, u32[]{:S(2)}) collective-permute-start(bf16[32,768]{1,0:T(8,128)(2,1)S(1)} %shard_map.68.refs_4_), channel_id=1, source_target_pairs={{0,24},{1,25},{2,26},{3,27},{4,28},{5,29},{6,30},{7,31},{8,16},{9,... | collective-permute-start | bytes 147464 | tf_op jit(solution)/shard_map/ppermute | solution.py:130
  46.9 0.5 collective-permute-start.20
  47.4 1.4 %collective-permute-start.21 = (bf16[32,768]{1,0:T(8,128)(2,1)S(1)}, bf16[32,768]{1,0:T(8,128)(2,1)S(1)}, u32[]{:S(2)}, u32[]{:S(2)}) collective-permute-start(bf16[32,768]{1,0:T(8,128)(2,1)S(1)} %shard_map.68.refs_4_), channel_id=1, source_target_pairs={{0,16},{1,17},{2,18},{3,19},{4,20},{5,21},{6,22},{7,23},{8,24},{9,... | collective-permute-start | bytes 147464 | tf_op jit(solution)/shard_map/ppermute | solution.py:130
  48.8 1.5 %collective-permute-done.19.refs_1_ = bf16[32,768]{1,0:T(8,128)(2,1)S(1)} collective-permute-done((bf16[32,768]{1,0:T(8,128)(2,1)S(1)}, bf16[32,768]{1,0:T(8,128)(2,1)S(1)}, u32[]{:S(2)}, u32[]{:S(2)}) %collective-permute-start.19) | collective-permute-done | bytes 49184 | tf_op jit(solution)/shard_map/ppermute | solution.py:130
  50.3 0.7 %collective-permute-done.20.refs_2_ = bf16[32,768]{1,0:T(8,128)(2,1)S(1)} collective-permute-done((bf16[32,768]{1,0:T(8,128)(2,1)S(1)}, bf16[32,768]{1,0:T(8,128)(2,1)S(1)}, u32[]{:S(2)}, u32[]{:S(2)}) %collective-permute-start.20) | collective-permute-done | bytes 49184 | tf_op jit(solution)/shard_map/ppermute | solution.py:130
  51.0 0.5 collective-permute-done.21.refs_3_
  51.6 0.1 collective-permute-start.22
  51.7 0.2 shard_map.65.refs_0_
  51.8 1.1 %collective-permute-done.22.refs_2_ = bf16[64,768]{1,0:T(8,128)(2,1)S(1)} collective-permute-done((bf16[64,768]{1,0:T(8,128)(2,1)S(1)}, bf16[64,768]{1,0:T(8,128)(2,1)S(1)}, u32[]{:S(2)}, u32[]{:S(2)}) %collective-permute-start.22) | collective-permute-done | bytes 98336 | tf_op jit(solution)/shard_map/ppermute | solution.py:130
  52.9 0.9 %shard_map.70 = (bf16[2,768,128]{2,1,0:T(8,128)(2,1)}, bf16[1,768,128]{2,1,0:T(8,128)(2,1)}) custom-call(s32[1]{0:T(128)} %bitcast.refs_0_.d_ref, s32[1]{0:T(128)} %bitcast.1.refs_1_.refs_0_.n_ref, bf16[768,128]{1,0:T(8,128)(2,1)S(1)} %shard_map.65.refs_0_, bf16[64,768]{1,0:T(8,128)(2,1)S(1)} %shard_map.69.refs_1_, ...), custom_call_target="tpu_custom_call" | custom-call | tf_op jit(solution)/shard_map/pallas_call | solution.py:313
  (19 shorter events, 0.1 us)
Async XLA Ops:
  0.6 5.9 %copy-start.3 = (bf16[1,768,128]{2,1,0:T(8,128)(2,1)S(1)}, bf16[1,768,128]{2,1,0:T(8,128)(2,1)}, u32[]{:S(2)}) copy-start(bf16[1,768,128]{2,1,0:T(8,128)(2,1)} %param.7) | copy-start | bytes 589828
  0.6 5.8 %copy-start.2 = (bf16[2,768,128]{2,1,0:T(8,128)(2,1)S(1)}, bf16[2,768,128]{2,1,0:T(8,128)(2,1)}, u32[]{:S(2)}) copy-start(bf16[2,768,128]{2,1,0:T(8,128)(2,1)} %refs_3_.3) | copy-start | bytes 1179652
  0.6 20.8 %collective-permute-start.2 = (bf16[768,768]{1,0:T(8,128)(2,1)}, bf16[768,768]{1,0:T(8,128)(2,1)S(1)}, u32[]{:S(2)}, u32[]{:S(2)}) collective-permute-start(bf16[768,768]{1,0:T(8,128)(2,1)} %refs_2_.3), channel_id=1, source_target_pairs={{0,4},{1,5},{2,6},{3,7},{4,0},{5,1},{6,2},{7,3},{8,12},{9,13},{10,... | collective-permute-start | bytes 3538952 | tf_op jit(solution)/shard_map/ppermute | solution.py:130
  1.2 24.6 %collective-permute-start = (bf16[768,768]{1,0:T(8,128)(2,1)}, bf16[768,768]{1,0:T(8,128)(2,1)S(1)}, u32[]{:S(2)}, u32[]{:S(2)}) collective-permute-start(bf16[768,768]{1,0:T(8,128)(2,1)} %bitcast.8), channel_id=1, source_target_pairs={{0,4},{1,5},{2,6},{3,7},{4,0},{5,1},{6,2},{7,3},{8,12},{9,13},{10,... | collective-permute-start | bytes 3538952 | tf_op jit(solution)/shard_map/ppermute | solution.py:130
  1.2 20.2 %copy-start.1 = (bf16[768,768]{1,0:T(8,128)(2,1)S(1)}, bf16[768,768]{1,0:T(8,128)(2,1)}, u32[]{:S(2)}) copy-start(bf16[768,768]{1,0:T(8,128)(2,1)} %refs_2_.3) | copy-start | bytes 3538948
  3.3 4.8 %collective-permute-start.4 = (bf16[32,768]{1,0:T(8,128)(2,1)S(1)}, bf16[32,768]{1,0:T(8,128)(2,1)S(1)}, u32[]{:S(2)}, u32[]{:S(2)}) collective-permute-start(bf16[32,768]{1,0:T(8,128)(2,1)S(1)} %get-tuple-element.16), channel_id=1, source_target_pairs={{0,20},{1,21},{2,22},{3,23},{4,16},{5,17},{6,18},{7,19},{8,28},{9,... | collective-permute-start | bytes 147464 | tf_op jit(solution)/shard_map/ppermute | solution.py:130
  6.0 4.1 %collective-permute-start.5 = (bf16[32,768]{1,0:T(8,128)(2,1)S(1)}, bf16[32,768]{1,0:T(8,128)(2,1)S(1)}, u32[]{:S(2)}, u32[]{:S(2)}) collective-permute-start(bf16[32,768]{1,0:T(8,128)(2,1)S(1)} %get-tuple-element.17), channel_id=1, source_target_pairs={{0,16},{1,17},{2,18},{3,19},{4,20},{5,21},{6,22},{7,23},{8,24},{9,... | collective-permute-start | bytes 147464 | tf_op jit(solution)/shard_map/ppermute | solution.py:130
  6.4 3.7 %collective-permute-start.6 = (bf16[32,768]{1,0:T(8,128)(2,1)S(1)}, bf16[32,768]{1,0:T(8,128)(2,1)S(1)}, u32[]{:S(2)}, u32[]{:S(2)}) collective-permute-start(bf16[32,768]{1,0:T(8,128)(2,1)S(1)} %get-tuple-element.18), channel_id=1, source_target_pairs={{0,4},{1,5},{2,6},{3,7},{4,0},{5,1},{6,2},{7,3},{8,12},{9,13},{10,... | collective-permute-start | bytes 147464 | tf_op jit(solution)/shard_map/ppermute | solution.py:130
  8.1 5.7 %collective-permute-start.3 = (bf16[32,768]{1,0:T(8,128)(2,1)S(1)}, bf16[32,768]{1,0:T(8,128)(2,1)S(1)}, u32[]{:S(2)}, u32[]{:S(2)}) collective-permute-start(bf16[32,768]{1,0:T(8,128)(2,1)S(1)} %get-tuple-element.14.refs_2_), channel_id=1, source_target_pairs={{0,4},{1,5},{2,6},{3,7},{4,0},{5,1},{6,2},{7,3},{8,12},{9,13},{10,... | collective-permute-start | bytes 147464 | tf_op jit(solution)/shard_map/ppermute | solution.py:130
  10.1 19.7 %copy-start = (bf16[1,768,768]{2,1,0:T(8,128)(2,1)S(1)}, bf16[1,768,768]{2,1,0:T(8,128)(2,1)}, u32[]{:S(2)}) copy-start(bf16[1,768,768]{2,1,0:T(8,128)(2,1)} %param.5) | copy-start | bytes 3538948
  10.1 7.4 %collective-permute-start.7 = (bf16[64,768]{1,0:T(8,128)(2,1)S(1)}, bf16[64,768]{1,0:T(8,128)(2,1)S(1)}, u32[]{:S(2)}, u32[]{:S(2)}) collective-permute-start(bf16[64,768]{1,0:T(8,128)(2,1)S(1)} %shard_map.62.refs_8_), channel_id=1, source_target_pairs={{0,3},{1,2},{2,1},{3,0},{4,7},{5,6},{6,5},{7,4},{8,11},{9,10},{10,... | collective-permute-start | bytes 294920 | tf_op jit(solution)/shard_map/ppermute | solution.py:130
  13.8 7.7 %collective-permute-start.8 = (bf16[64,768]{1,0:T(8,128)(2,1)S(1)}, bf16[64,768]{1,0:T(8,128)(2,1)S(1)}, u32[]{:S(2)}, u32[]{:S(2)}) collective-permute-start(bf16[64,768]{1,0:T(8,128)(2,1)S(1)} %shard_map.62.refs_8_), channel_id=1, source_target_pairs={{0,2},{1,3},{2,0},{3,1},{4,6},{5,7},{6,4},{7,5},{8,10},{9,11},{10,... | collective-permute-start | bytes 294920 | tf_op jit(solution)/shard_map/ppermute | solution.py:130
  13.8 7.7 %collective-permute-start.9 = (bf16[64,768]{1,0:T(8,128)(2,1)S(1)}, bf16[64,768]{1,0:T(8,128)(2,1)S(1)}, u32[]{:S(2)}, u32[]{:S(2)}) collective-permute-start(bf16[64,768]{1,0:T(8,128)(2,1)S(1)} %shard_map.62.refs_8_), channel_id=1, source_target_pairs={{0,1},{1,0},{2,3},{3,2},{4,5},{5,4},{6,7},{7,6},{8,9},{9,8},{10,11... | collective-permute-start | bytes 294920 | tf_op jit(solution)/shard_map/ppermute | solution.py:130
  17.5 8.3 %collective-permute-start.1 = (bf16[64,768]{1,0:T(8,128)(2,1)S(1)}, bf16[64,768]{1,0:T(8,128)(2,1)S(1)}, u32[]{:S(2)}, u32[]{:S(2)}) collective-permute-start(bf16[64,768]{1,0:T(8,128)(2,1)S(1)} %shard_map.60.refs_3_), channel_id=1, source_target_pairs={{0,16},{1,17},{2,18},{3,19},{4,20},{5,21},{6,22},{7,23},{8,24},{9,... | collective-permute-start | bytes 294920 | tf_op jit(solution)/shard_map/ppermute | solution.py:65
  22.3 5.1 %collective-permute-start.10 = (bf16[32,768]{1,0:T(8,128)(2,1)S(1)}, bf16[32,768]{1,0:T(8,128)(2,1)S(1)}, u32[]{:S(2)}, u32[]{:S(2)}) collective-permute-start(bf16[32,768]{1,0:T(8,128)(2,1)S(1)} %shard_map.63.refs_7_), channel_id=1, source_target_pairs={{0,24},{1,25},{2,26},{3,27},{4,28},{5,29},{6,30},{7,31},{8,16},{9,... | collective-permute-start | bytes 147464 | tf_op jit(solution)/shard_map/ppermute | solution.py:130
  25.1 4.1 %collective-permute-start.11 = (bf16[32,768]{1,0:T(8,128)(2,1)S(1)}, bf16[32,768]{1,0:T(8,128)(2,1)S(1)}, u32[]{:S(2)}, u32[]{:S(2)}) collective-permute-start(bf16[32,768]{1,0:T(8,128)(2,1)S(1)} %shard_map.63.refs_7_), channel_id=1, source_target_pairs={{0,8},{1,9},{2,10},{3,11},{4,12},{5,13},{6,14},{7,15},{8,0},{9,1},... | collective-permute-start | bytes 147464 | tf_op jit(solution)/shard_map/ppermute | solution.py:130
  25.7 4.1 %collective-permute-start.12 = (bf16[32,768]{1,0:T(8,128)(2,1)S(1)}, bf16[32,768]{1,0:T(8,128)(2,1)S(1)}, u32[]{:S(2)}, u32[]{:S(2)}) collective-permute-start(bf16[32,768]{1,0:T(8,128)(2,1)S(1)} %shard_map.63.refs_7_), channel_id=1, source_target_pairs={{0,16},{1,17},{2,18},{3,19},{4,20},{5,21},{6,22},{7,23},{8,24},{9,... | collective-permute-start | bytes 147464 | tf_op jit(solution)/shard_map/ppermute | solution.py:130
  30.6 4.7 %collective-permute-start.15 = (bf16[64,768]{1,0:T(8,128)(2,1)S(1)}, bf16[64,768]{1,0:T(8,128)(2,1)S(1)}, u32[]{:S(2)}, u32[]{:S(2)}) collective-permute-start(bf16[64,768]{1,0:T(8,128)(2,1)S(1)} %get-tuple-element.23), channel_id=1, source_target_pairs={{0,16},{1,17},{2,18},{3,19},{4,20},{5,21},{6,22},{7,23},{8,24},{9,... | collective-permute-start | bytes 294920 | tf_op jit(solution)/shard_map/ppermute | solution.py:130
  35.4 6.6 %collective-permute-start.16 = (bf16[64,768]{1,0:T(8,128)(2,1)S(1)}, bf16[64,768]{1,0:T(8,128)(2,1)S(1)}, u32[]{:S(2)}, u32[]{:S(2)}) collective-permute-start(bf16[64,768]{1,0:T(8,128)(2,1)S(1)} %shard_map.67.refs_8_), channel_id=1, source_target_pairs={{0,3},{1,2},{2,1},{3,0},{4,7},{5,6},{6,5},{7,4},{8,11},{9,10},{10,... | collective-permute-start | bytes 294920 | tf_op jit(solution)/shard_map/ppermute | solution.py:130
  37.9 6.6 %collective-permute-start.17 = (bf16[64,768]{1,0:T(8,128)(2,1)S(1)}, bf16[64,768]{1,0:T(8,128)(2,1)S(1)}, u32[]{:S(2)}, u32[]{:S(2)}) collective-permute-start(bf16[64,768]{1,0:T(8,128)(2,1)S(1)} %shard_map.67.refs_8_), channel_id=1, source_target_pairs={{0,2},{1,3},{2,0},{3,1},{4,6},{5,7},{6,4},{7,5},{8,10},{9,11},{10,... | collective-permute-start | bytes 294920 | tf_op jit(solution)/shard_map/ppermute | solution.py:130
  38.3 6.2 %collective-permute-start.18 = (bf16[64,768]{1,0:T(8,128)(2,1)S(1)}, bf16[64,768]{1,0:T(8,128)(2,1)S(1)}, u32[]{:S(2)}, u32[]{:S(2)}) collective-permute-start(bf16[64,768]{1,0:T(8,128)(2,1)S(1)} %shard_map.67.refs_8_), channel_id=1, source_target_pairs={{0,1},{1,0},{2,3},{3,2},{4,5},{5,4},{6,7},{7,6},{8,9},{9,8},{10,11... | collective-permute-start | bytes 294920 | tf_op jit(solution)/shard_map/ppermute | solution.py:130
  39.8 1.2 %collective-permute-start.14 = (bf16[32,768]{1,0:T(8,128)(2,1)S(1)}, bf16[32,768]{1,0:T(8,128)(2,1)S(1)}, u32[]{:S(2)}, u32[]{:S(2)}) collective-permute-start(bf16[32,768]{1,0:T(8,128)(2,1)S(1)} %get-tuple-element.21.refs_2_), channel_id=1, source_target_pairs={{0,4},{1,5},{2,6},{3,7},{4,0},{5,1},{6,2},{7,3},{8,12},{9,13},{10,... | collective-permute-start | bytes 147464 | tf_op jit(solution)/shard_map/ppermute | solution.py:130
  45.3 5.0 %collective-permute-start.19 = (bf16[32,768]{1,0:T(8,128)(2,1)S(1)}, bf16[32,768]{1,0:T(8,128)(2,1)S(1)}, u32[]{:S(2)}, u32[]{:S(2)}) collective-permute-start(bf16[32,768]{1,0:T(8,128)(2,1)S(1)} %shard_map.68.refs_4_), channel_id=1, source_target_pairs={{0,24},{1,25},{2,26},{3,27},{4,28},{5,29},{6,30},{7,31},{8,16},{9,... | collective-permute-start | bytes 147464 | tf_op jit(solution)/shard_map/ppermute | solution.py:130
  46.9 4.1 %collective-permute-start.20 = (bf16[32,768]{1,0:T(8,128)(2,1)S(1)}, bf16[32,768]{1,0:T(8,128)(2,1)S(1)}, u32[]{:S(2)}, u32[]{:S(2)}) collective-permute-start(bf16[32,768]{1,0:T(8,128)(2,1)S(1)} %shard_map.68.refs_4_), channel_id=1, source_target_pairs={{0,8},{1,9},{2,10},{3,11},{4,12},{5,13},{6,14},{7,15},{8,0},{9,1},... | collective-permute-start | bytes 147464 | tf_op jit(solution)/shard_map/ppermute | solution.py:130
  47.4 4.1 %collective-permute-start.21 = (bf16[32,768]{1,0:T(8,128)(2,1)S(1)}, bf16[32,768]{1,0:T(8,128)(2,1)S(1)}, u32[]{:S(2)}, u32[]{:S(2)}) collective-permute-start(bf16[32,768]{1,0:T(8,128)(2,1)S(1)} %shard_map.68.refs_4_), channel_id=1, source_target_pairs={{0,16},{1,17},{2,18},{3,19},{4,20},{5,21},{6,22},{7,23},{8,24},{9,... | collective-permute-start | bytes 147464 | tf_op jit(solution)/shard_map/ppermute | solution.py:130
  48.8 2.8 %collective-permute-start.13 = (bf16[64,768]{1,0:T(8,128)(2,1)S(1)}, bf16[64,768]{1,0:T(8,128)(2,1)S(1)}, u32[]{:S(2)}, u32[]{:S(2)}) collective-permute-start(bf16[64,768]{1,0:T(8,128)(2,1)S(1)} %get-tuple-element.19.refs_3_), channel_id=1, source_target_pairs={{0,4},{1,5},{2,6},{3,7},{4,0},{5,1},{6,2},{7,3},{8,12},{9,13},{10,... | collective-permute-start | bytes 294920 | tf_op jit(solution)/shard_map/ppermute | solution.py:130
  51.6 1.4 %collective-permute-start.22 = (bf16[64,768]{1,0:T(8,128)(2,1)S(1)}, bf16[64,768]{1,0:T(8,128)(2,1)S(1)}, u32[]{:S(2)}, u32[]{:S(2)}) collective-permute-start(bf16[64,768]{1,0:T(8,128)(2,1)S(1)} %shard_map.69.refs_1_), channel_id=1, source_target_pairs={{0,4},{1,5},{2,6},{3,7},{4,0},{5,1},{6,2},{7,3},{8,12},{9,13},{10,... | collective-permute-start | bytes 294920 | tf_op jit(solution)/shard_map/ppermute | solution.py:130

commit v5 on v4

--- a/solution.py
+++ b/solution.py
@@ -231,10 +231,9 @@
 
 
 def apply_body(near, nd, loose, info, *refs):
-    refs, (operand, value) = refs[loose:-2], refs[-2:]
-    refs, outs = refs[: -1 - nd], refs[-1 - nd :]
+    refs = refs[loose:]
+    refs, (current_ref, operand, *totals) = refs[: -1 - nd], refs[-1 - nd :]
     parts, past_ref, operators = refs[: -1 - near], refs[-1 - near], refs[-near:]
-    current_ref, totals = outs[0], outs[1:]
     rows = parts[0].shape[0]
     for kd in range(nd):
         current_ref[pl.ds(kd * rows, rows), :] = total_of(parts[kd::nd]).astype(BF16)
@@ -247,20 +246,28 @@
     def _():
         operand[...] = past_ref[...]
 
+    for kd, total in enumerate(totals, 1):
+        wanted = part_of(operand, info[0] ^ kd, rows)
+        for kn in range(near):
+            total[pl.ds(kn * rows, rows), :] = times_transposed(wanted, operators[kn][...]).astype(BF16)
+
+
+def own_body(near, loose, info, *refs):
+    operand, operators, total = refs[loose], refs[loose + 1 : -1], refs[-1]
+    rows = total.shape[0] // near
+    wanted = part_of(operand, info[0], rows)
     for kn in range(near):
-        value[...] = times_transposed(operand[...], operators[kn][...])
-        for kd in range(nd):
-            totals[kd][pl.ds(kn * rows, rows), :] = part_of(value, info[0] ^ kd, rows).astype(BF16)
+        total[pl.ds(kn * rows, rows), :] = times_transposed(wanted, operators[kn][...]).astype(BF16)
 
 
 def apply(lay, parts, past, operators):
     rows, columns = parts[0].shape
-    out = [jax.ShapeDtypeStruct((rows * lay.nd, columns), BF16)]
-    out += [jax.ShapeDtypeStruct((rows * lay.near, operators[0].shape[0]), BF16)] * lay.nd
+    total = jax.ShapeDtypeStruct((rows * lay.near, operators[0].shape[0]), BF16)
+    out = [jax.ShapeDtypeStruct((rows * lay.nd, columns), BF16)] * 2 + [total] * (lay.nd - 1)
     body = functools.partial(apply_body, lay.near, lay.nd)
-    scratch = [pltpu.VMEM(past.shape, BF16), pltpu.VMEM((rows * lay.nd, operators[0].shape[0]), F32)]
-    current, *totals = kernel_call(body, out, [lay.d], (*parts, past, *operators), (), scratch)
-    return current, totals
+    current, operand, *others = kernel_call(body, out, [lay.d], (*parts, past, *operators))
+    own = kernel_call(functools.partial(own_body, lay.near), total, [lay.d], (operand, *operators))
+    return current, [own, *others]
 
 
 def place(info, nd, blocks, total):
@@ -355,7 +362,7 @@
     direct = over_near(lay, operator)
     partial = invert(lay, along_col(lay, total), from_cores(lay, cuts), inverse)
     current, totals = apply(lay, over_rows(lay, partial), past, direct)
-    cuts = wave_cut(lay, excitation, 1, (totals[0],))
+    cuts = wave_cut(lay, excitation, 1, (totals[-1],))
     total = join(lay, [[lay.move(block, kd=kd) if kd else block for kd, block in enumerate(totals)]], cuts)
     turned = turn(lay, over_near(lay, current))
     partial = invert(lay, along_col(lay, total), from_cores(lay, cuts), inverse, ())

time: 54 us -> 53.9 us (level)
  waiting for transfers between devices: 23.8 us -> 23 us
  Pallas kernels: 4.07 us -> 4.77 us
    ppermute x22, waiting for transfers between devices: 23.8 us -> 23 us  [move(): return lax.ppermute(block, ('delay', 'row', 'col'), pairs)]
    pallas_call x11 -> x12, Pallas kernels: 3.14 us -> 3.84 us  [kernel_call(): pl.pallas_call(functools.partial(farthest_first, body, len(info), len(loo...]
  transfers between devices with their start and end apart: 23 -> 23, of which waited for: 15 -> 15; matrix products, arithmetic and copies ran while one was open for 4% -> 4% of each run, Pallas kernels for 3% -> 4%
where the time goes in v5:
time: 53.9 us; the launch traced here: 53.8 us
  starting transfers between devices  23.2 us (43%)
  waiting for transfers between devices  23 us (43%)
  Pallas kernels  4.77 us (9%)
  matrix products  1.98 us (4%)
  between operations  0.77 us (1%)
    ppermute x22, waiting for transfers between devices, move(): return lax.ppermute(block, ('delay', 'row', 'col'), pairs)  23 us
    ppermute x22, starting transfers between devices, move(): return lax.ppermute(block, ('delay', 'row', 'col'), pairs)  20 us
    pallas_call x12, Pallas kernels, kernel_call(): pl.pallas_call(functools.partial(farthest_first, body, len(info), len(loo...  3.84 us
    ppermute x1, starting transfers between devices, from_behind(): return lax.ppermute(block, axis, route) if route else jnp.zeros_like(block)  3.21 us
    dot_general x1, matrix products, begin(): lax.dot_general(past, operator, (((0,), (1,)), ((), ())), preferred_eleme...  1.98 us
  transfers between devices with their start and end apart: 23, of which 15 were waited for; matrix products, arithmetic and copies ran while one was open for 4% of the time, Pallas kernels for 4%

profile of v5, /device:TPU:0, one launch (start us, length us, event | category | flops | bytes accessed | tf_op | source)
XLA Modules:
  0.0 53.8 jit_solution(10234872617217386168)
XLA Ops:
  0.6 0.5 collective-permute-start.2
  1.2 0.1 collective-permute-start
  1.2 2.0 %convolution_convert_fusion.refs_2_ = bf16[128,768]{1,0:T(8,128)(2,1)S(1)} fusion(bf16[1,768,128]{2,1,0:T(8,128)(2,1)} %param.7, bf16[1,768,768]{2,1,0:T(8,128)(2,1)} %param.5), kind=kOutput, calls=%fused_computation | convolution fusion | flops 151093248 | bytes 1572864 | tf_op jit(solution)/shard_map/dot_general | solution.py:169
  3.3 2.7 %collective-permute-start.4 = (bf16[32,768]{1,0:T(8,128)(2,1)S(1)}, bf16[32,768]{1,0:T(8,128)(2,1)S(1)}, u32[]{:S(2)}, u32[]{:S(2)}) collective-permute-start(bf16[32,768]{1,0:T(8,128)(2,1)S(1)} %get-tuple-element.16), channel_id=1, source_target_pairs={{0,20},{1,21},{2,22},{3,23},{4,16},{5,17},{6,18},{7,19},{8,28},{9,... | collective-permute-start | bytes 147464 | tf_op jit(solution)/shard_map/ppermute | solution.py:130
  6.0 0.4 collective-permute-start.5
  6.4 0.0 collective-permute-start.6
  6.4 0.1 shard_map.61
  6.6 0.1 shard_map.60.refs_3_
  6.7 1.4 %collective-permute-done.4.refs_4_ = bf16[32,768]{1,0:T(8,128)(2,1)S(1)} collective-permute-done((bf16[32,768]{1,0:T(8,128)(2,1)S(1)}, bf16[32,768]{1,0:T(8,128)(2,1)S(1)}, u32[]{:S(2)}, u32[]{:S(2)}) %collective-permute-start.4) | collective-permute-done | bytes 49184 | tf_op jit(solution)/shard_map/ppermute | solution.py:130
  8.1 0.1 collective-permute-start.3
  8.2 1.9 %collective-permute-done.5.refs_5_ = bf16[32,768]{1,0:T(8,128)(2,1)S(1)} collective-permute-done((bf16[32,768]{1,0:T(8,128)(2,1)S(1)}, bf16[32,768]{1,0:T(8,128)(2,1)S(1)}, u32[]{:S(2)}, u32[]{:S(2)}) %collective-permute-start.5) | collective-permute-done | bytes 49184 | tf_op jit(solution)/shard_map/ppermute | solution.py:130
  10.1 0.0 collective-permute-done.6.refs_6_
  10.1 0.0 copy-start
  10.1 3.7 %collective-permute-start.7 = (bf16[64,768]{1,0:T(8,128)(2,1)S(1)}, bf16[64,768]{1,0:T(8,128)(2,1)S(1)}, u32[]{:S(2)}, u32[]{:S(2)}) collective-permute-start(bf16[64,768]{1,0:T(8,128)(2,1)S(1)} %shard_map.62.refs_8_), channel_id=1, source_target_pairs={{0,3},{1,2},{2,1},{3,0},{4,7},{5,6},{6,5},{7,4},{8,11},{9,10},{10,... | collective-permute-start | bytes 294920 | tf_op jit(solution)/shard_map/ppermute | solution.py:130
  13.8 0.8 %collective-permute-start.9 = (bf16[64,768]{1,0:T(8,128)(2,1)S(1)}, bf16[64,768]{1,0:T(8,128)(2,1)S(1)}, u32[]{:S(2)}, u32[]{:S(2)}) collective-permute-start(bf16[64,768]{1,0:T(8,128)(2,1)S(1)} %shard_map.62.refs_8_), channel_id=1, source_target_pairs={{0,1},{1,0},{2,3},{3,2},{4,5},{5,4},{6,7},{7,6},{8,9},{9,8},{10,11... | collective-permute-start | bytes 294920 | tf_op jit(solution)/shard_map/ppermute | solution.py:130
  14.6 2.9 %collective-permute-done.7.refs_5_ = bf16[64,768]{1,0:T(8,128)(2,1)S(1)} collective-permute-done((bf16[64,768]{1,0:T(8,128)(2,1)S(1)}, bf16[64,768]{1,0:T(8,128)(2,1)S(1)}, u32[]{:S(2)}, u32[]{:S(2)}) %collective-permute-start.7) | collective-permute-done | bytes 98336 | tf_op jit(solution)/shard_map/ppermute | solution.py:130
  17.5 3.2 %collective-permute-start.1 = (bf16[64,768]{1,0:T(8,128)(2,1)S(1)}, bf16[64,768]{1,0:T(8,128)(2,1)S(1)}, u32[]{:S(2)}, u32[]{:S(2)}) collective-permute-start(bf16[64,768]{1,0:T(8,128)(2,1)S(1)} %shard_map.60.refs_3_), channel_id=1, source_target_pairs={{0,16},{1,17},{2,18},{3,19},{4,20},{5,21},{6,22},{7,23},{8,24},{9,... | collective-permute-start | bytes 294920 | tf_op jit(solution)/shard_map/ppermute | solution.py:65
  20.7 0.8 %collective-permute-done.8.refs_6_ = bf16[64,768]{1,0:T(8,128)(2,1)S(1)} collective-permute-done((bf16[64,768]{1,0:T(8,128)(2,1)S(1)}, bf16[64,768]{1,0:T(8,128)(2,1)S(1)}, u32[]{:S(2)}, u32[]{:S(2)}) %collective-permute-start.8) | collective-permute-done | bytes 98336 | tf_op jit(solution)/shard_map/ppermute | solution.py:130
  21.5 0.0 collective-permute-done.9.refs_7_
  21.5 0.8 %shard_map.63.refs_7_ = bf16[32,768]{1,0:T(8,128)(2,1)S(1)} custom-call(s32[1]{0:T(128)} %bitcast.refs_0_.d_ref, bf16[768,768]{1,0:T(8,128)(2,1)S(1)} %collective-permute-done.2.refs_1_, bf16[768,768]{1,0:T(8,128)(2,1)S(1)} %copy-done.1, bf16[32,768]{1,0:T(8,128)(2,1)S(1)} %collective-permute-done.3.refs_3_, ...), custom_call_target="tpu_custom_call" | custom-call | tf_op jit(solution)/shard_map/pallas_call | solution.py:141
  22.3 2.9 %collective-permute-start.10 = (bf16[32,768]{1,0:T(8,128)(2,1)S(1)}, bf16[32,768]{1,0:T(8,128)(2,1)S(1)}, u32[]{:S(2)}, u32[]{:S(2)}) collective-permute-start(bf16[32,768]{1,0:T(8,128)(2,1)S(1)} %shard_map.63.refs_7_), channel_id=1, source_target_pairs={{0,24},{1,25},{2,26},{3,27},{4,28},{5,29},{6,30},{7,31},{8,16},{9,... | collective-permute-start | bytes 147464 | tf_op jit(solution)/shard_map/ppermute | solution.py:130
  25.1 0.5 collective-permute-start.11
  25.7 0.1 collective-permute-start.12
  25.8 1.5 %collective-permute-done.10.refs_4_ = bf16[32,768]{1,0:T(8,128)(2,1)S(1)} collective-permute-done((bf16[32,768]{1,0:T(8,128)(2,1)S(1)}, bf16[32,768]{1,0:T(8,128)(2,1)S(1)}, u32[]{:S(2)}, u32[]{:S(2)}) %collective-permute-start.10) | collective-permute-done | bytes 49184 | tf_op jit(solution)/shard_map/ppermute | solution.py:130
  27.3 1.9 %collective-permute-done.11.refs_5_ = bf16[32,768]{1,0:T(8,128)(2,1)S(1)} collective-permute-done((bf16[32,768]{1,0:T(8,128)(2,1)S(1)}, bf16[32,768]{1,0:T(8,128)(2,1)S(1)}, u32[]{:S(2)}, u32[]{:S(2)}) %collective-permute-start.11) | collective-permute-done | bytes 49184 | tf_op jit(solution)/shard_map/ppermute | solution.py:130
  29.2 0.5 collective-permute-done.12.refs_6_
  29.8 0.8 %shard_map.64 = (bf16[64,768]{1,0:T(8,128)(2,1)S(1)}, bf16[64,768]{1,0:T(8,128)(2,1)S(1)}, bf16[64,768]{1,0:T(8,128)(2,1)S(1)}) custom-call(s32[1]{0:T(128)} %bitcast.refs_0_.d_ref, bf16[768,768]{1,0:T(8,128)(2,1)S(1)} %collective-permute-done.refs_1_, bf16[768,768]{1,0:T(8,128)(2,1)S(1)} %bitcast.9, bf16[64,768]{1,0:T(8,128)(2,1)S(1)} %collective-permute-done.1.refs_3_, ...), custom_call_target="tpu_custom_call" | custom-call | tf_op jit(solution)/shard_map/pallas_call | solution.py:141
  30.6 0.2 collective-permute-start.15
  30.7 0.1 shard_map.66
  30.9 0.8 %shard_map.67.refs_4_ = bf16[64,768]{1,0:T(8,128)(2,1)S(1)} custom-call(s32[1]{0:T(128)} %bitcast.refs_0_.d_ref, bf16[768,768]{1,0:T(8,128)(2,1)S(1)} %collective-permute-done.refs_1_, bf16[768,768]{1,0:T(8,128)(2,1)S(1)} %bitcast.10, bf16[64,768]{1,0:T(8,128)(2,1)S(1)} %get-tuple-element.23.refs_3_), custom_call_target="tpu_custom_call" | custom-call | tf_op jit(solution)/shard_map/pallas_call | solution.py:141
  31.7 3.6 %collective-permute-done.15.refs_3_ = bf16[64,768]{1,0:T(8,128)(2,1)S(1)} collective-permute-done((bf16[64,768]{1,0:T(8,128)(2,1)S(1)}, bf16[64,768]{1,0:T(8,128)(2,1)S(1)}, u32[]{:S(2)}, u32[]{:S(2)}) %collective-permute-start.15) | collective-permute-done | bytes 98336 | tf_op jit(solution)/shard_map/ppermute | solution.py:130
  35.2 2.6 %collective-permute-start.16 = (bf16[64,768]{1,0:T(8,128)(2,1)S(1)}, bf16[64,768]{1,0:T(8,128)(2,1)S(1)}, u32[]{:S(2)}, u32[]{:S(2)}) collective-permute-start(bf16[64,768]{1,0:T(8,128)(2,1)S(1)} %shard_map.68.refs_8_), channel_id=1, source_target_pairs={{0,3},{1,2},{2,1},{3,0},{4,7},{5,6},{6,5},{7,4},{8,11},{9,10},{10,... | collective-permute-start | bytes 294920 | tf_op jit(solution)/shard_map/ppermute | solution.py:130
  37.8 0.4 collective-permute-start.17
  38.2 1.5 %collective-permute-start.18 = (bf16[64,768]{1,0:T(8,128)(2,1)S(1)}, bf16[64,768]{1,0:T(8,128)(2,1)S(1)}, u32[]{:S(2)}, u32[]{:S(2)}) collective-permute-start(bf16[64,768]{1,0:T(8,128)(2,1)S(1)} %shard_map.68.refs_8_), channel_id=1, source_target_pairs={{0,1},{1,0},{2,3},{3,2},{4,5},{5,4},{6,7},{7,6},{8,9},{9,8},{10,11... | collective-permute-start | bytes 294920 | tf_op jit(solution)/shard_map/ppermute | solution.py:130
  39.7 1.2 %collective-permute-done.14.refs_3_ = bf16[32,768]{1,0:T(8,128)(2,1)S(1)} collective-permute-done((bf16[32,768]{1,0:T(8,128)(2,1)S(1)}, bf16[32,768]{1,0:T(8,128)(2,1)S(1)}, u32[]{:S(2)}, u32[]{:S(2)}) %collective-permute-start.14) | collective-permute-done | bytes 49184 | tf_op jit(solution)/shard_map/ppermute | solution.py:130
  40.9 0.9 %collective-permute-done.16.refs_5_ = bf16[64,768]{1,0:T(8,128)(2,1)S(1)} collective-permute-done((bf16[64,768]{1,0:T(8,128)(2,1)S(1)}, bf16[64,768]{1,0:T(8,128)(2,1)S(1)}, u32[]{:S(2)}, u32[]{:S(2)}) %collective-permute-start.16) | collective-permute-done | bytes 98336 | tf_op jit(solution)/shard_map/ppermute | solution.py:130
  41.8 2.6 %collective-permute-done.17.refs_6_ = bf16[64,768]{1,0:T(8,128)(2,1)S(1)} collective-permute-done((bf16[64,768]{1,0:T(8,128)(2,1)S(1)}, bf16[64,768]{1,0:T(8,128)(2,1)S(1)}, u32[]{:S(2)}, u32[]{:S(2)}) %collective-permute-start.17) | collective-permute-done | bytes 98336 | tf_op jit(solution)/shard_map/ppermute | solution.py:130
  44.4 0.8 %shard_map.69.refs_4_ = bf16[32,768]{1,0:T(8,128)(2,1)S(1)} custom-call(s32[1]{0:T(128)} %bitcast.refs_0_.d_ref, bf16[768,768]{1,0:T(8,128)(2,1)S(1)} %collective-permute-done.2.refs_1_, bf16[768,768]{1,0:T(8,128)(2,1)S(1)} %copy-done.1, bf16[32,768]{1,0:T(8,128)(2,1)S(1)} %collective-permute-done.14.refs_3_, ...), custom_call_target="tpu_custom_call" | custom-call | tf_op jit(solution)/shard_map/pallas_call | solution.py:141
  45.2 1.6 %collective-permute-start.19 = (bf16[32,768]{1,0:T(8,128)(2,1)S(1)}, bf16[32,768]{1,0:T(8,128)(2,1)S(1)}, u32[]{:S(2)}, u32[]{:S(2)}) collective-permute-start(bf16[32,768]{1,0:T(8,128)(2,1)S(1)} %shard_map.69.refs_4_), channel_id=1, source_target_pairs={{0,24},{1,25},{2,26},{3,27},{4,28},{5,29},{6,30},{7,31},{8,16},{9,... | collective-permute-start | bytes 147464 | tf_op jit(solution)/shard_map/ppermute | solution.py:130
  46.8 0.5 collective-permute-start.20
  47.3 1.3 %collective-permute-start.21 = (bf16[32,768]{1,0:T(8,128)(2,1)S(1)}, bf16[32,768]{1,0:T(8,128)(2,1)S(1)}, u32[]{:S(2)}, u32[]{:S(2)}) collective-permute-start(bf16[32,768]{1,0:T(8,128)(2,1)S(1)} %shard_map.69.refs_4_), channel_id=1, source_target_pairs={{0,16},{1,17},{2,18},{3,19},{4,20},{5,21},{6,22},{7,23},{8,24},{9,... | collective-permute-start | bytes 147464 | tf_op jit(solution)/shard_map/ppermute | solution.py:130
  48.7 1.5 %collective-permute-done.19.refs_1_ = bf16[32,768]{1,0:T(8,128)(2,1)S(1)} collective-permute-done((bf16[32,768]{1,0:T(8,128)(2,1)S(1)}, bf16[32,768]{1,0:T(8,128)(2,1)S(1)}, u32[]{:S(2)}, u32[]{:S(2)}) %collective-permute-start.19) | collective-permute-done | bytes 49184 | tf_op jit(solution)/shard_map/ppermute | solution.py:130
  50.2 0.7 %collective-permute-done.20.refs_2_ = bf16[32,768]{1,0:T(8,128)(2,1)S(1)} collective-permute-done((bf16[32,768]{1,0:T(8,128)(2,1)S(1)}, bf16[32,768]{1,0:T(8,128)(2,1)S(1)}, u32[]{:S(2)}, u32[]{:S(2)}) %collective-permute-start.20) | collective-permute-done | bytes 49184 | tf_op jit(solution)/shard_map/ppermute | solution.py:130
  50.9 0.5 collective-permute-done.21.refs_3_
  51.5 0.1 collective-permute-start.22
  51.6 0.2 shard_map.65.refs_0_
  51.7 1.1 %collective-permute-done.22.refs_2_ = bf16[64,768]{1,0:T(8,128)(2,1)S(1)} collective-permute-done((bf16[64,768]{1,0:T(8,128)(2,1)S(1)}, bf16[64,768]{1,0:T(8,128)(2,1)S(1)}, u32[]{:S(2)}, u32[]{:S(2)}) %collective-permute-start.22) | collective-permute-done | bytes 98336 | tf_op jit(solution)/shard_map/ppermute | solution.py:130
  52.8 0.9 %shard_map.71 = (bf16[2,768,128]{2,1,0:T(8,128)(2,1)}, bf16[1,768,128]{2,1,0:T(8,128)(2,1)}) custom-call(s32[1]{0:T(128)} %bitcast.refs_0_.d_ref, s32[1]{0:T(128)} %bitcast.1.refs_1_.refs_0_.n_ref, bf16[768,128]{1,0:T(8,128)(2,1)S(1)} %shard_map.65.refs_0_, bf16[64,768]{1,0:T(8,128)(2,1)S(1)} %shard_map.70.refs_1_, ...), custom_call_target="tpu_custom_call" | custom-call | tf_op jit(solution)/shard_map/pallas_call | solution.py:320
  (20 shorter events, 0.1 us)
Async XLA Ops:
  0.6 5.9 %copy-start.3 = (bf16[1,768,128]{2,1,0:T(8,128)(2,1)S(1)}, bf16[1,768,128]{2,1,0:T(8,128)(2,1)}, u32[]{:S(2)}) copy-start(bf16[1,768,128]{2,1,0:T(8,128)(2,1)} %param.7) | copy-start | bytes 589828
  0.6 5.8 %copy-start.2 = (bf16[2,768,128]{2,1,0:T(8,128)(2,1)S(1)}, bf16[2,768,128]{2,1,0:T(8,128)(2,1)}, u32[]{:S(2)}) copy-start(bf16[2,768,128]{2,1,0:T(8,128)(2,1)} %refs_3_.3) | copy-start | bytes 1179652
  0.6 20.8 %collective-permute-start.2 = (bf16[768,768]{1,0:T(8,128)(2,1)}, bf16[768,768]{1,0:T(8,128)(2,1)S(1)}, u32[]{:S(2)}, u32[]{:S(2)}) collective-permute-start(bf16[768,768]{1,0:T(8,128)(2,1)} %refs_2_.3), channel_id=1, source_target_pairs={{0,4},{1,5},{2,6},{3,7},{4,0},{5,1},{6,2},{7,3},{8,12},{9,13},{10,... | collective-permute-start | bytes 3538952 | tf_op jit(solution)/shard_map/ppermute | solution.py:130
  1.2 24.6 %collective-permute-start = (bf16[768,768]{1,0:T(8,128)(2,1)}, bf16[768,768]{1,0:T(8,128)(2,1)S(1)}, u32[]{:S(2)}, u32[]{:S(2)}) collective-permute-start(bf16[768,768]{1,0:T(8,128)(2,1)} %bitcast.8), channel_id=1, source_target_pairs={{0,4},{1,5},{2,6},{3,7},{4,0},{5,1},{6,2},{7,3},{8,12},{9,13},{10,... | collective-permute-start | bytes 3538952 | tf_op jit(solution)/shard_map/ppermute | solution.py:130
  1.2 20.2 %copy-start.1 = (bf16[768,768]{1,0:T(8,128)(2,1)S(1)}, bf16[768,768]{1,0:T(8,128)(2,1)}, u32[]{:S(2)}) copy-start(bf16[768,768]{1,0:T(8,128)(2,1)} %refs_2_.3) | copy-start | bytes 3538948
  3.3 4.8 %collective-permute-start.4 = (bf16[32,768]{1,0:T(8,128)(2,1)S(1)}, bf16[32,768]{1,0:T(8,128)(2,1)S(1)}, u32[]{:S(2)}, u32[]{:S(2)}) collective-permute-start(bf16[32,768]{1,0:T(8,128)(2,1)S(1)} %get-tuple-element.16), channel_id=1, source_target_pairs={{0,20},{1,21},{2,22},{3,23},{4,16},{5,17},{6,18},{7,19},{8,28},{9,... | collective-permute-start | bytes 147464 | tf_op jit(solution)/shard_map/ppermute | solution.py:130
  6.0 4.1 %collective-permute-start.5 = (bf16[32,768]{1,0:T(8,128)(2,1)S(1)}, bf16[32,768]{1,0:T(8,128)(2,1)S(1)}, u32[]{:S(2)}, u32[]{:S(2)}) collective-permute-start(bf16[32,768]{1,0:T(8,128)(2,1)S(1)} %get-tuple-element.17), channel_id=1, source_target_pairs={{0,16},{1,17},{2,18},{3,19},{4,20},{5,21},{6,22},{7,23},{8,24},{9,... | collective-permute-start | bytes 147464 | tf_op jit(solution)/shard_map/ppermute | solution.py:130
  6.4 3.7 %collective-permute-start.6 = (bf16[32,768]{1,0:T(8,128)(2,1)S(1)}, bf16[32,768]{1,0:T(8,128)(2,1)S(1)}, u32[]{:S(2)}, u32[]{:S(2)}) collective-permute-start(bf16[32,768]{1,0:T(8,128)(2,1)S(1)} %get-tuple-element.18), channel_id=1, source_target_pairs={{0,4},{1,5},{2,6},{3,7},{4,0},{5,1},{6,2},{7,3},{8,12},{9,13},{10,... | collective-permute-start | bytes 147464 | tf_op jit(solution)/shard_map/ppermute | solution.py:130
  8.1 5.7 %collective-permute-start.3 = (bf16[32,768]{1,0:T(8,128)(2,1)S(1)}, bf16[32,768]{1,0:T(8,128)(2,1)S(1)}, u32[]{:S(2)}, u32[]{:S(2)}) collective-permute-start(bf16[32,768]{1,0:T(8,128)(2,1)S(1)} %get-tuple-element.14.refs_2_), channel_id=1, source_target_pairs={{0,4},{1,5},{2,6},{3,7},{4,0},{5,1},{6,2},{7,3},{8,12},{9,13},{10,... | collective-permute-start | bytes 147464 | tf_op jit(solution)/shard_map/ppermute | solution.py:130
  10.1 19.7 %copy-start = (bf16[1,768,768]{2,1,0:T(8,128)(2,1)S(1)}, bf16[1,768,768]{2,1,0:T(8,128)(2,1)}, u32[]{:S(2)}) copy-start(bf16[1,768,768]{2,1,0:T(8,128)(2,1)} %param.5) | copy-start | bytes 3538948
  10.1 7.4 %collective-permute-start.7 = (bf16[64,768]{1,0:T(8,128)(2,1)S(1)}, bf16[64,768]{1,0:T(8,128)(2,1)S(1)}, u32[]{:S(2)}, u32[]{:S(2)}) collective-permute-start(bf16[64,768]{1,0:T(8,128)(2,1)S(1)} %shard_map.62.refs_8_), channel_id=1, source_target_pairs={{0,3},{1,2},{2,1},{3,0},{4,7},{5,6},{6,5},{7,4},{8,11},{9,10},{10,... | collective-permute-start | bytes 294920 | tf_op jit(solution)/shard_map/ppermute | solution.py:130
  13.8 7.7 %collective-permute-start.8 = (bf16[64,768]{1,0:T(8,128)(2,1)S(1)}, bf16[64,768]{1,0:T(8,128)(2,1)S(1)}, u32[]{:S(2)}, u32[]{:S(2)}) collective-permute-start(bf16[64,768]{1,0:T(8,128)(2,1)S(1)} %shard_map.62.refs_8_), channel_id=1, source_target_pairs={{0,2},{1,3},{2,0},{3,1},{4,6},{5,7},{6,4},{7,5},{8,10},{9,11},{10,... | collective-permute-start | bytes 294920 | tf_op jit(solution)/shard_map/ppermute | solution.py:130
  13.8 7.7 %collective-permute-start.9 = (bf16[64,768]{1,0:T(8,128)(2,1)S(1)}, bf16[64,768]{1,0:T(8,128)(2,1)S(1)}, u32[]{:S(2)}, u32[]{:S(2)}) collective-permute-start(bf16[64,768]{1,0:T(8,128)(2,1)S(1)} %shard_map.62.refs_8_), channel_id=1, source_target_pairs={{0,1},{1,0},{2,3},{3,2},{4,5},{5,4},{6,7},{7,6},{8,9},{9,8},{10,11... | collective-permute-start | bytes 294920 | tf_op jit(solution)/shard_map/ppermute | solution.py:130
  17.5 8.3 %collective-permute-start.1 = (bf16[64,768]{1,0:T(8,128)(2,1)S(1)}, bf16[64,768]{1,0:T(8,128)(2,1)S(1)}, u32[]{:S(2)}, u32[]{:S(2)}) collective-permute-start(bf16[64,768]{1,0:T(8,128)(2,1)S(1)} %shard_map.60.refs_3_), channel_id=1, source_target_pairs={{0,16},{1,17},{2,18},{3,19},{4,20},{5,21},{6,22},{7,23},{8,24},{9,... | collective-permute-start | bytes 294920 | tf_op jit(solution)/shard_map/ppermute | solution.py:65
  22.3 5.1 %collective-permute-start.10 = (bf16[32,768]{1,0:T(8,128)(2,1)S(1)}, bf16[32,768]{1,0:T(8,128)(2,1)S(1)}, u32[]{:S(2)}, u32[]{:S(2)}) collective-permute-start(bf16[32,768]{1,0:T(8,128)(2,1)S(1)} %shard_map.63.refs_7_), channel_id=1, source_target_pairs={{0,24},{1,25},{2,26},{3,27},{4,28},{5,29},{6,30},{7,31},{8,16},{9,... | collective-permute-start | bytes 147464 | tf_op jit(solution)/shard_map/ppermute | solution.py:130
  25.1 4.1 %collective-permute-start.11 = (bf16[32,768]{1,0:T(8,128)(2,1)S(1)}, bf16[32,768]{1,0:T(8,128)(2,1)S(1)}, u32[]{:S(2)}, u32[]{:S(2)}) collective-permute-start(bf16[32,768]{1,0:T(8,128)(2,1)S(1)} %shard_map.63.refs_7_), channel_id=1, source_target_pairs={{0,8},{1,9},{2,10},{3,11},{4,12},{5,13},{6,14},{7,15},{8,0},{9,1},... | collective-permute-start | bytes 147464 | tf_op jit(solution)/shard_map/ppermute | solution.py:130
  25.7 4.1 %collective-permute-start.12 = (bf16[32,768]{1,0:T(8,128)(2,1)S(1)}, bf16[32,768]{1,0:T(8,128)(2,1)S(1)}, u32[]{:S(2)}, u32[]{:S(2)}) collective-permute-start(bf16[32,768]{1,0:T(8,128)(2,1)S(1)} %shard_map.63.refs_7_), channel_id=1, source_target_pairs={{0,16},{1,17},{2,18},{3,19},{4,20},{5,21},{6,22},{7,23},{8,24},{9,... | collective-permute-start | bytes 147464 | tf_op jit(solution)/shard_map/ppermute | solution.py:130
  30.6 4.7 %collective-permute-start.15 = (bf16[64,768]{1,0:T(8,128)(2,1)S(1)}, bf16[64,768]{1,0:T(8,128)(2,1)S(1)}, u32[]{:S(2)}, u32[]{:S(2)}) collective-permute-start(bf16[64,768]{1,0:T(8,128)(2,1)S(1)} %get-tuple-element.20.refs_2_), channel_id=1, source_target_pairs={{0,16},{1,17},{2,18},{3,19},{4,20},{5,21},{6,22},{7,23},{8,24},{9,... | collective-permute-start | bytes 294920 | tf_op jit(solution)/shard_map/ppermute | solution.py:130
  35.2 6.6 %collective-permute-start.16 = (bf16[64,768]{1,0:T(8,128)(2,1)S(1)}, bf16[64,768]{1,0:T(8,128)(2,1)S(1)}, u32[]{:S(2)}, u32[]{:S(2)}) collective-permute-start(bf16[64,768]{1,0:T(8,128)(2,1)S(1)} %shard_map.68.refs_8_), channel_id=1, source_target_pairs={{0,3},{1,2},{2,1},{3,0},{4,7},{5,6},{6,5},{7,4},{8,11},{9,10},{10,... | collective-permute-start | bytes 294920 | tf_op jit(solution)/shard_map/ppermute | solution.py:130
  37.8 6.6 %collective-permute-start.17 = (bf16[64,768]{1,0:T(8,128)(2,1)S(1)}, bf16[64,768]{1,0:T(8,128)(2,1)S(1)}, u32[]{:S(2)}, u32[]{:S(2)}) collective-permute-start(bf16[64,768]{1,0:T(8,128)(2,1)S(1)} %shard_map.68.refs_8_), channel_id=1, source_target_pairs={{0,2},{1,3},{2,0},{3,1},{4,6},{5,7},{6,4},{7,5},{8,10},{9,11},{10,... | collective-permute-start | bytes 294920 | tf_op jit(solution)/shard_map/ppermute | solution.py:130
  38.2 6.2 %collective-permute-start.18 = (bf16[64,768]{1,0:T(8,128)(2,1)S(1)}, bf16[64,768]{1,0:T(8,128)(2,1)S(1)}, u32[]{:S(2)}, u32[]{:S(2)}) collective-permute-start(bf16[64,768]{1,0:T(8,128)(2,1)S(1)} %shard_map.68.refs_8_), channel_id=1, source_target_pairs={{0,1},{1,0},{2,3},{3,2},{4,5},{5,4},{6,7},{7,6},{8,9},{9,8},{10,11... | collective-permute-start | bytes 294920 | tf_op jit(solution)/shard_map/ppermute | solution.py:130
  39.7 1.2 %collective-permute-start.14 = (bf16[32,768]{1,0:T(8,128)(2,1)S(1)}, bf16[32,768]{1,0:T(8,128)(2,1)S(1)}, u32[]{:S(2)}, u32[]{:S(2)}) collective-permute-start(bf16[32,768]{1,0:T(8,128)(2,1)S(1)} %get-tuple-element.21.refs_2_), channel_id=1, source_target_pairs={{0,4},{1,5},{2,6},{3,7},{4,0},{5,1},{6,2},{7,3},{8,12},{9,13},{10,... | collective-permute-start | bytes 147464 | tf_op jit(solution)/shard_map/ppermute | solution.py:130
  45.2 5.0 %collective-permute-start.19 = (bf16[32,768]{1,0:T(8,128)(2,1)S(1)}, bf16[32,768]{1,0:T(8,128)(2,1)S(1)}, u32[]{:S(2)}, u32[]{:S(2)}) collective-permute-start(bf16[32,768]{1,0:T(8,128)(2,1)S(1)} %shard_map.69.refs_4_), channel_id=1, source_target_pairs={{0,24},{1,25},{2,26},{3,27},{4,28},{5,29},{6,30},{7,31},{8,16},{9,... | collective-permute-start | bytes 147464 | tf_op jit(solution)/shard_map/ppermute | solution.py:130
  46.8 4.1 %collective-permute-start.20 = (bf16[32,768]{1,0:T(8,128)(2,1)S(1)}, bf16[32,768]{1,0:T(8,128)(2,1)S(1)}, u32[]{:S(2)}, u32[]{:S(2)}) collective-permute-start(bf16[32,768]{1,0:T(8,128)(2,1)S(1)} %shard_map.69.refs_4_), channel_id=1, source_target_pairs={{0,8},{1,9},{2,10},{3,11},{4,12},{5,13},{6,14},{7,15},{8,0},{9,1},... | collective-permute-start | bytes 147464 | tf_op jit(solution)/shard_map/ppermute | solution.py:130
  47.3 4.1 %collective-permute-start.21 = (bf16[32,768]{1,0:T(8,128)(2,1)S(1)}, bf16[32,768]{1,0:T(8,128)(2,1)S(1)}, u32[]{:S(2)}, u32[]{:S(2)}) collective-permute-start(bf16[32,768]{1,0:T(8,128)(2,1)S(1)} %shard_map.69.refs_4_), channel_id=1, source_target_pairs={{0,16},{1,17},{2,18},{3,19},{4,20},{5,21},{6,22},{7,23},{8,24},{9,... | collective-permute-start | bytes 147464 | tf_op jit(solution)/shard_map/ppermute | solution.py:130
  48.7 2.9 %collective-permute-start.13 = (bf16[64,768]{1,0:T(8,128)(2,1)S(1)}, bf16[64,768]{1,0:T(8,128)(2,1)S(1)}, u32[]{:S(2)}, u32[]{:S(2)}) collective-permute-start(bf16[64,768]{1,0:T(8,128)(2,1)S(1)} %get-tuple-element.19.refs_3_), channel_id=1, source_target_pairs={{0,4},{1,5},{2,6},{3,7},{4,0},{5,1},{6,2},{7,3},{8,12},{9,13},{10,... | collective-permute-start | bytes 294920 | tf_op jit(solution)/shard_map/ppermute | solution.py:130
  51.5 1.4 %collective-permute-start.22 = (bf16[64,768]{1,0:T(8,128)(2,1)S(1)}, bf16[64,768]{1,0:T(8,128)(2,1)S(1)}, u32[]{:S(2)}, u32[]{:S(2)}) collective-permute-start(bf16[64,768]{1,0:T(8,128)(2,1)S(1)} %shard_map.70.refs_1_), channel_id=1, source_target_pairs={{0,4},{1,5},{2,6},{3,7},{4,0},{5,1},{6,2},{7,3},{8,12},{9,13},{10,... | collective-permute-start | bytes 294920 | tf_op jit(solution)/shard_map/ppermute | solution.py:130

commit v6 on v5

--- a/solution.py
+++ b/solution.py
@@ -144,6 +144,7 @@
         in_specs=[smem] * len(info) + [pl.BlockSpec(memory_space=pl.ANY)] * len(loose) + [vmem] * len(inputs),
         out_specs=jax.tree.map(lambda _: vmem, out_shape),
         scratch_shapes=list(scratch),
+        cost_estimate=pl.CostEstimate(flops=1 << 28, bytes_accessed=1 << 20, transcendentals=0),
         compiler_params=pltpu.CompilerParams(vmem_limit_bytes=8 << 20),
     )(*[jnp.reshape(number, (1,)) for number in info], *loose, *inputs[::-1])
 

time: 53.9 us -> 53.9 us (level)
  no operation moved by 1% of the time
where the time goes in v6:
time: 53.9 us; the launch traced here: 53.7 us
  starting transfers between devices  23.2 us (43%)
  waiting for transfers between devices  23 us (43%)
  Pallas kernels  4.8 us (9%)
  matrix products  1.95 us (4%)
  between operations  0.76 us (1%)
    ppermute x22, waiting for transfers between devices, move(): return lax.ppermute(block, ('delay', 'row', 'col'), pairs)  23 us
    ppermute x22, starting transfers between devices, move(): return lax.ppermute(block, ('delay', 'row', 'col'), pairs)  20 us
    pallas_call x12, Pallas kernels, kernel_call(): pl.pallas_call(functools.partial(farthest_first, body, len(info), len(loo...  3.87 us
    ppermute x1, starting transfers between devices, from_behind(): return lax.ppermute(block, axis, route) if route else jnp.zeros_like(block)  3.19 us
    dot_general x1, matrix products, begin(): lax.dot_general(past, operator, (((0,), (1,)), ((), ())), preferred_eleme...  1.95 us
  transfers between devices with their start and end apart: 23, of which 15 were waited for; matrix products, arithmetic and copies ran while one was open for 4% of the time, Pallas kernels for 4%

profile of v6, /device:TPU:0, one launch (start us, length us, event | category | flops | bytes accessed | tf_op | source)
XLA Modules:
  0.0 53.7 jit_solution(14833074618398536690)
XLA Ops:
  0.6 0.5 collective-permute-start.2
  1.1 0.1 collective-permute-start
  1.2 1.9 %convolution_convert_fusion.refs_2_ = bf16[128,768]{1,0:T(8,128)(2,1)S(1)} fusion(bf16[1,768,128]{2,1,0:T(8,128)(2,1)} %param.7, bf16[1,768,768]{2,1,0:T(8,128)(2,1)} %param.5), kind=kOutput, calls=%fused_computation | convolution fusion | flops 151093248 | bytes 1572864 | tf_op jit(solution)/shard_map/dot_general | solution.py:170
  3.2 0.0 copy-start.2
  3.2 2.7 %collective-permute-start.4 = (bf16[32,768]{1,0:T(8,128)(2,1)S(1)}, bf16[32,768]{1,0:T(8,128)(2,1)S(1)}, u32[]{:S(2)}, u32[]{:S(2)}) collective-permute-start(bf16[32,768]{1,0:T(8,128)(2,1)S(1)} %get-tuple-element.16), channel_id=1, source_target_pairs={{0,20},{1,21},{2,22},{3,23},{4,16},{5,17},{6,18},{7,19},{8,28},{9,... | collective-permute-start | bytes 147464 | tf_op jit(solution)/shard_map/ppermute | solution.py:130
  5.9 0.4 collective-permute-start.5
  6.3 0.0 collective-permute-start.6
  6.4 0.1 shard_map.61
  6.5 0.0 copy-start.1
  6.5 0.1 shard_map.60.refs_3_
  6.7 1.4 %collective-permute-done.4.refs_4_ = bf16[32,768]{1,0:T(8,128)(2,1)S(1)} collective-permute-done((bf16[32,768]{1,0:T(8,128)(2,1)S(1)}, bf16[32,768]{1,0:T(8,128)(2,1)S(1)}, u32[]{:S(2)}, u32[]{:S(2)}) %collective-permute-start.4) | collective-permute-done | bytes 49184 | tf_op jit(solution)/shard_map/ppermute | solution.py:130
  8.1 0.1 collective-permute-start.3
  8.1 1.9 %collective-permute-done.5.refs_5_ = bf16[32,768]{1,0:T(8,128)(2,1)S(1)} collective-permute-done((bf16[32,768]{1,0:T(8,128)(2,1)S(1)}, bf16[32,768]{1,0:T(8,128)(2,1)S(1)}, u32[]{:S(2)}, u32[]{:S(2)}) %collective-permute-start.5) | collective-permute-done | bytes 49184 | tf_op jit(solution)/shard_map/ppermute | solution.py:130
  10.0 0.0 copy-start
  10.1 3.7 %collective-permute-start.7 = (bf16[64,768]{1,0:T(8,128)(2,1)S(1)}, bf16[64,768]{1,0:T(8,128)(2,1)S(1)}, u32[]{:S(2)}, u32[]{:S(2)}) collective-permute-start(bf16[64,768]{1,0:T(8,128)(2,1)S(1)} %shard_map.62.refs_8_), channel_id=1, source_target_pairs={{0,3},{1,2},{2,1},{3,0},{4,7},{5,6},{6,5},{7,4},{8,11},{9,10},{10,... | collective-permute-start | bytes 294920 | tf_op jit(solution)/shard_map/ppermute | solution.py:130
  13.7 0.8 %collective-permute-start.9 = (bf16[64,768]{1,0:T(8,128)(2,1)S(1)}, bf16[64,768]{1,0:T(8,128)(2,1)S(1)}, u32[]{:S(2)}, u32[]{:S(2)}) collective-permute-start(bf16[64,768]{1,0:T(8,128)(2,1)S(1)} %shard_map.62.refs_8_), channel_id=1, source_target_pairs={{0,1},{1,0},{2,3},{3,2},{4,5},{5,4},{6,7},{7,6},{8,9},{9,8},{10,11... | collective-permute-start | bytes 294920 | tf_op jit(solution)/shard_map/ppermute | solution.py:130
  14.5 2.9 %collective-permute-done.7.refs_5_ = bf16[64,768]{1,0:T(8,128)(2,1)S(1)} collective-permute-done((bf16[64,768]{1,0:T(8,128)(2,1)S(1)}, bf16[64,768]{1,0:T(8,128)(2,1)S(1)}, u32[]{:S(2)}, u32[]{:S(2)}) %collective-permute-start.7) | collective-permute-done | bytes 98336 | tf_op jit(solution)/shard_map/ppermute | solution.py:130
  17.5 3.2 %collective-permute-start.1 = (bf16[64,768]{1,0:T(8,128)(2,1)S(1)}, bf16[64,768]{1,0:T(8,128)(2,1)S(1)}, u32[]{:S(2)}, u32[]{:S(2)}) collective-permute-start(bf16[64,768]{1,0:T(8,128)(2,1)S(1)} %shard_map.60.refs_3_), channel_id=1, source_target_pairs={{0,16},{1,17},{2,18},{3,19},{4,20},{5,21},{6,22},{7,23},{8,24},{9,... | collective-permute-start | bytes 294920 | tf_op jit(solution)/shard_map/ppermute | solution.py:65
  20.7 0.8 %collective-permute-done.8.refs_6_ = bf16[64,768]{1,0:T(8,128)(2,1)S(1)} collective-permute-done((bf16[64,768]{1,0:T(8,128)(2,1)S(1)}, bf16[64,768]{1,0:T(8,128)(2,1)S(1)}, u32[]{:S(2)}, u32[]{:S(2)}) %collective-permute-start.8) | collective-permute-done | bytes 98336 | tf_op jit(solution)/shard_map/ppermute | solution.py:130
  21.5 0.8 %shard_map.63.refs_7_ = bf16[32,768]{1,0:T(8,128)(2,1)S(1)} custom-call(s32[1]{0:T(128)} %bitcast.refs_0_.d_ref, bf16[768,768]{1,0:T(8,128)(2,1)S(1)} %collective-permute-done.2.refs_1_, bf16[768,768]{1,0:T(8,128)(2,1)S(1)} %copy-done.1, bf16[32,768]{1,0:T(8,128)(2,1)S(1)} %collective-permute-done.3.refs_3_, ...), custom_call_target="tpu_custom_call" | custom-call | flops 268435456 | bytes 1048576 | tf_op jit(solution)/shard_map/pallas_call | solution.py:141
  22.3 2.8 %collective-permute-start.10 = (bf16[32,768]{1,0:T(8,128)(2,1)S(1)}, bf16[32,768]{1,0:T(8,128)(2,1)S(1)}, u32[]{:S(2)}, u32[]{:S(2)}) collective-permute-start(bf16[32,768]{1,0:T(8,128)(2,1)S(1)} %shard_map.63.refs_7_), channel_id=1, source_target_pairs={{0,24},{1,25},{2,26},{3,27},{4,28},{5,29},{6,30},{7,31},{8,16},{9,... | collective-permute-start | bytes 147464 | tf_op jit(solution)/shard_map/ppermute | solution.py:130
  25.1 0.5 collective-permute-start.11
  25.6 0.2 collective-permute-start.12
  25.8 1.5 %collective-permute-done.10.refs_4_ = bf16[32,768]{1,0:T(8,128)(2,1)S(1)} collective-permute-done((bf16[32,768]{1,0:T(8,128)(2,1)S(1)}, bf16[32,768]{1,0:T(8,128)(2,1)S(1)}, u32[]{:S(2)}, u32[]{:S(2)}) %collective-permute-start.10) | collective-permute-done | bytes 49184 | tf_op jit(solution)/shard_map/ppermute | solution.py:130
  27.3 1.9 %collective-permute-done.11.refs_5_ = bf16[32,768]{1,0:T(8,128)(2,1)S(1)} collective-permute-done((bf16[32,768]{1,0:T(8,128)(2,1)S(1)}, bf16[32,768]{1,0:T(8,128)(2,1)S(1)}, u32[]{:S(2)}, u32[]{:S(2)}) %collective-permute-start.11) | collective-permute-done | bytes 49184 | tf_op jit(solution)/shard_map/ppermute | solution.py:130
  29.2 0.5 collective-permute-done.12.refs_6_
  29.7 0.8 %shard_map.64 = (bf16[64,768]{1,0:T(8,128)(2,1)S(1)}, bf16[64,768]{1,0:T(8,128)(2,1)S(1)}, bf16[64,768]{1,0:T(8,128)(2,1)S(1)}) custom-call(s32[1]{0:T(128)} %bitcast.refs_0_.d_ref, bf16[768,768]{1,0:T(8,128)(2,1)S(1)} %collective-permute-done.refs_1_, bf16[768,768]{1,0:T(8,128)(2,1)S(1)} %bitcast.9, bf16[64,768]{1,0:T(8,128)(2,1)S(1)} %collective-permute-done.1.refs_3_, ...), custom_call_target="tpu_custom_call" | custom-call | flops 268435456 | bytes 1048576 | tf_op jit(solution)/shard_map/pallas_call | solution.py:141
  30.5 0.2 collective-permute-start.15
  30.7 0.1 shard_map.66
  30.9 0.8 %shard_map.67.refs_4_ = bf16[64,768]{1,0:T(8,128)(2,1)S(1)} custom-call(s32[1]{0:T(128)} %bitcast.refs_0_.d_ref, bf16[768,768]{1,0:T(8,128)(2,1)S(1)} %collective-permute-done.refs_1_, bf16[768,768]{1,0:T(8,128)(2,1)S(1)} %bitcast.10, bf16[64,768]{1,0:T(8,128)(2,1)S(1)} %get-tuple-element.23.refs_3_), custom_call_target="tpu_custom_call" | custom-call | flops 268435456 | bytes 1048576 | tf_op jit(solution)/shard_map/pallas_call | solution.py:141
  31.6 3.5 %collective-permute-done.15.refs_3_ = bf16[64,768]{1,0:T(8,128)(2,1)S(1)} collective-permute-done((bf16[64,768]{1,0:T(8,128)(2,1)S(1)}, bf16[64,768]{1,0:T(8,128)(2,1)S(1)}, u32[]{:S(2)}, u32[]{:S(2)}) %collective-permute-start.15) | collective-permute-done | bytes 98336 | tf_op jit(solution)/shard_map/ppermute | solution.py:130
  35.2 2.6 %collective-permute-start.16 = (bf16[64,768]{1,0:T(8,128)(2,1)S(1)}, bf16[64,768]{1,0:T(8,128)(2,1)S(1)}, u32[]{:S(2)}, u32[]{:S(2)}) collective-permute-start(bf16[64,768]{1,0:T(8,128)(2,1)S(1)} %shard_map.68.refs_8_), channel_id=1, source_target_pairs={{0,3},{1,2},{2,1},{3,0},{4,7},{5,6},{6,5},{7,4},{8,11},{9,10},{10,... | collective-permute-start | bytes 294920 | tf_op jit(solution)/shard_map/ppermute | solution.py:130
  37.8 0.4 collective-permute-start.17
  38.2 1.5 %collective-permute-start.18 = (bf16[64,768]{1,0:T(8,128)(2,1)S(1)}, bf16[64,768]{1,0:T(8,128)(2,1)S(1)}, u32[]{:S(2)}, u32[]{:S(2)}) collective-permute-start(bf16[64,768]{1,0:T(8,128)(2,1)S(1)} %shard_map.68.refs_8_), channel_id=1, source_target_pairs={{0,1},{1,0},{2,3},{3,2},{4,5},{5,4},{6,7},{7,6},{8,9},{9,8},{10,11... | collective-permute-start | bytes 294920 | tf_op jit(solution)/shard_map/ppermute | solution.py:130
  39.7 1.2 %collective-permute-done.14.refs_3_ = bf16[32,768]{1,0:T(8,128)(2,1)S(1)} collective-permute-done((bf16[32,768]{1,0:T(8,128)(2,1)S(1)}, bf16[32,768]{1,0:T(8,128)(2,1)S(1)}, u32[]{:S(2)}, u32[]{:S(2)}) %collective-permute-start.14) | collective-permute-done | bytes 49184 | tf_op jit(solution)/shard_map/ppermute | solution.py:130
  40.9 0.9 %collective-permute-done.16.refs_5_ = bf16[64,768]{1,0:T(8,128)(2,1)S(1)} collective-permute-done((bf16[64,768]{1,0:T(8,128)(2,1)S(1)}, bf16[64,768]{1,0:T(8,128)(2,1)S(1)}, u32[]{:S(2)}, u32[]{:S(2)}) %collective-permute-start.16) | collective-permute-done | bytes 98336 | tf_op jit(solution)/shard_map/ppermute | solution.py:130
  41.8 2.6 %collective-permute-done.17.refs_6_ = bf16[64,768]{1,0:T(8,128)(2,1)S(1)} collective-permute-done((bf16[64,768]{1,0:T(8,128)(2,1)S(1)}, bf16[64,768]{1,0:T(8,128)(2,1)S(1)}, u32[]{:S(2)}, u32[]{:S(2)}) %collective-permute-start.17) | collective-permute-done | bytes 98336 | tf_op jit(solution)/shard_map/ppermute | solution.py:130
  44.4 0.8 %shard_map.69.refs_4_ = bf16[32,768]{1,0:T(8,128)(2,1)S(1)} custom-call(s32[1]{0:T(128)} %bitcast.refs_0_.d_ref, bf16[768,768]{1,0:T(8,128)(2,1)S(1)} %collective-permute-done.2.refs_1_, bf16[768,768]{1,0:T(8,128)(2,1)S(1)} %copy-done.1, bf16[32,768]{1,0:T(8,128)(2,1)S(1)} %collective-permute-done.14.refs_3_, ...), custom_call_target="tpu_custom_call" | custom-call | flops 268435456 | bytes 1048576 | tf_op jit(solution)/shard_map/pallas_call | solution.py:141
  45.2 1.7 %collective-permute-start.19 = (bf16[32,768]{1,0:T(8,128)(2,1)S(1)}, bf16[32,768]{1,0:T(8,128)(2,1)S(1)}, u32[]{:S(2)}, u32[]{:S(2)}) collective-permute-start(bf16[32,768]{1,0:T(8,128)(2,1)S(1)} %shard_map.69.refs_4_), channel_id=1, source_target_pairs={{0,24},{1,25},{2,26},{3,27},{4,28},{5,29},{6,30},{7,31},{8,16},{9,... | collective-permute-start | bytes 147464 | tf_op jit(solution)/shard_map/ppermute | solution.py:130
  46.8 0.5 collective-permute-start.20
  47.3 1.4 %collective-permute-start.21 = (bf16[32,768]{1,0:T(8,128)(2,1)S(1)}, bf16[32,768]{1,0:T(8,128)(2,1)S(1)}, u32[]{:S(2)}, u32[]{:S(2)}) collective-permute-start(bf16[32,768]{1,0:T(8,128)(2,1)S(1)} %shard_map.69.refs_4_), channel_id=1, source_target_pairs={{0,16},{1,17},{2,18},{3,19},{4,20},{5,21},{6,22},{7,23},{8,24},{9,... | collective-permute-start | bytes 147464 | tf_op jit(solution)/shard_map/ppermute | solution.py:130
  48.7 1.5 %collective-permute-done.19.refs_1_ = bf16[32,768]{1,0:T(8,128)(2,1)S(1)} collective-permute-done((bf16[32,768]{1,0:T(8,128)(2,1)S(1)}, bf16[32,768]{1,0:T(8,128)(2,1)S(1)}, u32[]{:S(2)}, u32[]{:S(2)}) %collective-permute-start.19) | collective-permute-done | bytes 49184 | tf_op jit(solution)/shard_map/ppermute | solution.py:130
  50.2 0.7 %collective-permute-done.20.refs_2_ = bf16[32,768]{1,0:T(8,128)(2,1)S(1)} collective-permute-done((bf16[32,768]{1,0:T(8,128)(2,1)S(1)}, bf16[32,768]{1,0:T(8,128)(2,1)S(1)}, u32[]{:S(2)}, u32[]{:S(2)}) %collective-permute-start.20) | collective-permute-done | bytes 49184 | tf_op jit(solution)/shard_map/ppermute | solution.py:130
  50.9 0.5 collective-permute-done.21.refs_3_
  51.4 0.1 collective-permute-start.22
  51.5 0.2 shard_map.65.refs_0_
  51.7 1.1 %collective-permute-done.22.refs_2_ = bf16[64,768]{1,0:T(8,128)(2,1)S(1)} collective-permute-done((bf16[64,768]{1,0:T(8,128)(2,1)S(1)}, bf16[64,768]{1,0:T(8,128)(2,1)S(1)}, u32[]{:S(2)}, u32[]{:S(2)}) %collective-permute-start.22) | collective-permute-done | bytes 98336 | tf_op jit(solution)/shard_map/ppermute | solution.py:130
  52.8 0.9 %shard_map.71 = (bf16[2,768,128]{2,1,0:T(8,128)(2,1)}, bf16[1,768,128]{2,1,0:T(8,128)(2,1)}) custom-call(s32[1]{0:T(128)} %bitcast.refs_0_.d_ref, s32[1]{0:T(128)} %bitcast.1.refs_1_.refs_0_.n_ref, bf16[768,128]{1,0:T(8,128)(2,1)S(1)} %shard_map.65.refs_0_, bf16[64,768]{1,0:T(8,128)(2,1)S(1)} %shard_map.70.refs_1_, ...), custom_call_target="tpu_custom_call" | custom-call | tf_op jit(solution)/shard_map/pallas_call | solution.py:321
  (20 shorter events, 0.1 us)
Async XLA Ops:
  0.6 20.8 %collective-permute-start.2 = (bf16[768,768]{1,0:T(8,128)(2,1)}, bf16[768,768]{1,0:T(8,128)(2,1)S(1)}, u32[]{:S(2)}, u32[]{:S(2)}) collective-permute-start(bf16[768,768]{1,0:T(8,128)(2,1)} %refs_2_.3), channel_id=1, source_target_pairs={{0,4},{1,5},{2,6},{3,7},{4,0},{5,1},{6,2},{7,3},{8,12},{9,13},{10,... | collective-permute-start | bytes 3538952 | tf_op jit(solution)/shard_map/ppermute | solution.py:130
  1.1 24.6 %collective-permute-start = (bf16[768,768]{1,0:T(8,128)(2,1)}, bf16[768,768]{1,0:T(8,128)(2,1)S(1)}, u32[]{:S(2)}, u32[]{:S(2)}) collective-permute-start(bf16[768,768]{1,0:T(8,128)(2,1)} %bitcast.8), channel_id=1, source_target_pairs={{0,4},{1,5},{2,6},{3,7},{4,0},{5,1},{6,2},{7,3},{8,12},{9,13},{10,... | collective-permute-start | bytes 3538952 | tf_op jit(solution)/shard_map/ppermute | solution.py:130
  1.2 5.1 %copy-start.3 = (bf16[2,768,128]{2,1,0:T(8,128)(2,1)S(1)}, bf16[2,768,128]{2,1,0:T(8,128)(2,1)}, u32[]{:S(2)}) copy-start(bf16[2,768,128]{2,1,0:T(8,128)(2,1)} %refs_3_.3) | copy-start | bytes 1179652
  3.2 3.3 %copy-start.2 = (bf16[1,768,128]{2,1,0:T(8,128)(2,1)S(1)}, bf16[1,768,128]{2,1,0:T(8,128)(2,1)}, u32[]{:S(2)}) copy-start(bf16[1,768,128]{2,1,0:T(8,128)(2,1)} %param.7) | copy-start | bytes 589828
  3.2 4.8 %collective-permute-start.4 = (bf16[32,768]{1,0:T(8,128)(2,1)S(1)}, bf16[32,768]{1,0:T(8,128)(2,1)S(1)}, u32[]{:S(2)}, u32[]{:S(2)}) collective-permute-start(bf16[32,768]{1,0:T(8,128)(2,1)S(1)} %get-tuple-element.16), channel_id=1, source_target_pairs={{0,20},{1,21},{2,22},{3,23},{4,16},{5,17},{6,18},{7,19},{8,28},{9,... | collective-permute-start | bytes 147464 | tf_op jit(solution)/shard_map/ppermute | solution.py:130
  5.9 4.1 %collective-permute-start.5 = (bf16[32,768]{1,0:T(8,128)(2,1)S(1)}, bf16[32,768]{1,0:T(8,128)(2,1)S(1)}, u32[]{:S(2)}, u32[]{:S(2)}) collective-permute-start(bf16[32,768]{1,0:T(8,128)(2,1)S(1)} %get-tuple-element.17), channel_id=1, source_target_pairs={{0,16},{1,17},{2,18},{3,19},{4,20},{5,21},{6,22},{7,23},{8,24},{9,... | collective-permute-start | bytes 147464 | tf_op jit(solution)/shard_map/ppermute | solution.py:130
  6.3 3.7 %collective-permute-start.6 = (bf16[32,768]{1,0:T(8,128)(2,1)S(1)}, bf16[32,768]{1,0:T(8,128)(2,1)S(1)}, u32[]{:S(2)}, u32[]{:S(2)}) collective-permute-start(bf16[32,768]{1,0:T(8,128)(2,1)S(1)} %get-tuple-element.18), channel_id=1, source_target_pairs={{0,4},{1,5},{2,6},{3,7},{4,0},{5,1},{6,2},{7,3},{8,12},{9,13},{10,... | collective-permute-start | bytes 147464 | tf_op jit(solution)/shard_map/ppermute | solution.py:130
  6.5 14.9 %copy-start.1 = (bf16[768,768]{1,0:T(8,128)(2,1)S(1)}, bf16[768,768]{1,0:T(8,128)(2,1)}, u32[]{:S(2)}) copy-start(bf16[768,768]{1,0:T(8,128)(2,1)} %refs_2_.3) | copy-start | bytes 3538948
  8.1 5.7 %collective-permute-start.3 = (bf16[32,768]{1,0:T(8,128)(2,1)S(1)}, bf16[32,768]{1,0:T(8,128)(2,1)S(1)}, u32[]{:S(2)}, u32[]{:S(2)}) collective-permute-start(bf16[32,768]{1,0:T(8,128)(2,1)S(1)} %get-tuple-element.14.refs_2_), channel_id=1, source_target_pairs={{0,4},{1,5},{2,6},{3,7},{4,0},{5,1},{6,2},{7,3},{8,12},{9,13},{10,... | collective-permute-start | bytes 147464 | tf_op jit(solution)/shard_map/ppermute | solution.py:130
  10.0 19.7 %copy-start = (bf16[1,768,768]{2,1,0:T(8,128)(2,1)S(1)}, bf16[1,768,768]{2,1,0:T(8,128)(2,1)}, u32[]{:S(2)}) copy-start(bf16[1,768,768]{2,1,0:T(8,128)(2,1)} %param.5) | copy-start | bytes 3538948
  10.1 7.4 %collective-permute-start.7 = (bf16[64,768]{1,0:T(8,128)(2,1)S(1)}, bf16[64,768]{1,0:T(8,128)(2,1)S(1)}, u32[]{:S(2)}, u32[]{:S(2)}) collective-permute-start(bf16[64,768]{1,0:T(8,128)(2,1)S(1)} %shard_map.62.refs_8_), channel_id=1, source_target_pairs={{0,3},{1,2},{2,1},{3,0},{4,7},{5,6},{6,5},{7,4},{8,11},{9,10},{10,... | collective-permute-start | bytes 294920 | tf_op jit(solution)/shard_map/ppermute | solution.py:130
  13.7 7.7 %collective-permute-start.8 = (bf16[64,768]{1,0:T(8,128)(2,1)S(1)}, bf16[64,768]{1,0:T(8,128)(2,1)S(1)}, u32[]{:S(2)}, u32[]{:S(2)}) collective-permute-start(bf16[64,768]{1,0:T(8,128)(2,1)S(1)} %shard_map.62.refs_8_), channel_id=1, source_target_pairs={{0,2},{1,3},{2,0},{3,1},{4,6},{5,7},{6,4},{7,5},{8,10},{9,11},{10,... | collective-permute-start | bytes 294920 | tf_op jit(solution)/shard_map/ppermute | solution.py:130
  13.7 7.7 %collective-permute-start.9 = (bf16[64,768]{1,0:T(8,128)(2,1)S(1)}, bf16[64,768]{1,0:T(8,128)(2,1)S(1)}, u32[]{:S(2)}, u32[]{:S(2)}) collective-permute-start(bf16[64,768]{1,0:T(8,128)(2,1)S(1)} %shard_map.62.refs_8_), channel_id=1, source_target_pairs={{0,1},{1,0},{2,3},{3,2},{4,5},{5,4},{6,7},{7,6},{8,9},{9,8},{10,11... | collective-permute-start | bytes 294920 | tf_op jit(solution)/shard_map/ppermute | solution.py:130
  17.5 8.3 %collective-permute-start.1 = (bf16[64,768]{1,0:T(8,128)(2,1)S(1)}, bf16[64,768]{1,0:T(8,128)(2,1)S(1)}, u32[]{:S(2)}, u32[]{:S(2)}) collective-permute-start(bf16[64,768]{1,0:T(8,128)(2,1)S(1)} %shard_map.60.refs_3_), channel_id=1, source_target_pairs={{0,16},{1,17},{2,18},{3,19},{4,20},{5,21},{6,22},{7,23},{8,24},{9,... | collective-permute-start | bytes 294920 | tf_op jit(solution)/shard_map/ppermute | solution.py:65
  22.3 5.1 %collective-permute-start.10 = (bf16[32,768]{1,0:T(8,128)(2,1)S(1)}, bf16[32,768]{1,0:T(8,128)(2,1)S(1)}, u32[]{:S(2)}, u32[]{:S(2)}) collective-permute-start(bf16[32,768]{1,0:T(8,128)(2,1)S(1)} %shard_map.63.refs_7_), channel_id=1, source_target_pairs={{0,24},{1,25},{2,26},{3,27},{4,28},{5,29},{6,30},{7,31},{8,16},{9,... | collective-permute-start | bytes 147464 | tf_op jit(solution)/shard_map/ppermute | solution.py:130
  25.1 4.1 %collective-permute-start.11 = (bf16[32,768]{1,0:T(8,128)(2,1)S(1)}, bf16[32,768]{1,0:T(8,128)(2,1)S(1)}, u32[]{:S(2)}, u32[]{:S(2)}) collective-permute-start(bf16[32,768]{1,0:T(8,128)(2,1)S(1)} %shard_map.63.refs_7_), channel_id=1, source_target_pairs={{0,8},{1,9},{2,10},{3,11},{4,12},{5,13},{6,14},{7,15},{8,0},{9,1},... | collective-permute-start | bytes 147464 | tf_op jit(solution)/shard_map/ppermute | solution.py:130
  25.6 4.1 %collective-permute-start.12 = (bf16[32,768]{1,0:T(8,128)(2,1)S(1)}, bf16[32,768]{1,0:T(8,128)(2,1)S(1)}, u32[]{:S(2)}, u32[]{:S(2)}) collective-permute-start(bf16[32,768]{1,0:T(8,128)(2,1)S(1)} %shard_map.63.refs_7_), channel_id=1, source_target_pairs={{0,16},{1,17},{2,18},{3,19},{4,20},{5,21},{6,22},{7,23},{8,24},{9,... | collective-permute-start | bytes 147464 | tf_op jit(solution)/shard_map/ppermute | solution.py:130
  30.5 4.7 %collective-permute-start.15 = (bf16[64,768]{1,0:T(8,128)(2,1)S(1)}, bf16[64,768]{1,0:T(8,128)(2,1)S(1)}, u32[]{:S(2)}, u32[]{:S(2)}) collective-permute-start(bf16[64,768]{1,0:T(8,128)(2,1)S(1)} %get-tuple-element.20.refs_2_), channel_id=1, source_target_pairs={{0,16},{1,17},{2,18},{3,19},{4,20},{5,21},{6,22},{7,23},{8,24},{9,... | collective-permute-start | bytes 294920 | tf_op jit(solution)/shard_map/ppermute | solution.py:130
  35.2 6.6 %collective-permute-start.16 = (bf16[64,768]{1,0:T(8,128)(2,1)S(1)}, bf16[64,768]{1,0:T(8,128)(2,1)S(1)}, u32[]{:S(2)}, u32[]{:S(2)}) collective-permute-start(bf16[64,768]{1,0:T(8,128)(2,1)S(1)} %shard_map.68.refs_8_), channel_id=1, source_target_pairs={{0,3},{1,2},{2,1},{3,0},{4,7},{5,6},{6,5},{7,4},{8,11},{9,10},{10,... | collective-permute-start | bytes 294920 | tf_op jit(solution)/shard_map/ppermute | solution.py:130
  37.8 6.6 %collective-permute-start.17 = (bf16[64,768]{1,0:T(8,128)(2,1)S(1)}, bf16[64,768]{1,0:T(8,128)(2,1)S(1)}, u32[]{:S(2)}, u32[]{:S(2)}) collective-permute-start(bf16[64,768]{1,0:T(8,128)(2,1)S(1)} %shard_map.68.refs_8_), channel_id=1, source_target_pairs={{0,2},{1,3},{2,0},{3,1},{4,6},{5,7},{6,4},{7,5},{8,10},{9,11},{10,... | collective-permute-start | bytes 294920 | tf_op jit(solution)/shard_map/ppermute | solution.py:130
  38.2 6.2 %collective-permute-start.18 = (bf16[64,768]{1,0:T(8,128)(2,1)S(1)}, bf16[64,768]{1,0:T(8,128)(2,1)S(1)}, u32[]{:S(2)}, u32[]{:S(2)}) collective-permute-start(bf16[64,768]{1,0:T(8,128)(2,1)S(1)} %shard_map.68.refs_8_), channel_id=1, source_target_pairs={{0,1},{1,0},{2,3},{3,2},{4,5},{5,4},{6,7},{7,6},{8,9},{9,8},{10,11... | collective-permute-start | bytes 294920 | tf_op jit(solution)/shard_map/ppermute | solution.py:130
  39.7 1.2 %collective-permute-start.14 = (bf16[32,768]{1,0:T(8,128)(2,1)S(1)}, bf16[32,768]{1,0:T(8,128)(2,1)S(1)}, u32[]{:S(2)}, u32[]{:S(2)}) collective-permute-start(bf16[32,768]{1,0:T(8,128)(2,1)S(1)} %get-tuple-element.21.refs_2_), channel_id=1, source_target_pairs={{0,4},{1,5},{2,6},{3,7},{4,0},{5,1},{6,2},{7,3},{8,12},{9,13},{10,... | collective-permute-start | bytes 147464 | tf_op jit(solution)/shard_map/ppermute | solution.py:130
  45.2 5.0 %collective-permute-start.19 = (bf16[32,768]{1,0:T(8,128)(2,1)S(1)}, bf16[32,768]{1,0:T(8,128)(2,1)S(1)}, u32[]{:S(2)}, u32[]{:S(2)}) collective-permute-start(bf16[32,768]{1,0:T(8,128)(2,1)S(1)} %shard_map.69.refs_4_), channel_id=1, source_target_pairs={{0,24},{1,25},{2,26},{3,27},{4,28},{5,29},{6,30},{7,31},{8,16},{9,... | collective-permute-start | bytes 147464 | tf_op jit(solution)/shard_map/ppermute | solution.py:130
  46.8 4.1 %collective-permute-start.20 = (bf16[32,768]{1,0:T(8,128)(2,1)S(1)}, bf16[32,768]{1,0:T(8,128)(2,1)S(1)}, u32[]{:S(2)}, u32[]{:S(2)}) collective-permute-start(bf16[32,768]{1,0:T(8,128)(2,1)S(1)} %shard_map.69.refs_4_), channel_id=1, source_target_pairs={{0,8},{1,9},{2,10},{3,11},{4,12},{5,13},{6,14},{7,15},{8,0},{9,1},... | collective-permute-start | bytes 147464 | tf_op jit(solution)/shard_map/ppermute | solution.py:130
  47.3 4.1 %collective-permute-start.21 = (bf16[32,768]{1,0:T(8,128)(2,1)S(1)}, bf16[32,768]{1,0:T(8,128)(2,1)S(1)}, u32[]{:S(2)}, u32[]{:S(2)}) collective-permute-start(bf16[32,768]{1,0:T(8,128)(2,1)S(1)} %shard_map.69.refs_4_), channel_id=1, source_target_pairs={{0,16},{1,17},{2,18},{3,19},{4,20},{5,21},{6,22},{7,23},{8,24},{9,... | collective-permute-start | bytes 147464 | tf_op jit(solution)/shard_map/ppermute | solution.py:130
  48.7 2.8 %collective-permute-start.13 = (bf16[64,768]{1,0:T(8,128)(2,1)S(1)}, bf16[64,768]{1,0:T(8,128)(2,1)S(1)}, u32[]{:S(2)}, u32[]{:S(2)}) collective-permute-start(bf16[64,768]{1,0:T(8,128)(2,1)S(1)} %get-tuple-element.19.refs_3_), channel_id=1, source_target_pairs={{0,4},{1,5},{2,6},{3,7},{4,0},{5,1},{6,2},{7,3},{8,12},{9,13},{10,... | collective-permute-start | bytes 294920 | tf_op jit(solution)/shard_map/ppermute | solution.py:130
  51.4 1.4 %collective-permute-start.22 = (bf16[64,768]{1,0:T(8,128)(2,1)S(1)}, bf16[64,768]{1,0:T(8,128)(2,1)S(1)}, u32[]{:S(2)}, u32[]{:S(2)}) collective-permute-start(bf16[64,768]{1,0:T(8,128)(2,1)S(1)} %shard_map.70.refs_1_), channel_id=1, source_target_pairs={{0,4},{1,5},{2,6},{3,7},{4,0},{5,1},{6,2},{7,3},{8,12},{9,13},{10,... | collective-permute-start | bytes 294920 | tf_op jit(solution)/shard_map/ppermute | solution.py:130
